TPU v7x, 32 devices: a whole 2x2x4 slice. The times are simulated.
32 devices in a mesh: grp: 2 (over x), beam: 16 (over z, y, core).
Axes of the slice: x: 2, y: 2, z: 4, core: 2. Of those that a mesh axis runs over, the one named last changes fastest.
Arguments:
- s_matrix: bfloat16 [2, 2048, 16, 4096], P(None, ('grp', 'beam')), parts along dimension 1, may hold values from -6 to 6
- beam_weight: float32 [2, 2048], P(None, ('grp', 'beam')), parts along dimension 1, may hold values from -0.25 to 0.25
- probe_shift: int32 [256, 2], P(('grp', 'beam')), parts along dimension 0, may hold values from 0 to 191
- probe_cutoff: int32 [256], P(('grp', 'beam')), parts along dimension 0, may hold values from 64 to 512
- target: bfloat16 [2, 256, 4096], P(None, ('grp', 'beam')), parts along dimension 1, may hold values from -3 to 3
- target_exp: int32 [256], P(('grp', 'beam')), parts along dimension 0, may hold values from -1 to 2
Outputs:
- s_grad: bfloat16 [2, 2048, 16, 4096], P(None, ('grp', 'beam')), parts along dimension 1
There are 2 independent parts, one for each index of `grp`. A program takes and returns all parts, laid end to end along the dimension named above; each array names one. Nothing has to cross between parts.
All inputs are finite; a program needn't handle non-finite values.
Results may differ from a plain program's by a relative error of at most 0.006.
Values may be sent and summed in bfloat16 or wider, within the bound.
No kernel may reach another device: no remote copies, remote signals or barrier semaphores. Data moves between devices by JAX's collectives and lax.ppermute only.
A program may use at most 128 MiB of HBM per device.

v0:
```python
import math

import jax
import jax.numpy as jnp
from jax import lax
from jax.sharding import PartitionSpec as P

SIDE = 32
GRID = 192
TILE_SIDE = 4


TWO_PI = 2.0 * math.pi


def window_of(shift):
    step = GRID // TILE_SIDE
    return shift[:, 0] // step * TILE_SIDE + shift[:, 1] // step


def coefficients(beam_index, weight, shift, cutoff):
    half = SIDE // 2
    freq_x = beam_index % SIDE - half
    freq_y = beam_index // SIDE - half
    ramp = (freq_x[None, :] * shift[:, 0:1] + freq_y[None, :] * shift[:, 1:2]) % GRID
    phase = ramp.astype(jnp.float32) * (TWO_PI / GRID)
    inside = (freq_x * freq_x + freq_y * freq_y)[None, :] <= cutoff[:, None]
    cosine = jnp.cos(phase)
    sine = jnp.sin(phase)
    w_real = weight[0][None, :]
    w_imag = weight[1][None, :]
    c_real = jnp.where(inside, w_real * cosine + w_imag * sine, 0.0)
    c_imag = jnp.where(inside, w_imag * cosine - w_real * sine, 0.0)
    return (c_real.astype(jnp.bfloat16), c_imag.astype(jnp.bfloat16))


def body(s_matrix, beam_weight, probe_shift, probe_cutoff, target, target_exp):
    local = s_matrix.shape[1]
    tile_count = s_matrix.shape[2]
    pixels = s_matrix.shape[3]
    beam_index = lax.axis_index("beam") * local + jnp.arange(local, dtype=jnp.int32)
    shifts, cutoffs, exponents = (
        lax.all_gather(probe_shift, "beam", axis=0, tiled=True),
        lax.all_gather(probe_cutoff, "beam", axis=0, tiled=True),
        lax.all_gather(target_exp, "beam", axis=0, tiled=True),
    )
    total = shifts.shape[0]
    c_real, c_imag = coefficients(beam_index, beam_weight, shifts, cutoffs)
    windows = window_of(shifts)
    onehot = windows[:, None] == jnp.arange(tile_count, dtype=jnp.int32)[None, :]
    zero = jnp.zeros((), jnp.bfloat16)
    width = local * tile_count
    e_real = jnp.where(onehot[:, None, :], c_real[:, :, None], zero).reshape(total, width)
    e_imag = jnp.where(onehot[:, None, :], c_imag[:, :, None], zero).reshape(total, width)
    s_flat = s_matrix.reshape(2 * width, pixels)
    left_re = jnp.concatenate([e_real, -e_imag], axis=1)
    left_im = jnp.concatenate([e_imag, e_real], axis=1)
    wave_re = jnp.dot(left_re, s_flat, preferred_element_type=jnp.float32)
    wave_im = jnp.dot(left_im, s_flat, preferred_element_type=jnp.float32)
    whole_targets = lax.all_gather(target, "beam", axis=1, tiled=True)
    full_re, full_im = lax.psum((wave_re, wave_im), "beam")
    scale = jnp.exp2(exponents.astype(jnp.float32))[None, :, None]
    residual = (jnp.stack([full_re, full_im]) - whole_targets.astype(jnp.float32) * scale).astype(
        jnp.bfloat16
    )
    stacked_coef = jnp.concatenate([e_real, e_imag], axis=0)
    flipped_coef = jnp.concatenate([e_real, -e_imag], axis=0)
    res_direct = jnp.concatenate([residual[0], residual[1]], axis=0)
    res_swapped = jnp.concatenate([residual[1], residual[0]], axis=0)
    dims = (((0,), (0,)), ((), ()))
    g_re = lax.dot_general(stacked_coef, res_direct, dims, preferred_element_type=jnp.float32)
    g_im = lax.dot_general(flipped_coef, res_swapped, dims, preferred_element_type=jnp.float32)
    s_grad = jnp.stack([g_re, g_im]).reshape(2, local, tile_count, pixels)
    return s_grad.astype(jnp.bfloat16)


def solution(mesh):
    return jax.shard_map(
        body,
        mesh=mesh,
        in_specs=(
            P(None, ("grp", "beam"), None, None),
            P(None, ("grp", "beam")),
            P(("grp", "beam"), None),
            P(("grp", "beam")),
            P(None, ("grp", "beam"), None),
            P(("grp", "beam")),
        ),
        out_specs=P(None, ("grp", "beam"), None, None),
        check_vma=False,
    )
```

profile of v0, /device:TPU:1, one launch (start us, length us, event | category | flops | bytes accessed | tf_op | source)
XLA Modules:
  0.0 235.6 jit_solution(14886051234407672063)
XLA Ops:
  6.5 0.0 all-reduce.6.cloned.1.call-start
  6.6 0.8 slice_bitcast_fusion.3
  7.3 23.2 %all-gather = s32[16,8,2]{1,2,0:T(2,128)S(1)} all-gather(s32[1,8,2]{1,2,0:T(2,128)} %bitcast.40), channel_id=1, replica_groups=mesh['grp'=2,'beam'=16] {'beam'}, dimensions={0}, use_global_device_ids=true | all-gather | bytes 1088 | tf_op jit(solution)/shard_map/all_gather | solution.py:43
  30.5 0.1 reshape.326
  30.7 1.2 dynamic-slice
  32.6 0.9 dynamic-update-slice
  33.4 0.8 dynamic-update-slice.1
  34.3 4.4 %all-reduce.2 = (s32[128]{0:T(128)S(1)}, s32[128]{0:T(128)S(1)}) all-reduce(s32[128]{0:T(128)S(1)} %dynamic-update-slice, s32[128]{0:T(128)S(1)} %dynamic-update-slice.1), channel_id=1, replica_groups=mesh['grp'=2,'beam'=16] {'beam'}, use_global_device_ids=true, to_apply=%add | all-reduce | flops 256 | bytes 2048
  38.7 0.2 fusion.16
  38.9 0.1 broadcast_select_fusion
  39.0 0.1 bitcast_negate_fusion
  39.0 0.0 copy-start
  39.0 9.6 %convolution_bitcast_fusion.1 = f32[1,128,4096]{2,1,0:T(8,128)} fusion(bf16[2048,4096]{1,0:T(8,128)(2,1)} %bitcast.30, bf16[128,1024]{0,1:T(8,128)(2,1)S(1)} %bitcast_negate_fusion, bf16[128,1024]{0,1:T(8,128)(2,1)S(1)} %bitcast.34), kind=kOutput, calls=%fused_computation.4 | convolution fusion | flops 2148532224 | bytes 19398656 | tf_op jit(solution)/shard_map/dot_general | solution.py:58
  48.7 1.7 copy-done
  50.3 3.7 %convolution_bitcast_fusion = f32[1,128,4096]{2,1,0:T(8,128)} fusion(bf16[2048,4096]{1,0:T(8,128)(2,1)S(1)} %bitcast.31, bf16[128,1024]{0,1:T(8,128)(2,1)S(1)} %bitcast.35, bf16[128,1024]{0,1:T(8,128)(2,1)S(1)} %bitcast.38), kind=kOutput, calls=%fused_computation.3 | convolution fusion | flops 2148532224 | bytes 19398656 | tf_op jit(solution)/shard_map/dot_general | solution.py:59
  54.0 0.0 all-reduce.6.cloned.1.call-update
  54.1 0.2 all-gather.3.cloned.1.call-start
  54.3 0.5 all-gather.3.cloned.1.call-update
  54.8 114.3 %all-reduce.6.cloned.1.call-done = (f32[1,128,4096]{2,1,0:T(8,128)}, f32[1,128,4096]{2,1,0:T(8,128)}) async-done(((f32[1,128,4096]{2,1,0:T(8,128)}, f32[1,128,4096]{2,1,0:T(8,128)}), (f32[1,128,4096]{2,1,0:T(8,128)}, f32[1,128,4096]{2,1,0:T(8,128)})) %all-reduce.6.cloned.1.call-update) | async-done | bytes 4194320 | tf_op jit(solution)/shard_map/psum | solution.py:61
  169.1 44.4 %all-gather.3.cloned.1.call-done = bf16[2,128,4096]{2,1,0:T(8,128)(2,1)} async-done(((bf16[2,8,4096]{2,1,0:T(8,128)(2,1)}), bf16[2,128,4096]{2,1,0:T(8,128)(2,1)}) %all-gather.3.cloned.1.call-update) | async-done | bytes 2097168 | tf_op jit(solution)/shard_map/all_gather | solution.py:60
  213.5 3.6 %fusion = bf16[2,128,4096]{2,1,0:T(8,128)(2,1)S(1)} fusion(f32[1,128,4096]{2,1,0:T(8,128)} %get-tuple-element.7, f32[1,128,4096]{2,1,0:T(8,128)} %get-tuple-element.8, bf16[2,128,4096]{2,1,0:T(8,128)(2,1)} %all-gather.3.cloned.1.call-done, f32[128]{0:T(128)S(1)} %multiply_exponential_fusion), kind=kLoop, calls=%fused_computation.6 | loop fusion | flops 5242880 | bytes 8389120 | tf_op jit(solution)/shard_map/convert_element_type | solution.py:63
  217.2 0.1 slice_bitcast_fusion
  217.3 2.4 convolution_convert_fusion
  219.7 2.4 convolution_convert_fusion.1
  222.0 6.8 %pad_maximum_fusion = bf16[2,64,16,4096]{3,2,1,0:T(8,128)(2,1)} fusion(bf16[1,64,16,4096]{3,2,1,0:T(8,128)(2,1)S(1)} %bitcast.32, bf16[1,64,16,4096]{3,2,1,0:T(8,128)(2,1)S(1)} %bitcast.33), kind=kLoop, calls=%fused_computation | loop fusion | flops 8388608 | bytes 33554432 | tf_op jit(solution)/shard_map/stack | solution.py:73
  (8 shorter events, 0.1 us)
Async XLA Ops:
  6.5 162.6 %all-reduce.6.cloned.1.call-start = ((), (), s32[]{:S(2)}) async-start(), calls=%async_computation.1 | async-start | bytes 8388608 | tf_op jit(solution)/shard_map/psum | solution.py:61
  39.0 11.3 %copy-start = (bf16[2,64,16,4096]{3,2,1,0:T(8,128)(2,1)S(1)}, bf16[2,64,16,4096]{3,2,1,0:T(8,128)(2,1)}, u32[]{:S(2)}) copy-start(bf16[2,64,16,4096]{3,2,1,0:T(8,128)(2,1)} %param.6) | copy-start | bytes 50331652
  54.1 159.5 %all-gather.3.cloned.1.call-start = ((), (), s32[]{:S(2)}) async-start(), calls=%async_computation | async-start | bytes 2228224 | tf_op jit(solution)/shard_map/all_gather | solution.py:60
Sparse Core Ops, SparseCore 0:
  54.2 114.8 all-reduce.5
  171.6 41.9 all-gather.2
where the time goes:
time: 236 us
  waiting for transfers between devices  159 us (67%)
  blocking collectives  27.6 us (12%)
  matrix products  18 us (8%)
  between operations  14.2 us (6%)
  other arithmetic  10.8 us (5%)
  local copies, waits for them, and re-layouts  5.59 us (2%)
    psum x1, waiting for transfers between devices, body(): full_re, full_im = lax.psum((wave_re, wave_im), 'beam')  114 us
    all_gather x1, waiting for transfers between devices, body(): whole_targets = lax.all_gather(target, 'beam', axis=1, tiled=True)  44.4 us
    all_gather x1, blocking collectives, body(): lax.all_gather(probe_shift, 'beam', axis=0, tiled=True)  23.2 us
    dot_general x1, matrix products, body(): wave_re = jnp.dot(left_re, s_flat, preferred_element_type=jnp.float32)  9.63 us
    another operation x1, other arithmetic, body(): s_grad = jnp.stack([g_re, g_im]).reshape(2, local, tile_count, pixels)  6.75 us
  transfers between devices with their start and end apart: 2, of which 2 were waited for; matrix products, arithmetic and copies ran while one was open for 0% of the time, Pallas kernels for 0%

commit v1 on v0

v1 whole, which is shorter than its diff:
```python
import functools
import math

import jax
import jax.numpy as jnp
from jax import lax
from jax.experimental import pallas as pl
from jax.experimental.pallas import tpu as pltpu
from jax.sharding import PartitionSpec as P

SIDE = 32
GRID = 192
TILE_SIDE = 4
TWO_PI = 2.0 * math.pi
CHUNKS = 2
FWD_COLUMNS = 512
BWD_COLUMNS = 512


def orders(count):
    masks = [1 << bit for bit in range(1, count.bit_length() - 1)]
    other = masks[:]
    if len(other) > 1:
        other[0], other[1] = other[1], other[0]
    return masks, other


def swap(x, count, stage):
    if stage < 0:
        pairs = [(i, i ^ 1) for i in range(count)]
    else:
        by_core = orders(count)
        pairs = [(i, i ^ by_core[i % 2][stage]) for i in range(count)]
    return lax.ppermute(x, "beam", pairs)


def forward_kernel(at_ref, s_ref, keep_ref, send_ref, a_ref):
    @pl.when(pl.program_id(0) == 0)
    def _():
        a_ref[...] = at_ref[...].T

    half = keep_ref.shape[0]
    wave = jnp.dot(a_ref[...], s_ref[...], preferred_element_type=jnp.float32)
    keep_ref[...] = wave[:half]
    send_ref[...] = wave[half:].astype(jnp.bfloat16)


def forward(at, s_flat, chunk, width):
    depth, rows = at.shape
    half = rows // 2
    steps = width // FWD_COLUMNS
    first = chunk * steps
    return pl.pallas_call(
        forward_kernel,
        grid=(steps,),
        in_specs=[
            pl.BlockSpec((depth, rows), lambda j: (0, 0)),
            pl.BlockSpec((depth, FWD_COLUMNS), lambda j: (0, first + j)),
        ],
        out_specs=[
            pl.BlockSpec((half, FWD_COLUMNS), lambda j: (0, j)),
            pl.BlockSpec((half, FWD_COLUMNS), lambda j: (0, j)),
        ],
        out_shape=[
            jax.ShapeDtypeStruct((half, width), jnp.float32),
            jax.ShapeDtypeStruct((half, width), jnp.bfloat16),
        ],
        scratch_shapes=[pltpu.VMEM((rows, depth), jnp.bfloat16)],
        compiler_params=pltpu.CompilerParams(vmem_limit_bytes=32 << 20),
        cost_estimate=pl.CostEstimate(
            flops=2 * rows * depth * width, bytes_accessed=2 * depth * width, transcendentals=0
        ),
    )(at, s_flat)


def backward_kernel(at_ref, own_ref, other_ref, *refs):
    out_ref = refs[-1]
    res = jnp.concatenate([own_ref[...], other_ref[...]], axis=0)
    out_ref[...] = jnp.dot(at_ref[...], res, preferred_element_type=jnp.float32).astype(jnp.bfloat16)


def backward(at, own, other, so_far, chunk, pixels):
    depth, rows = at.shape
    half, width = own.shape
    steps = width // BWD_COLUMNS
    first = chunk * steps
    extra = [] if so_far is None else [so_far]
    return pl.pallas_call(
        backward_kernel,
        grid=(steps,),
        in_specs=[
            pl.BlockSpec((depth, rows), lambda j: (0, 0)),
            pl.BlockSpec((half, BWD_COLUMNS), lambda j: (0, j)),
            pl.BlockSpec((half, BWD_COLUMNS), lambda j: (0, j)),
        ]
        + [pl.BlockSpec(memory_space=pl.ANY) for _ in extra],
        out_specs=pl.BlockSpec((depth, BWD_COLUMNS), lambda j: (0, first + j)),
        out_shape=jax.ShapeDtypeStruct((depth, pixels), jnp.bfloat16),
        input_output_aliases={3: 0} if extra else {},
        compiler_params=pltpu.CompilerParams(vmem_limit_bytes=32 << 20),
        cost_estimate=pl.CostEstimate(
            flops=2 * rows * depth * width, bytes_accessed=2 * depth * width, transcendentals=0
        ),
    )(at, own, other, *extra)


def expanded(first_beam, weight, shift_x, shift_y, cutoff, imaginary, tile_count):
    local = weight.shape[1]
    half = SIDE // 2
    beam = first_beam + jnp.arange(local, dtype=jnp.int32)
    freq_x = (beam % SIDE - half)[:, None]
    freq_y = (beam // SIDE - half)[:, None]
    ramp = (freq_x * shift_x[None, :] + freq_y * shift_y[None, :]) % GRID
    phase = ramp.astype(jnp.float32) * (TWO_PI / GRID)
    inside = freq_x * freq_x + freq_y * freq_y <= cutoff[None, :]
    cosine = jnp.cos(phase)
    sine = jnp.sin(phase)
    w_real = weight[0][:, None]
    w_imag = weight[1][:, None]
    c_real = jnp.where(inside, w_real * cosine + w_imag * sine, 0.0).astype(jnp.bfloat16)
    c_imag = jnp.where(inside, w_imag * cosine - w_real * sine, 0.0).astype(jnp.bfloat16)
    by_real = jnp.where(imaginary, c_imag, c_real)
    by_imag = jnp.where(imaginary, c_real, -c_imag)
    step = GRID // TILE_SIDE
    window = shift_x // step * TILE_SIDE + shift_y // step
    onehot = window[None, :] == jnp.arange(tile_count, dtype=jnp.int32)[:, None]
    both = jnp.stack([by_real, by_imag])
    spread = jnp.where(onehot[None, None], both[:, :, None, :], jnp.zeros((), jnp.bfloat16))
    return spread.reshape(2 * local * tile_count, shift_x.shape[0])


def body(count, s_matrix, beam_weight, probe_shift, probe_cutoff, target, target_exp):
    _, local, tile_count, pixels = s_matrix.shape
    stages = count.bit_length() - 2
    own_probes = probe_cutoff.shape[0]
    block = 2 * own_probes
    params = jnp.concatenate([probe_shift.T, probe_cutoff[None]], axis=0)
    params = jnp.concatenate([params, params], axis=1)
    for stage in list(range(stages - 1, -1, -1)) + [-1]:
        params = jnp.concatenate([params, swap(params, count, stage)], axis=1)
    rows = params.shape[1]
    imaginary = (jnp.arange(rows, dtype=jnp.int32) // own_probes % 2 == 1)[None, :]
    at = expanded(
        lax.axis_index("beam") * local, beam_weight, params[0], params[1], params[2], imaginary, tile_count
    )
    s_flat = s_matrix.reshape(2 * local * tile_count, pixels)
    scale = jnp.exp2(target_exp.astype(jnp.float32))[None, :, None]
    width = pixels // CHUNKS
    states = [forward(at, s_flat, chunk, width) for chunk in range(CHUNKS)]
    for stage in range(-1, stages):
        for chunk in range(CHUNKS):
            keep, send = states[chunk]
            total = keep + swap(send, count, stage).astype(jnp.float32)
            half = total.shape[0] // 2
            states[chunk] = (total[:half], total[half:].astype(jnp.bfloat16)) if stage < stages - 1 else total
    held = []
    for chunk in range(CHUNKS):
        part = target[:, :, chunk * width : (chunk + 1) * width].astype(jnp.float32) * scale
        held.append((states[chunk] - part.reshape(block, width)).astype(jnp.bfloat16))
    for stage in range(stages - 1, -1, -1):
        for chunk in range(CHUNKS):
            held[chunk] = jnp.concatenate([held[chunk], swap(held[chunk], count, stage)], axis=0)
    grad = None
    for chunk in range(CHUNKS):
        grad = backward(at, held[chunk], swap(held[chunk], count, -1), grad, chunk, pixels)
    return grad.reshape(2, local, tile_count, pixels)


def solution(mesh):
    return jax.shard_map(
        functools.partial(body, mesh.shape["beam"]),
        mesh=mesh,
        in_specs=(
            P(None, ("grp", "beam"), None, None),
            P(None, ("grp", "beam")),
            P(("grp", "beam"), None),
            P(("grp", "beam")),
            P(None, ("grp", "beam"), None),
            P(("grp", "beam")),
        ),
        out_specs=P(None, ("grp", "beam"), None, None),
        check_vma=False,
    )
```

time: 236 us -> 84.6 us (0.36)
  waiting for transfers between devices: 159 us -> 18.3 us
  starting transfers between devices: 0.22 us -> 37.1 us
  blocking collectives: 27.6 us -> 0 us
  matrix products: 18 us -> 0 us
  Pallas kernels: 0 us -> 17.6 us
  between operations: 14.2 us -> 0.21 us
  other arithmetic: 10.8 us -> 4.34 us
    psum x1 -> x0, waiting for transfers between devices: 114 us -> none  [body(): full_re, full_im = lax.psum((wave_re, wave_im), 'beam')]
    all_gather x1 -> x0, waiting for transfers between devices: 44.4 us -> none  [body(): whole_targets = lax.all_gather(target, 'beam', axis=1, tiled=True)]
    ppermute x0 -> x20, starting transfers between devices: none -> 37.1 us  [swap(): return lax.ppermute(x, 'beam', pairs)]
    all_gather x1 -> x0, blocking collectives: 23.2 us -> none  [body(): lax.all_gather(probe_shift, 'beam', axis=0, tiled=True)]
    ppermute x0 -> x20, waiting for transfers between devices: none -> 18.3 us  [swap(): return lax.ppermute(x, 'beam', pairs)]
    dot_general x4 -> x0, matrix products: 18 us -> none  [the longest x1 9.63 us: body(): wave_re = jnp.dot(left_re, s_flat, preferred_element_type=jnp.float32)]
    pallas_call x0 -> x4, Pallas kernels: none -> 17.6 us  [the longest x2 9.68 us: backward(): pl.pallas_call(backward_kernel, grid=(steps,), in_specs=[pl.BlockSpec((de...]
    another operation x1, other arithmetic: 6.75 us -> 0.01 us  [expanded(): both = jnp.stack([by_real, by_imag])]
  transfers between devices with their start and end apart: 2 -> 20, of which waited for: 2 -> 13; matrix products, arithmetic and copies ran while one was open for 0% -> 2% of each run, Pallas kernels for 0% -> 10%
where the time goes in v1:
time: 84.6 us; the launch traced here: 84.4 us
  starting transfers between devices  37.1 us (44%)
  waiting for transfers between devices  18.3 us (22%)
  Pallas kernels  17.6 us (21%)
  local copies, waits for them, and re-layouts  6.84 us (8%)
  other arithmetic  4.34 us (5%)
    ppermute x20, starting transfers between devices, swap(): return lax.ppermute(x, 'beam', pairs)  37.1 us
    ppermute x20, waiting for transfers between devices, swap(): return lax.ppermute(x, 'beam', pairs)  18.3 us
    pallas_call x2, Pallas kernels, backward(): pl.pallas_call(backward_kernel, grid=(steps,), in_specs=[pl.BlockSpec((de...  9.68 us
    pallas_call x2, Pallas kernels, forward(): pl.pallas_call(forward_kernel, grid=(steps,), in_specs=[pl.BlockSpec((dep...  7.91 us
    unnamed x6, local copies, waits for them, and re-layouts  5.78 us
  transfers between devices with their start and end apart: 20, of which 13 were waited for; matrix products, arithmetic and copies ran while one was open for 2% of the time, Pallas kernels for 10%

profile of v1, /device:TPU:1, one launch (start us, length us, event | category | flops | bytes accessed | tf_op | source)
XLA Modules:
  0.0 84.4 jit_solution(16818127804801801414)
XLA Ops:
  0.0 0.8 add_add_fusion
  0.8 3.1 %collective-permute-start = (s32[3,16]{1,0:T(4,128)S(1)}, s32[3,16]{1,0:T(4,128)S(1)}, u32[]{:S(2)}, u32[]{:S(2)}) collective-permute-start(s32[3,16]{1,0:T(4,128)S(1)} %add_add_fusion), channel_id=1, source_target_pairs={{0,8},{1,9},{2,10},{3,11},{4,12},{5,13},{6,14},{7,15},{8,0},{9,1},... | collective-permute-start | bytes 584 | tf_op jit(solution)/shard_map/ppermute | solution.py:34
  4.0 0.7 pad_add_fusion
  4.7 0.8 slice_bitcast_fusion
  5.4 0.8 pad_add_fusion.1
  6.3 1.2 %collective-permute-start.1 = (s32[3,32]{1,0:T(4,128)S(1)}, s32[3,32]{1,0:T(4,128)S(1)}, u32[]{:S(2)}, u32[]{:S(2)}) collective-permute-start(s32[3,32]{1,0:T(4,128)S(1)} %pad_add_fusion.1), channel_id=1, source_target_pairs={{0,4},{1,3},{2,6},{3,1},{4,0},{5,7},{6,2},{7,5},{8,12},{9,11},{10,... | collective-permute-start | bytes 1160 | tf_op jit(solution)/shard_map/ppermute | solution.py:34
  7.5 1.2 %collective-permute-done.1 = s32[3,32]{1,0:T(4,128)S(1)} collective-permute-done((s32[3,32]{1,0:T(4,128)S(1)}, s32[3,32]{1,0:T(4,128)S(1)}, u32[]{:S(2)}, u32[]{:S(2)}) %collective-permute-start.1) | collective-permute-done | bytes 416 | tf_op jit(solution)/shard_map/ppermute | solution.py:34
  8.7 0.8 pad_add_fusion.2
  9.5 1.3 %collective-permute-start.2 = (s32[3,64]{1,0:T(4,128)S(1)}, s32[3,64]{1,0:T(4,128)S(1)}, u32[]{:S(2)}, u32[]{:S(2)}) collective-permute-start(s32[3,64]{1,0:T(4,128)S(1)} %pad_add_fusion.2), channel_id=1, source_target_pairs={{0,2},{1,5},{2,0},{3,7},{4,6},{5,1},{6,4},{7,3},{8,10},{9,13},{10,... | collective-permute-start | bytes 2312 | tf_op jit(solution)/shard_map/ppermute | solution.py:34
  10.9 1.1 %collective-permute-done.2 = s32[3,64]{1,0:T(4,128)S(1)} collective-permute-done((s32[3,64]{1,0:T(4,128)S(1)}, s32[3,64]{1,0:T(4,128)S(1)}, u32[]{:S(2)}, u32[]{:S(2)}) %collective-permute-start.2) | collective-permute-done | bytes 800 | tf_op jit(solution)/shard_map/ppermute | solution.py:34
  12.0 0.1 concatenate.48
  12.1 3.4 %collective-permute-start.3 = (s32[3,128]{1,0:T(4,128)S(1)}, s32[3,128]{1,0:T(4,128)S(1)}, u32[]{:S(2)}, u32[]{:S(2)}) collective-permute-start(s32[3,128]{1,0:T(4,128)S(1)} %concatenate.48), channel_id=1, source_target_pairs={{0,1},{1,0},{2,3},{3,2},{4,5},{5,4},{6,7},{7,6},{8,9},{9,8},{10,11... | collective-permute-start | bytes 4616 | tf_op jit(solution)/shard_map/ppermute | solution.py:34
  15.4 0.8 collective-permute-done.3
  16.3 0.1 concatenate.49
  16.4 0.4 broadcast_select_fusion.1
  16.9 5.8 %copy-done = bf16[2,64,16,4096]{3,2,1,0:T(8,128)(2,1)S(1)} copy-done((bf16[2,64,16,4096]{3,2,1,0:T(8,128)(2,1)S(1)}, bf16[2,64,16,4096]{3,2,1,0:T(8,128)(2,1)}, u32[]{:S(2)}) %copy-start) | copy-done | bytes 16777240
  22.7 3.9 %shard_map.65 = (f32[128,2048]{1,0:T(8,128)S(1)}, bf16[128,2048]{1,0:T(8,128)(2,1)S(1)}) custom-call(bf16[2048,256]{1,0:T(8,128)(2,1)S(1)} %bitcast.19, bf16[2048,4096]{1,0:T(8,128)(2,1)S(1)} %bitcast.17), custom_call_target="tpu_custom_call" | custom-call | flops 2147483648 | bytes 8388608 | tf_op jit(solution)/shard_map/pallas_call | solution.py:53
  26.6 0.4 collective-permute-start.12
  27.0 4.0 %shard_map.64 = (f32[128,2048]{1,0:T(8,128)S(1)}, bf16[128,2048]{1,0:T(8,128)(2,1)S(1)}) custom-call(bf16[2048,256]{1,0:T(8,128)(2,1)S(1)} %bitcast.20, bf16[2048,4096]{1,0:T(8,128)(2,1)S(1)} %bitcast.18), custom_call_target="tpu_custom_call" | custom-call | flops 2147483648 | bytes 8388608 | tf_op jit(solution)/shard_map/pallas_call | solution.py:53
  31.0 0.2 collective-permute-start.4
  31.3 0.1 convert_add_fusion
  31.4 1.7 %collective-permute-start.13 = (bf16[64,2048]{1,0:T(8,128)(2,1)S(1)}, bf16[64,2048]{1,0:T(8,128)(2,1)S(1)}, u32[]{:S(2)}, u32[]{:S(2)}) collective-permute-start(bf16[64,2048]{1,0:T(8,128)(2,1)S(1)} %slice.129), channel_id=1, source_target_pairs={{0,2},{1,5},{2,0},{3,7},{4,6},{5,1},{6,4},{7,3},{8,10},{9,13},{10,... | collective-permute-start | bytes 786440 | tf_op jit(solution)/shard_map/ppermute | solution.py:34
  33.1 0.1 convert_add_fusion.1
  33.3 1.6 %collective-permute-start.5 = (bf16[64,2048]{1,0:T(8,128)(2,1)S(1)}, bf16[64,2048]{1,0:T(8,128)(2,1)S(1)}, u32[]{:S(2)}, u32[]{:S(2)}) collective-permute-start(bf16[64,2048]{1,0:T(8,128)(2,1)S(1)} %slice.130), channel_id=1, source_target_pairs={{0,2},{1,5},{2,0},{3,7},{4,6},{5,1},{6,4},{7,3},{8,10},{9,13},{10,... | collective-permute-start | bytes 786440 | tf_op jit(solution)/shard_map/ppermute | solution.py:34
  34.8 2.3 %collective-permute-done.13 = bf16[64,2048]{1,0:T(8,128)(2,1)S(1)} collective-permute-done((bf16[64,2048]{1,0:T(8,128)(2,1)S(1)}, bf16[64,2048]{1,0:T(8,128)(2,1)S(1)}, u32[]{:S(2)}, u32[]{:S(2)}) %collective-permute-start.13) | collective-permute-done | bytes 262176 | tf_op jit(solution)/shard_map/ppermute | solution.py:34
  37.2 1.5 %collective-permute-start.14 = (bf16[32,2048]{1,0:T(8,128)(2,1)S(1)}, bf16[32,2048]{1,0:T(8,128)(2,1)S(1)}, u32[]{:S(2)}, u32[]{:S(2)}) collective-permute-start(bf16[32,2048]{1,0:T(8,128)(2,1)S(1)} %slice.131), channel_id=1, source_target_pairs={{0,4},{1,3},{2,6},{3,1},{4,0},{5,7},{6,2},{7,5},{8,12},{9,11},{10,... | collective-permute-start | bytes 393224 | tf_op jit(solution)/shard_map/ppermute | solution.py:34
  38.7 1.3 %collective-permute-done.5 = bf16[64,2048]{1,0:T(8,128)(2,1)S(1)} collective-permute-done((bf16[64,2048]{1,0:T(8,128)(2,1)S(1)}, bf16[64,2048]{1,0:T(8,128)(2,1)S(1)}, u32[]{:S(2)}, u32[]{:S(2)}) %collective-permute-start.5) | collective-permute-done | bytes 262176 | tf_op jit(solution)/shard_map/ppermute | solution.py:34
  40.0 1.5 %collective-permute-start.6 = (bf16[32,2048]{1,0:T(8,128)(2,1)S(1)}, bf16[32,2048]{1,0:T(8,128)(2,1)S(1)}, u32[]{:S(2)}, u32[]{:S(2)}) collective-permute-start(bf16[32,2048]{1,0:T(8,128)(2,1)S(1)} %slice.132), channel_id=1, source_target_pairs={{0,4},{1,3},{2,6},{3,1},{4,0},{5,7},{6,2},{7,5},{8,12},{9,11},{10,... | collective-permute-start | bytes 393224 | tf_op jit(solution)/shard_map/ppermute | solution.py:34
  41.5 0.5 collective-permute-done.14
  42.0 2.7 %collective-permute-start.15 = (bf16[16,2048]{1,0:T(8,128)(2,1)S(1)}, bf16[16,2048]{1,0:T(8,128)(2,1)S(1)}, u32[]{:S(2)}, u32[]{:S(2)}) collective-permute-start(bf16[16,2048]{1,0:T(8,128)(2,1)S(1)} %slice.133), channel_id=1, source_target_pairs={{0,8},{1,9},{2,10},{3,11},{4,12},{5,13},{6,14},{7,15},{8,0},{9,1},... | collective-permute-start | bytes 196616 | tf_op jit(solution)/shard_map/ppermute | solution.py:34
  44.8 1.7 %collective-permute-start.7 = (bf16[16,2048]{1,0:T(8,128)(2,1)S(1)}, bf16[16,2048]{1,0:T(8,128)(2,1)S(1)}, u32[]{:S(2)}, u32[]{:S(2)}) collective-permute-start(bf16[16,2048]{1,0:T(8,128)(2,1)S(1)} %slice.134), channel_id=1, source_target_pairs={{0,8},{1,9},{2,10},{3,11},{4,12},{5,13},{6,14},{7,15},{8,0},{9,1},... | collective-permute-start | bytes 196616 | tf_op jit(solution)/shard_map/ppermute | solution.py:34
  46.6 4.0 %collective-permute-done.7 = bf16[16,2048]{1,0:T(8,128)(2,1)S(1)} collective-permute-done((bf16[16,2048]{1,0:T(8,128)(2,1)S(1)}, bf16[16,2048]{1,0:T(8,128)(2,1)S(1)}, u32[]{:S(2)}, u32[]{:S(2)}) %collective-permute-start.7) | collective-permute-done | bytes 65568 | tf_op jit(solution)/shard_map/ppermute | solution.py:34
  50.6 0.1 fusion.1
  50.7 0.9 %collective-permute-start.16 = (bf16[16,2048]{1,0:T(8,128)(2,1)S(1)}, bf16[16,2048]{1,0:T(8,128)(2,1)S(1)}, u32[]{:S(2)}, u32[]{:S(2)}) collective-permute-start(bf16[16,2048]{1,0:T(8,128)(2,1)S(1)} %get-tuple-element.13), channel_id=1, source_target_pairs={{0,8},{1,9},{2,10},{3,11},{4,12},{5,13},{6,14},{7,15},{8,0},{9,1},... | collective-permute-start | bytes 196616 | tf_op jit(solution)/shard_map/ppermute | solution.py:34
  51.6 1.5 %collective-permute-start.8 = (bf16[16,2048]{1,0:T(8,128)(2,1)S(1)}, bf16[16,2048]{1,0:T(8,128)(2,1)S(1)}, u32[]{:S(2)}, u32[]{:S(2)}) collective-permute-start(bf16[16,2048]{1,0:T(8,128)(2,1)S(1)} %get-tuple-element.14), channel_id=1, source_target_pairs={{0,8},{1,9},{2,10},{3,11},{4,12},{5,13},{6,14},{7,15},{8,0},{9,1},... | collective-permute-start | bytes 196616 | tf_op jit(solution)/shard_map/ppermute | solution.py:34
  53.1 1.6 %collective-permute-done.16 = bf16[16,2048]{1,0:T(8,128)(2,1)S(1)} collective-permute-done((bf16[16,2048]{1,0:T(8,128)(2,1)S(1)}, bf16[16,2048]{1,0:T(8,128)(2,1)S(1)}, u32[]{:S(2)}, u32[]{:S(2)}) %collective-permute-start.16) | collective-permute-done | bytes 65568 | tf_op jit(solution)/shard_map/ppermute | solution.py:34
  54.8 1.3 %collective-permute-start.17 = (bf16[32,2048]{1,0:T(8,128)(2,1)S(1)}, bf16[32,2048]{1,0:T(8,128)(2,1)S(1)}, u32[]{:S(2)}, u32[]{:S(2)}) collective-permute-start(bf16[32,2048]{1,0:T(8,128)(2,1)S(1)} %pad_maximum_fusion.5), channel_id=1, source_target_pairs={{0,4},{1,3},{2,6},{3,1},{4,0},{5,7},{6,2},{7,5},{8,12},{9,11},{10,... | collective-permute-start | bytes 393224 | tf_op jit(solution)/shard_map/ppermute | solution.py:34
  56.1 0.2 collective-permute-done.8
  56.3 1.3 %collective-permute-start.9 = (bf16[32,2048]{1,0:T(8,128)(2,1)S(1)}, bf16[32,2048]{1,0:T(8,128)(2,1)S(1)}, u32[]{:S(2)}, u32[]{:S(2)}) collective-permute-start(bf16[32,2048]{1,0:T(8,128)(2,1)S(1)} %pad_maximum_fusion.4), channel_id=1, source_target_pairs={{0,4},{1,3},{2,6},{3,1},{4,0},{5,7},{6,2},{7,5},{8,12},{9,11},{10,... | collective-permute-start | bytes 393224 | tf_op jit(solution)/shard_map/ppermute | solution.py:34
  57.6 1.0 %collective-permute-done.17 = bf16[32,2048]{1,0:T(8,128)(2,1)S(1)} collective-permute-done((bf16[32,2048]{1,0:T(8,128)(2,1)S(1)}, bf16[32,2048]{1,0:T(8,128)(2,1)S(1)}, u32[]{:S(2)}, u32[]{:S(2)}) %collective-permute-start.17) | collective-permute-done | bytes 131104 | tf_op jit(solution)/shard_map/ppermute | solution.py:34
  58.7 1.5 %collective-permute-start.18 = (bf16[64,2048]{1,0:T(8,128)(2,1)S(1)}, bf16[64,2048]{1,0:T(8,128)(2,1)S(1)}, u32[]{:S(2)}, u32[]{:S(2)}) collective-permute-start(bf16[64,2048]{1,0:T(8,128)(2,1)S(1)} %pad_maximum_fusion.3), channel_id=1, source_target_pairs={{0,2},{1,5},{2,0},{3,7},{4,6},{5,1},{6,4},{7,3},{8,10},{9,13},{10,... | collective-permute-start | bytes 786440 | tf_op jit(solution)/shard_map/ppermute | solution.py:34
  60.2 0.3 collective-permute-done.9
  60.5 2.1 %collective-permute-start.10 = (bf16[64,2048]{1,0:T(8,128)(2,1)S(1)}, bf16[64,2048]{1,0:T(8,128)(2,1)S(1)}, u32[]{:S(2)}, u32[]{:S(2)}) collective-permute-start(bf16[64,2048]{1,0:T(8,128)(2,1)S(1)} %pad_maximum_fusion.2), channel_id=1, source_target_pairs={{0,2},{1,5},{2,0},{3,7},{4,6},{5,1},{6,4},{7,3},{8,10},{9,13},{10,... | collective-permute-start | bytes 786440 | tf_op jit(solution)/shard_map/ppermute | solution.py:34
  62.6 3.8 %collective-permute-done.18 = bf16[64,2048]{1,0:T(8,128)(2,1)S(1)} collective-permute-done((bf16[64,2048]{1,0:T(8,128)(2,1)S(1)}, bf16[64,2048]{1,0:T(8,128)(2,1)S(1)}, u32[]{:S(2)}, u32[]{:S(2)}) %collective-permute-start.18) | collective-permute-done | bytes 262176 | tf_op jit(solution)/shard_map/ppermute | solution.py:34
  66.4 5.2 %collective-permute-start.19 = (bf16[128,2048]{1,0:T(8,128)(2,1)S(1)}, bf16[128,2048]{1,0:T(8,128)(2,1)S(1)}, u32[]{:S(2)}, u32[]{:S(2)}) collective-permute-start(bf16[128,2048]{1,0:T(8,128)(2,1)S(1)} %pad_maximum_fusion.1.own_ref), channel_id=1, source_target_pairs={{0,1},{1,0},{2,3},{3,2},{4,5},{5,4},{6,7},{7,6},{8,9},{9,8},{10,11... | collective-permute-start | bytes 1572872 | tf_op jit(solution)/shard_map/ppermute | solution.py:34
  71.7 3.0 %collective-permute-start.11 = (bf16[128,2048]{1,0:T(8,128)(2,1)S(1)}, bf16[128,2048]{1,0:T(8,128)(2,1)S(1)}, u32[]{:S(2)}, u32[]{:S(2)}) collective-permute-start(bf16[128,2048]{1,0:T(8,128)(2,1)S(1)} %pad_maximum_fusion.own_ref), channel_id=1, source_target_pairs={{0,1},{1,0},{2,3},{3,2},{4,5},{5,4},{6,7},{7,6},{8,9},{9,8},{10,11... | collective-permute-start | bytes 1572872 | tf_op jit(solution)/shard_map/ppermute | solution.py:34
  74.7 4.8 %shard_map.66.refs_0_ = bf16[2048,4096]{1,0:T(8,128)(2,1)} custom-call(bf16[2048,256]{1,0:T(8,128)(2,1)S(1)} %bitcast.21, bf16[128,2048]{1,0:T(8,128)(2,1)S(1)} %pad_maximum_fusion.1.own_ref, bf16[128,2048]{1,0:T(8,128)(2,1)S(1)} %collective-permute-done.19.other_ref), custom_call_target="tpu_custom_call" | custom-call | flops 2147483648 | bytes 8388608 | tf_op jit(solution)/shard_map/pallas_call | solution.py:88
  79.5 4.8 %shard_map.67 = bf16[2048,4096]{1,0:T(8,128)(2,1)} custom-call(bf16[2048,256]{1,0:T(8,128)(2,1)S(1)} %bitcast.22, bf16[128,2048]{1,0:T(8,128)(2,1)S(1)} %pad_maximum_fusion.own_ref, bf16[128,2048]{1,0:T(8,128)(2,1)S(1)} %collective-permute-done.11.other_ref, bf16[2048,4096]{1,0:T(8,128)(2,1)} %shard_map.66.refs_0_), custom_call_target="tpu_custom_call", output_to_operand_aliasing={{}: (3, {})} | custom-call | flops 2147483648 | bytes 8388608 | tf_op jit(solution)/shard_map/pallas_call | solution.py:88
  (37 shorter events, 0.6 us)
Async XLA Ops:
  0.8 4.6 %collective-permute-start = (s32[3,16]{1,0:T(4,128)S(1)}, s32[3,16]{1,0:T(4,128)S(1)}, u32[]{:S(2)}, u32[]{:S(2)}) collective-permute-start(s32[3,16]{1,0:T(4,128)S(1)} %add_add_fusion), channel_id=1, source_target_pairs={{0,8},{1,9},{2,10},{3,11},{4,12},{5,13},{6,14},{7,15},{8,0},{9,1},... | collective-permute-start | bytes 584 | tf_op jit(solution)/shard_map/ppermute | solution.py:34
  6.3 2.4 %collective-permute-start.1 = (s32[3,32]{1,0:T(4,128)S(1)}, s32[3,32]{1,0:T(4,128)S(1)}, u32[]{:S(2)}, u32[]{:S(2)}) collective-permute-start(s32[3,32]{1,0:T(4,128)S(1)} %pad_add_fusion.1), channel_id=1, source_target_pairs={{0,4},{1,3},{2,6},{3,1},{4,0},{5,7},{6,2},{7,5},{8,12},{9,11},{10,... | collective-permute-start | bytes 1160 | tf_op jit(solution)/shard_map/ppermute | solution.py:34
  9.5 2.4 %collective-permute-start.2 = (s32[3,64]{1,0:T(4,128)S(1)}, s32[3,64]{1,0:T(4,128)S(1)}, u32[]{:S(2)}, u32[]{:S(2)}) collective-permute-start(s32[3,64]{1,0:T(4,128)S(1)} %pad_add_fusion.2), channel_id=1, source_target_pairs={{0,2},{1,5},{2,0},{3,7},{4,6},{5,1},{6,4},{7,3},{8,10},{9,13},{10,... | collective-permute-start | bytes 2312 | tf_op jit(solution)/shard_map/ppermute | solution.py:34
  12.1 4.2 %collective-permute-start.3 = (s32[3,128]{1,0:T(4,128)S(1)}, s32[3,128]{1,0:T(4,128)S(1)}, u32[]{:S(2)}, u32[]{:S(2)}) collective-permute-start(s32[3,128]{1,0:T(4,128)S(1)} %concatenate.48), channel_id=1, source_target_pairs={{0,1},{1,0},{2,3},{3,2},{4,5},{5,4},{6,7},{7,6},{8,9},{9,8},{10,11... | collective-permute-start | bytes 4616 | tf_op jit(solution)/shard_map/ppermute | solution.py:34
  16.9 5.8 %copy-start = (bf16[2,64,16,4096]{3,2,1,0:T(8,128)(2,1)S(1)}, bf16[2,64,16,4096]{3,2,1,0:T(8,128)(2,1)}, u32[]{:S(2)}) copy-start(bf16[2,64,16,4096]{3,2,1,0:T(8,128)(2,1)} %param.6) | copy-start | bytes 50331652
  26.6 19.9 %copy-start.2 = (s32[8]{0:T(128)S(1)}, s32[8]{0:T(128)}, u32[]{:S(2)}) copy-start(s32[8]{0:T(128)} %param.11) | copy-start | bytes 100
  26.6 23.9 %copy-start.1 = (bf16[2,8,4096]{2,1,0:T(8,128)(2,1)S(1)}, bf16[2,8,4096]{2,1,0:T(8,128)(2,1)}, u32[]{:S(2)}) copy-start(bf16[2,8,4096]{2,1,0:T(8,128)(2,1)} %param.10) | copy-start | bytes 393220
  26.6 4.6 %collective-permute-start.12 = (bf16[128,2048]{1,0:T(8,128)(2,1)S(1)}, bf16[128,2048]{1,0:T(8,128)(2,1)S(1)}, u32[]{:S(2)}, u32[]{:S(2)}) collective-permute-start(bf16[128,2048]{1,0:T(8,128)(2,1)S(1)} %get-tuple-element.12), channel_id=1, source_target_pairs={{0,1},{1,0},{2,3},{3,2},{4,5},{5,4},{6,7},{7,6},{8,9},{9,8},{10,11... | collective-permute-start | bytes 1572872 | tf_op jit(solution)/shard_map/ppermute | solution.py:34
  31.0 2.1 %collective-permute-start.4 = (bf16[128,2048]{1,0:T(8,128)(2,1)S(1)}, bf16[128,2048]{1,0:T(8,128)(2,1)S(1)}, u32[]{:S(2)}, u32[]{:S(2)}) collective-permute-start(bf16[128,2048]{1,0:T(8,128)(2,1)S(1)} %get-tuple-element.10), channel_id=1, source_target_pairs={{0,1},{1,0},{2,3},{3,2},{4,5},{5,4},{6,7},{7,6},{8,9},{9,8},{10,11... | collective-permute-start | bytes 1572872 | tf_op jit(solution)/shard_map/ppermute | solution.py:34
  31.4 5.7 %collective-permute-start.13 = (bf16[64,2048]{1,0:T(8,128)(2,1)S(1)}, bf16[64,2048]{1,0:T(8,128)(2,1)S(1)}, u32[]{:S(2)}, u32[]{:S(2)}) collective-permute-start(bf16[64,2048]{1,0:T(8,128)(2,1)S(1)} %slice.129), channel_id=1, source_target_pairs={{0,2},{1,5},{2,0},{3,7},{4,6},{5,1},{6,4},{7,3},{8,10},{9,13},{10,... | collective-permute-start | bytes 786440 | tf_op jit(solution)/shard_map/ppermute | solution.py:34
  33.3 6.7 %collective-permute-start.5 = (bf16[64,2048]{1,0:T(8,128)(2,1)S(1)}, bf16[64,2048]{1,0:T(8,128)(2,1)S(1)}, u32[]{:S(2)}, u32[]{:S(2)}) collective-permute-start(bf16[64,2048]{1,0:T(8,128)(2,1)S(1)} %slice.130), channel_id=1, source_target_pairs={{0,2},{1,5},{2,0},{3,7},{4,6},{5,1},{6,4},{7,3},{8,10},{9,13},{10,... | collective-permute-start | bytes 786440 | tf_op jit(solution)/shard_map/ppermute | solution.py:34
  37.2 4.8 %collective-permute-start.14 = (bf16[32,2048]{1,0:T(8,128)(2,1)S(1)}, bf16[32,2048]{1,0:T(8,128)(2,1)S(1)}, u32[]{:S(2)}, u32[]{:S(2)}) collective-permute-start(bf16[32,2048]{1,0:T(8,128)(2,1)S(1)} %slice.131), channel_id=1, source_target_pairs={{0,4},{1,3},{2,6},{3,1},{4,0},{5,7},{6,2},{7,5},{8,12},{9,11},{10,... | collective-permute-start | bytes 393224 | tf_op jit(solution)/shard_map/ppermute | solution.py:34
  40.0 4.7 %collective-permute-start.6 = (bf16[32,2048]{1,0:T(8,128)(2,1)S(1)}, bf16[32,2048]{1,0:T(8,128)(2,1)S(1)}, u32[]{:S(2)}, u32[]{:S(2)}) collective-permute-start(bf16[32,2048]{1,0:T(8,128)(2,1)S(1)} %slice.132), channel_id=1, source_target_pairs={{0,4},{1,3},{2,6},{3,1},{4,0},{5,7},{6,2},{7,5},{8,12},{9,11},{10,... | collective-permute-start | bytes 393224 | tf_op jit(solution)/shard_map/ppermute | solution.py:34
  42.0 4.5 %collective-permute-start.15 = (bf16[16,2048]{1,0:T(8,128)(2,1)S(1)}, bf16[16,2048]{1,0:T(8,128)(2,1)S(1)}, u32[]{:S(2)}, u32[]{:S(2)}) collective-permute-start(bf16[16,2048]{1,0:T(8,128)(2,1)S(1)} %slice.133), channel_id=1, source_target_pairs={{0,8},{1,9},{2,10},{3,11},{4,12},{5,13},{6,14},{7,15},{8,0},{9,1},... | collective-permute-start | bytes 196616 | tf_op jit(solution)/shard_map/ppermute | solution.py:34
  44.8 5.8 %collective-permute-start.7 = (bf16[16,2048]{1,0:T(8,128)(2,1)S(1)}, bf16[16,2048]{1,0:T(8,128)(2,1)S(1)}, u32[]{:S(2)}, u32[]{:S(2)}) collective-permute-start(bf16[16,2048]{1,0:T(8,128)(2,1)S(1)} %slice.134), channel_id=1, source_target_pairs={{0,8},{1,9},{2,10},{3,11},{4,12},{5,13},{6,14},{7,15},{8,0},{9,1},... | collective-permute-start | bytes 196616 | tf_op jit(solution)/shard_map/ppermute | solution.py:34
  50.7 4.1 %collective-permute-start.16 = (bf16[16,2048]{1,0:T(8,128)(2,1)S(1)}, bf16[16,2048]{1,0:T(8,128)(2,1)S(1)}, u32[]{:S(2)}, u32[]{:S(2)}) collective-permute-start(bf16[16,2048]{1,0:T(8,128)(2,1)S(1)} %get-tuple-element.13), channel_id=1, source_target_pairs={{0,8},{1,9},{2,10},{3,11},{4,12},{5,13},{6,14},{7,15},{8,0},{9,1},... | collective-permute-start | bytes 196616 | tf_op jit(solution)/shard_map/ppermute | solution.py:34
  51.6 4.7 %collective-permute-start.8 = (bf16[16,2048]{1,0:T(8,128)(2,1)S(1)}, bf16[16,2048]{1,0:T(8,128)(2,1)S(1)}, u32[]{:S(2)}, u32[]{:S(2)}) collective-permute-start(bf16[16,2048]{1,0:T(8,128)(2,1)S(1)} %get-tuple-element.14), channel_id=1, source_target_pairs={{0,8},{1,9},{2,10},{3,11},{4,12},{5,13},{6,14},{7,15},{8,0},{9,1},... | collective-permute-start | bytes 196616 | tf_op jit(solution)/shard_map/ppermute | solution.py:34
  54.8 3.9 %collective-permute-start.17 = (bf16[32,2048]{1,0:T(8,128)(2,1)S(1)}, bf16[32,2048]{1,0:T(8,128)(2,1)S(1)}, u32[]{:S(2)}, u32[]{:S(2)}) collective-permute-start(bf16[32,2048]{1,0:T(8,128)(2,1)S(1)} %pad_maximum_fusion.5), channel_id=1, source_target_pairs={{0,4},{1,3},{2,6},{3,1},{4,0},{5,7},{6,2},{7,5},{8,12},{9,11},{10,... | collective-permute-start | bytes 393224 | tf_op jit(solution)/shard_map/ppermute | solution.py:34
  56.3 4.1 %collective-permute-start.9 = (bf16[32,2048]{1,0:T(8,128)(2,1)S(1)}, bf16[32,2048]{1,0:T(8,128)(2,1)S(1)}, u32[]{:S(2)}, u32[]{:S(2)}) collective-permute-start(bf16[32,2048]{1,0:T(8,128)(2,1)S(1)} %pad_maximum_fusion.4), channel_id=1, source_target_pairs={{0,4},{1,3},{2,6},{3,1},{4,0},{5,7},{6,2},{7,5},{8,12},{9,11},{10,... | collective-permute-start | bytes 393224 | tf_op jit(solution)/shard_map/ppermute | solution.py:34
  58.7 7.7 %collective-permute-start.18 = (bf16[64,2048]{1,0:T(8,128)(2,1)S(1)}, bf16[64,2048]{1,0:T(8,128)(2,1)S(1)}, u32[]{:S(2)}, u32[]{:S(2)}) collective-permute-start(bf16[64,2048]{1,0:T(8,128)(2,1)S(1)} %pad_maximum_fusion.3), channel_id=1, source_target_pairs={{0,2},{1,5},{2,0},{3,7},{4,6},{5,1},{6,4},{7,3},{8,10},{9,13},{10,... | collective-permute-start | bytes 786440 | tf_op jit(solution)/shard_map/ppermute | solution.py:34
  60.5 11.2 %collective-permute-start.10 = (bf16[64,2048]{1,0:T(8,128)(2,1)S(1)}, bf16[64,2048]{1,0:T(8,128)(2,1)S(1)}, u32[]{:S(2)}, u32[]{:S(2)}) collective-permute-start(bf16[64,2048]{1,0:T(8,128)(2,1)S(1)} %pad_maximum_fusion.2), channel_id=1, source_target_pairs={{0,2},{1,5},{2,0},{3,7},{4,6},{5,1},{6,4},{7,3},{8,10},{9,13},{10,... | collective-permute-start | bytes 786440 | tf_op jit(solution)/shard_map/ppermute | solution.py:34
  66.4 8.2 %collective-permute-start.19 = (bf16[128,2048]{1,0:T(8,128)(2,1)S(1)}, bf16[128,2048]{1,0:T(8,128)(2,1)S(1)}, u32[]{:S(2)}, u32[]{:S(2)}) collective-permute-start(bf16[128,2048]{1,0:T(8,128)(2,1)S(1)} %pad_maximum_fusion.1.own_ref), channel_id=1, source_target_pairs={{0,1},{1,0},{2,3},{3,2},{4,5},{5,4},{6,7},{7,6},{8,9},{9,8},{10,11... | collective-permute-start | bytes 1572872 | tf_op jit(solution)/shard_map/ppermute | solution.py:34
  71.7 7.8 %collective-permute-start.11 = (bf16[128,2048]{1,0:T(8,128)(2,1)S(1)}, bf16[128,2048]{1,0:T(8,128)(2,1)S(1)}, u32[]{:S(2)}, u32[]{:S(2)}) collective-permute-start(bf16[128,2048]{1,0:T(8,128)(2,1)S(1)} %pad_maximum_fusion.own_ref), channel_id=1, source_target_pairs={{0,1},{1,0},{2,3},{3,2},{4,5},{5,4},{6,7},{7,6},{8,9},{9,8},{10,11... | collective-permute-start | bytes 1572872 | tf_op jit(solution)/shard_map/ppermute | solution.py:34

commit v2 on v1

v2 whole, which is shorter than its diff:
```python
import functools
import math

import jax
import jax.numpy as jnp
from jax import lax
from jax.experimental import pallas as pl
from jax.experimental.pallas import tpu as pltpu
from jax.sharding import PartitionSpec as P

SIDE = 32
GRID = 192
TILE_SIDE = 4
TWO_PI = 2.0 * math.pi
CHUNKS = 2
PIECES = 2
FWD_COLUMNS = 512
BWD_ROWS = 256


def orders(count):
    masks = [1 << bit for bit in range(1, count.bit_length() - 1)]
    other = masks[:]
    if len(other) > 1:
        other[0], other[1] = other[1], other[0]
    return masks, other


def swap(x, count, stage):
    if stage < 0:
        pairs = [(i, i ^ 1) for i in range(count)]
    else:
        by_core = orders(count)
        pairs = [(i, i ^ by_core[i % 2][stage]) for i in range(count)]
    return lax.ppermute(x, "beam", pairs)


def stage_kernel(first_row, s_ref, out_ref, sem):
    rows, columns = out_ref.shape
    copy = pltpu.make_async_copy(s_ref.at[first_row : first_row + rows, 0:columns], out_ref, sem)
    copy.start()
    copy.wait()


def staged(s_flat, first_row, rows, columns):
    return pl.pallas_call(
        functools.partial(stage_kernel, first_row),
        in_specs=[pl.BlockSpec(memory_space=pl.ANY)],
        out_specs=pl.BlockSpec(memory_space=pltpu.VMEM),
        out_shape=pltpu.VMEM((rows, columns), s_flat.dtype),
        scratch_shapes=[pltpu.SemaphoreType.DMA],
        compiler_params=pltpu.CompilerParams(vmem_limit_bytes=20 << 20),
        cost_estimate=pl.CostEstimate(flops=0, bytes_accessed=2 * rows * columns, transcendentals=0),
    )(pltpu.with_memory_space_constraint(s_flat, pltpu.HBM))


def forward_kernel(count, next_column, waits, at_ref, *refs):
    pieces, refs = refs[:count], refs[count + waits :]
    copy = None
    if next_column is None:
        keep_ref, send_ref = refs
    else:
        s_ref, keep_ref, send_ref, next_ref, sem = refs
        columns = next_ref.shape[1]
        copy = pltpu.make_async_copy(s_ref.at[:, next_column : next_column + columns], next_ref, sem)
        copy.start()
    a = at_ref[...].T
    half, width = keep_ref.shape
    for start in range(0, width, FWD_COLUMNS):
        stop = start + FWD_COLUMNS
        wave, done = 0.0, 0
        for piece in pieces:
            rows = piece.shape[0]
            wave += jnp.dot(
                a[:, done : done + rows], piece[:, start:stop], preferred_element_type=jnp.float32
            )
            done += rows
        keep_ref[:, start:stop] = wave[:half]
        send_ref[:, start:stop] = wave[half:].astype(jnp.bfloat16)
    if copy is not None:
        copy.wait()


def forward(at, pieces, s_flat, next_column, after):
    depth, rows = at.shape
    half, width = rows // 2, pieces[0].shape[1]
    whole = pl.BlockSpec(memory_space=pltpu.VMEM)
    more = next_column is not None
    return pl.pallas_call(
        functools.partial(forward_kernel, len(pieces), next_column, len(after)),
        in_specs=[whole] * (1 + len(pieces)) + [pl.BlockSpec(memory_space=pl.ANY)] * (len(after) + more),
        out_specs=[whole] * (2 + more),
        out_shape=[
            jax.ShapeDtypeStruct((half, width), jnp.float32),
            jax.ShapeDtypeStruct((half, width), jnp.bfloat16),
        ]
        + [pltpu.VMEM((depth, width), s_flat.dtype)] * more,
        scratch_shapes=[pltpu.SemaphoreType.DMA] * more,
        compiler_params=pltpu.CompilerParams(vmem_limit_bytes=30 << 20),
        cost_estimate=pl.CostEstimate(
            flops=2 * rows * depth * width, bytes_accessed=2 * depth * width, transcendentals=0
        ),
    )(at, *pieces, *after, *([pltpu.with_memory_space_constraint(s_flat, pltpu.HBM)] if more else []))


def backward_kernel(first, at_ref, own_ref, other_ref, *refs):
    out_ref, held_ref, sems = refs[-3:]
    depth, width = held_ref.shape
    res = jnp.concatenate([own_ref[...], other_ref[...]], axis=0)
    copies = []
    for index, start in enumerate(range(0, depth, BWD_ROWS)):
        stop = start + BWD_ROWS
        held_ref[start:stop] = jnp.dot(
            at_ref[start:stop], res, preferred_element_type=jnp.float32
        ).astype(jnp.bfloat16)
        copies.append(
            pltpu.make_async_copy(
                held_ref.at[start:stop], out_ref.at[start:stop, first : first + width], sems.at[index]
            )
        )
        copies[-1].start()
    for copy in copies:
        copy.wait()


def backward(at, own, other, so_far, chunk, pixels):
    depth, rows = at.shape
    half, width = own.shape
    whole = pl.BlockSpec(memory_space=pltpu.VMEM)
    extra = [] if so_far is None else [so_far]
    return pl.pallas_call(
        functools.partial(backward_kernel, chunk * width),
        in_specs=[whole] * 3 + [pl.BlockSpec(memory_space=pl.ANY) for _ in extra],
        out_specs=pl.BlockSpec(memory_space=pl.ANY),
        out_shape=jax.ShapeDtypeStruct((depth, pixels), jnp.bfloat16),
        scratch_shapes=[
            pltpu.VMEM((depth, width), jnp.bfloat16),
            pltpu.SemaphoreType.DMA((depth // BWD_ROWS,)),
        ],
        input_output_aliases={3: 0} if extra else {},
        compiler_params=pltpu.CompilerParams(vmem_limit_bytes=30 << 20),
        cost_estimate=pl.CostEstimate(
            flops=2 * rows * depth * width, bytes_accessed=2 * depth * width, transcendentals=0
        ),
    )(at, own, other, *extra)


def joined(parts):
    total, done = 0, 0
    width = sum(part.shape[1] for part in parts)
    for part in parts:
        after = width - done - part.shape[1]
        total = total + lax.pad(part, jnp.zeros((), part.dtype), ((0, 0, 0), (done, after, 0)))
        done += part.shape[1]
    return total


def gathered(x, count):
    by_core = orders(count)

    def spread(core, block):
        return sum(mask for bit, mask in enumerate(reversed(by_core[core])) if block >> bit & 1)

    def fetch(x, source_of):
        return lax.ppermute(x, "beam", [(source_of(i), i) for i in range(count)])

    inner = count // 4
    x = joined([x] + [fetch(x, lambda i, k=k: i ^ spread(i % 2, k)) for k in range(1, inner)])
    return joined(
        [
            x,
            fetch(x, lambda i: i ^ spread(i % 2, inner)),
            fetch(x, lambda i: i ^ 1),
            fetch(x, lambda i: i ^ 1 ^ spread(1 - i % 2, inner)),
        ]
    )


def step(kernel, inputs, outputs, after):
    whole = pl.BlockSpec(memory_space=pltpu.VMEM)

    def run(*refs):
        kernel(*refs[: len(inputs)], *refs[len(inputs) + len(after) :])

    return pl.pallas_call(
        run,
        in_specs=[whole] * len(inputs) + [pl.BlockSpec(memory_space=pl.ANY)] * len(after),
        out_specs=[whole] * len(outputs),
        out_shape=[jax.ShapeDtypeStruct(shape, dtype) for shape, dtype in outputs],
        compiler_params=pltpu.CompilerParams(vmem_limit_bytes=4 << 20),
        cost_estimate=pl.CostEstimate(flops=0, bytes_accessed=0, transcendentals=0),
    )(*inputs, *after)


def halve_kernel(keep_ref, came_ref, near_ref, send_ref):
    half = near_ref.shape[0]
    near_ref[...] = keep_ref[:half] + came_ref[:half].astype(jnp.float32)
    send_ref[...] = (keep_ref[half:] + came_ref[half:].astype(jnp.float32)).astype(jnp.bfloat16)


def halved(keep, came, after):
    half = (keep.shape[0] // 2, keep.shape[1])
    return step(halve_kernel, [keep, came], [(half, jnp.float32), (half, jnp.bfloat16)], after)


def lessen_kernel(keep_ref, came_ref, target_ref, sum_ref, send_ref):
    block = target_ref.shape[0]
    total = keep_ref[...] + came_ref[...].astype(jnp.float32)
    own = total[:block] - target_ref[...].astype(jnp.float32)
    sum_ref[:block] = own
    sum_ref[block:] = total[block:]
    send_ref[:block] = own.astype(jnp.bfloat16)
    send_ref[block:] = total[block:].astype(jnp.bfloat16)


def lessened(keep, came, target, after):
    both = [(keep.shape, jnp.float32), (keep.shape, jnp.bfloat16)]
    return step(lessen_kernel, [keep, came, target], both, after)


def close_kernel(keep_ref, came_ref, out_ref):
    block = keep_ref.shape[0] // 2
    near, far = came_ref[block:], came_ref[:block]
    out_ref[:block] = (keep_ref[:block] + near.astype(jnp.float32)).astype(jnp.bfloat16)
    out_ref[block:] = (keep_ref[block:] + far.astype(jnp.float32)).astype(jnp.bfloat16)


def closed(keep, came, after):
    return step(close_kernel, [keep, came], [(keep.shape, jnp.bfloat16)], after)[0]


def stack_kernel(own_ref, came_ref, out_ref):
    rows = own_ref.shape[0]
    out_ref[:rows] = own_ref[...]
    out_ref[rows:] = came_ref[...]


def stacked(own, came, after):
    shape = (2 * own.shape[0], own.shape[1])
    return step(stack_kernel, [own, came], [(shape, own.dtype)], after)[0]


def expanded(first_beam, weight, shift_x, shift_y, cutoff, imaginary, tile_count):
    local = weight.shape[1]
    half = SIDE // 2
    beam = first_beam + jnp.arange(local, dtype=jnp.int32)
    freq_x = (beam % SIDE - half)[:, None]
    freq_y = (beam // SIDE - half)[:, None]
    ramp = (freq_x * shift_x[None, :] + freq_y * shift_y[None, :]) % GRID
    phase = ramp.astype(jnp.float32) * (TWO_PI / GRID)
    inside = freq_x * freq_x + freq_y * freq_y <= cutoff[None, :]
    cosine = jnp.cos(phase)
    sine = jnp.sin(phase)
    w_real = weight[0][:, None]
    w_imag = weight[1][:, None]
    c_real = jnp.where(inside, w_real * cosine + w_imag * sine, 0.0).astype(jnp.bfloat16)
    c_imag = jnp.where(inside, w_imag * cosine - w_real * sine, 0.0).astype(jnp.bfloat16)
    by_real = jnp.where(imaginary, c_imag, c_real)
    by_imag = jnp.where(imaginary, c_real, -c_imag)
    step = GRID // TILE_SIDE
    window = shift_x // step * TILE_SIDE + shift_y // step
    onehot = window[None, :] == jnp.arange(tile_count, dtype=jnp.int32)[:, None]
    both = jnp.stack([by_real, by_imag])
    spread = jnp.where(onehot[None, None], both[:, :, None, :], jnp.zeros((), jnp.bfloat16))
    return spread.reshape(2 * local * tile_count, shift_x.shape[0])


def body(count, s_matrix, beam_weight, probe_shift, probe_cutoff, target, target_exp):
    _, local, tile_count, pixels = s_matrix.shape
    stages = count.bit_length() - 2
    own_probes = probe_cutoff.shape[0]
    block = 2 * own_probes
    params = jnp.concatenate([probe_shift.T, probe_cutoff[None]], axis=0)
    params = jnp.concatenate([params, params], axis=1)
    params = gathered(params, count)
    rows = params.shape[1]
    imaginary = (jnp.arange(rows, dtype=jnp.int32) // own_probes % 2 == 1)[None, :]
    at = expanded(
        lax.axis_index("beam") * local, beam_weight, params[0], params[1], params[2], imaginary, tile_count
    )
    s_flat = s_matrix.reshape(2 * local * tile_count, pixels)
    scale = jnp.exp2(target_exp.astype(jnp.float32))[None, :, None]
    scaled = (target.astype(jnp.float32) * scale).astype(jnp.bfloat16).reshape(block, pixels)
    width = pixels // CHUNKS
    scaled = lax.optimization_barrier([scaled[:, c * width : (c + 1) * width] for c in range(CHUNKS)])
    depth = s_flat.shape[0] // PIECES
    pieces = [staged(s_flat, piece * depth, depth, width) for piece in range(PIECES)]
    states, after = [], []
    for chunk in range(CHUNKS):
        next_column = (chunk + 1) * width if chunk < CHUNKS - 1 else None
        keep, send, *pieces = forward(at, pieces, s_flat, next_column, after)
        states.append(halved(keep, swap(send, count, -1), after))
        after = [states[-1][1]]
    for stage in range(stages - 1):
        for chunk in range(CHUNKS):
            keep, send = states[chunk]
            after = [states[chunk + 1][1]] if stage == 0 and chunk < CHUNKS - 1 else []
            came = swap(send, count, stage)
            if stage < stages - 2:
                states[chunk] = halved(keep, came, after)
            else:
                states[chunk] = lessened(keep, came, scaled[chunk], after)
    held = [closed(keep, swap(send, count, stages - 1), []) for keep, send in states]
    for stage in range(stages - 2, -1, -1):
        held = [stacked(part, swap(part, count, stage), []) for part in held]
    grad = None
    for chunk in range(CHUNKS):
        grad = backward(at, held[chunk], swap(held[chunk], count, -1), grad, chunk, pixels)
    return grad.reshape(2, local, tile_count, pixels)


def solution(mesh):
    return jax.shard_map(
        functools.partial(body, mesh.shape["beam"]),
        mesh=mesh,
        in_specs=(
            P(None, ("grp", "beam"), None, None),
            P(None, ("grp", "beam")),
            P(("grp", "beam"), None),
            P(("grp", "beam")),
            P(None, ("grp", "beam"), None),
            P(("grp", "beam")),
        ),
        out_specs=P(None, ("grp", "beam"), None, None),
        check_vma=False,
    )
```

time: 84.6 us -> 73.8 us (0.87)
  starting transfers between devices: 37.1 us -> 21.2 us
  waiting for transfers between devices: 18.3 us -> 31.3 us
  local copies, waits for them, and re-layouts: 6.84 us -> 0.78 us
  other arithmetic: 4.34 us -> 1.61 us
    ppermute x20 -> x14, starting transfers between devices: 37.1 us -> 13 us  [swap(): return lax.ppermute(x, 'beam', pairs)]
    ppermute x20 -> x14, waiting for transfers between devices: 18.3 us -> 28.9 us  [swap(): return lax.ppermute(x, 'beam', pairs)]
    ppermute x0 -> x6, starting transfers between devices: none -> 8.21 us  [fetch(): return lax.ppermute(x, 'beam', [(source_of(i), i) for i in range(count)])]
    unnamed x6 -> x4, local copies, waits for them, and re-layouts: 5.78 us -> 0.01 us
    concatenate x9 -> x0, other arithmetic: 2.51 us -> none  [the longest x2 1.67 us: body(): params = jnp.concatenate([params, swap(params, count, stage)], axis=1)]
    ppermute x0 -> x6, waiting for transfers between devices: none -> 2.41 us  [fetch(): return lax.ppermute(x, 'beam', [(source_of(i), i) for i in range(count)])]
    pallas_call x4 -> x18, Pallas kernels: 17.6 us -> 18.3 us  [the longest x2 7.62 us: backward(): pl.pallas_call(functools.partial(backward_kernel, chunk * width), in_spec...]
  transfers between devices with their start and end apart: 20 -> 20, of which waited for: 13 -> 10; matrix products, arithmetic and copies ran while one was open for 2% -> 1% of each run, Pallas kernels for 10% -> 15%
where the time goes in v2:
time: 73.8 us; the launch traced here: 73.5 us
  waiting for transfers between devices  31.3 us (42%)
  starting transfers between devices  21.2 us (29%)
  Pallas kernels  18.3 us (25%)
  other arithmetic  1.61 us (2%)
  local copies, waits for them, and re-layouts  0.78 us (1%)
    ppermute x14, waiting for transfers between devices, swap(): return lax.ppermute(x, 'beam', pairs)  28.9 us
    ppermute x14, starting transfers between devices, swap(): return lax.ppermute(x, 'beam', pairs)  13 us
    ppermute x6, starting transfers between devices, fetch(): return lax.ppermute(x, 'beam', [(source_of(i), i) for i in range(count)])  8.21 us
    pallas_call x2, Pallas kernels, backward(): pl.pallas_call(functools.partial(backward_kernel, chunk * width), in_spec...  7.62 us
    pallas_call x2, Pallas kernels, forward(): pl.pallas_call(functools.partial(forward_kernel, len(pieces), next_column...  5.81 us
    pallas_call x2, Pallas kernels, staged(): pl.pallas_call(functools.partial(stage_kernel, first_row), in_specs=[pl.B...  4.39 us
    ppermute x6, waiting for transfers between devices, fetch(): return lax.ppermute(x, 'beam', [(source_of(i), i) for i in range(count)])  2.41 us
  transfers between devices with their start and end apart: 20, of which 10 were waited for; matrix products, arithmetic and copies ran while one was open for 1% of the time, Pallas kernels for 15%

profile of v2, /device:TPU:1, one launch (start us, length us, event | category | flops | bytes accessed | tf_op | source)
XLA Modules:
  0.0 73.5 jit_solution(11481425578443026004)
XLA Ops:
  0.0 0.8 %add_add_fusion = s32[3,16]{1,0:T(4,128)S(1)} fusion(s32[1,8]{1,0:T(1,128)} %bitcast.27, s32[2,8]{1,0:T(2,128)} %bitcast.26), kind=kLoop, calls=%fused_computation.24 | loop fusion | flops 144 | bytes 288 | tf_op jit(solution)/shard_map/concatenate | solution.py:274
  0.8 4.1 %collective-permute-start.2 = (s32[3,16]{1,0:T(4,128)S(1)}, s32[3,16]{1,0:T(4,128)S(1)}, u32[]{:S(2)}, u32[]{:S(2)}) collective-permute-start(s32[3,16]{1,0:T(4,128)S(1)} %add_add_fusion), channel_id=1, source_target_pairs={{12,0},{11,1},{14,2},{9,3},{8,4},{15,5},{10,6},{13,7},{4,8},{3,9},... | collective-permute-start | bytes 584 | tf_op jit(solution)/shard_map/ppermute | solution.py:165
  4.9 0.2 collective-permute-start.1
  5.2 0.1 collective-permute-start
  5.3 0.8 %slice_bitcast_fusion = (f32[64]{0:T(128)S(1)}, f32[64]{0:T(128)S(1)}) fusion(f32[2,64]{1,0:T(2,128)} %param.7), kind=kLoop, calls=%fused_computation.46 | loop fusion | bytes 1024 | tf_op jit(solution)/shard_map/slice | solution.py:254
  6.1 1.3 %collective-permute-done.1 = s32[3,16]{1,0:T(4,128)S(1)} collective-permute-done((s32[3,16]{1,0:T(4,128)S(1)}, s32[3,16]{1,0:T(4,128)S(1)}, u32[]{:S(2)}, u32[]{:S(2)}) %collective-permute-start.1) | collective-permute-done | bytes 224 | tf_op jit(solution)/shard_map/ppermute | solution.py:165
  7.4 1.1 %collective-permute-done = s32[3,16]{1,0:T(4,128)S(1)} collective-permute-done((s32[3,16]{1,0:T(4,128)S(1)}, s32[3,16]{1,0:T(4,128)S(1)}, u32[]{:S(2)}, u32[]{:S(2)}) %collective-permute-start) | collective-permute-done | bytes 224 | tf_op jit(solution)/shard_map/ppermute | solution.py:165
  8.5 0.1 pad_add_fusion
  8.6 3.6 %collective-permute-start.5 = (s32[3,64]{1,0:T(4,128)S(1)}, s32[3,64]{1,0:T(4,128)S(1)}, u32[]{:S(2)}, u32[]{:S(2)}) collective-permute-start(s32[3,64]{1,0:T(4,128)S(1)} %pad_add_fusion), channel_id=1, source_target_pairs={{5,0},{2,1},{7,2},{0,3},{1,4},{6,5},{3,6},{4,7},{13,8},{10,9},{15,... | collective-permute-start | bytes 2312 | tf_op jit(solution)/shard_map/ppermute | solution.py:165
  12.1 0.2 collective-permute-start.3
  12.3 2.2 %shard_map.65.refs_1_ = bf16[1024,2048]{1,0:T(8,128)(2,1)S(1)} custom-call(bf16[2048,4096]{1,0:T(8,128)(2,1)} %bitcast.19), custom_call_target="tpu_custom_call" | custom-call | bytes 4194304 | tf_op jit(solution)/shard_map/pallas_call | solution.py:46
  14.5 2.2 %shard_map.64.refs_0_ = bf16[1024,2048]{1,0:T(8,128)(2,1)S(1)} custom-call(bf16[2048,4096]{1,0:T(8,128)(2,1)} %bitcast.20), custom_call_target="tpu_custom_call" | custom-call | bytes 4194304 | tf_op jit(solution)/shard_map/pallas_call | solution.py:46
  16.7 0.0 copy-start.1
  16.8 0.0 collective-permute-done.3
  16.8 0.1 fusion.12
  16.9 0.4 broadcast_select_fusion.1
  17.3 0.1 broadcast_select_fusion
  17.4 0.0 copy-start
  17.4 3.5 %shard_map.66 = (f32[128,2048]{1,0:T(8,128)S(1)}, bf16[128,2048]{1,0:T(8,128)(2,1)S(1)}, bf16[2048,2048]{1,0:T(8,128)(2,1)S(1)}) custom-call(bf16[2048,256]{1,0:T(8,128)(2,1)S(1)} %bitcast.15, bf16[1024,2048]{1,0:T(8,128)(2,1)S(1)} %shard_map.64.refs_0_, bf16[1024,2048]{1,0:T(8,128)(2,1)S(1)} %shard_map.65.refs_1_, bf16[2048,4096]{1,0:T(8,128)(2,1)} %bitcast.21), custom_call_target="tpu_custom_call" | custom-call | flops 2147483648 | bytes 8388608 | tf_op jit(solution)/shard_map/pallas_call | solution.py:89
  20.9 1.9 %collective-permute-start.6 = (bf16[128,2048]{1,0:T(8,128)(2,1)S(1)}, bf16[128,2048]{1,0:T(8,128)(2,1)S(1)}, u32[]{:S(2)}, u32[]{:S(2)}) collective-permute-start(bf16[128,2048]{1,0:T(8,128)(2,1)S(1)} %get-tuple-element.26), channel_id=1, source_target_pairs={{0,1},{1,0},{2,3},{3,2},{4,5},{5,4},{6,7},{7,6},{8,9},{9,8},{10,11... | collective-permute-start | bytes 1572872 | tf_op jit(solution)/shard_map/ppermute | solution.py:35
  22.8 1.5 %collective-permute-done.6.refs_1_ = bf16[128,2048]{1,0:T(8,128)(2,1)S(1)} collective-permute-done((bf16[128,2048]{1,0:T(8,128)(2,1)S(1)}, bf16[128,2048]{1,0:T(8,128)(2,1)S(1)}, u32[]{:S(2)}, u32[]{:S(2)}) %collective-permute-start.6) | collective-permute-done | bytes 524320 | tf_op jit(solution)/shard_map/ppermute | solution.py:35
  24.3 0.1 shard_map.67
  24.4 0.1 collective-permute-start.14
  24.5 2.4 %shard_map.68 = (f32[128,2048]{1,0:T(8,128)S(1)}, bf16[128,2048]{1,0:T(8,128)(2,1)S(1)}) custom-call(bf16[2048,256]{1,0:T(8,128)(2,1)S(1)} %bitcast.16, bf16[2048,2048]{1,0:T(8,128)(2,1)S(1)} %get-tuple-element.24.refs_0_, bf16[64,2048]{1,0:T(8,128)(2,1)S(1)} %get-tuple-element.27.refs_1_.refs_2_), custom_call_target="tpu_custom_call" | custom-call | flops 2147483648 | bytes 8388608 | tf_op jit(solution)/shard_map/pallas_call | solution.py:89
  26.8 0.9 %collective-permute-start.7 = (bf16[128,2048]{1,0:T(8,128)(2,1)S(1)}, bf16[128,2048]{1,0:T(8,128)(2,1)S(1)}, u32[]{:S(2)}, u32[]{:S(2)}) collective-permute-start(bf16[128,2048]{1,0:T(8,128)(2,1)S(1)} %get-tuple-element.29), channel_id=1, source_target_pairs={{0,1},{1,0},{2,3},{3,2},{4,5},{5,4},{6,7},{7,6},{8,9},{9,8},{10,11... | collective-permute-start | bytes 1572872 | tf_op jit(solution)/shard_map/ppermute | solution.py:35
  27.8 0.1 fusion
  27.9 1.4 %collective-permute-done.7.refs_1_ = bf16[128,2048]{1,0:T(8,128)(2,1)S(1)} collective-permute-done((bf16[128,2048]{1,0:T(8,128)(2,1)S(1)}, bf16[128,2048]{1,0:T(8,128)(2,1)S(1)}, u32[]{:S(2)}, u32[]{:S(2)}) %collective-permute-start.7) | collective-permute-done | bytes 524320 | tf_op jit(solution)/shard_map/ppermute | solution.py:35
  29.3 0.1 shard_map.69
  29.4 1.0 %collective-permute-start.8 = (bf16[64,2048]{1,0:T(8,128)(2,1)S(1)}, bf16[64,2048]{1,0:T(8,128)(2,1)S(1)}, u32[]{:S(2)}, u32[]{:S(2)}) collective-permute-start(bf16[64,2048]{1,0:T(8,128)(2,1)S(1)} %get-tuple-element.31.refs_2_), channel_id=1, source_target_pairs={{0,2},{1,5},{2,0},{3,7},{4,6},{5,1},{6,4},{7,3},{8,10},{9,13},{10,... | collective-permute-start | bytes 786440 | tf_op jit(solution)/shard_map/ppermute | solution.py:35
  30.4 0.0 collective-permute-done.14.refs_1_
  30.5 0.4 collective-permute-start.15
  30.9 5.2 %collective-permute-done.15.refs_1_ = bf16[32,2048]{1,0:T(8,128)(2,1)S(1)} collective-permute-done((bf16[32,2048]{1,0:T(8,128)(2,1)S(1)}, bf16[32,2048]{1,0:T(8,128)(2,1)S(1)}, u32[]{:S(2)}, u32[]{:S(2)}) %collective-permute-start.15) | collective-permute-done | bytes 131104 | tf_op jit(solution)/shard_map/ppermute | solution.py:35
  36.1 0.1 collective-permute-start.16
  36.3 1.4 %collective-permute-start.9 = (bf16[32,2048]{1,0:T(8,128)(2,1)S(1)}, bf16[32,2048]{1,0:T(8,128)(2,1)S(1)}, u32[]{:S(2)}, u32[]{:S(2)}) collective-permute-start(bf16[32,2048]{1,0:T(8,128)(2,1)S(1)} %get-tuple-element.33), channel_id=1, source_target_pairs={{0,4},{1,3},{2,6},{3,1},{4,0},{5,7},{6,2},{7,5},{8,12},{9,11},{10,... | collective-permute-start | bytes 393224 | tf_op jit(solution)/shard_map/ppermute | solution.py:35
  37.7 7.4 %collective-permute-done.16.refs_1_ = bf16[32,2048]{1,0:T(8,128)(2,1)S(1)} collective-permute-done((bf16[32,2048]{1,0:T(8,128)(2,1)S(1)}, bf16[32,2048]{1,0:T(8,128)(2,1)S(1)}, u32[]{:S(2)}, u32[]{:S(2)}) %collective-permute-start.16) | collective-permute-done | bytes 131104 | tf_op jit(solution)/shard_map/ppermute | solution.py:35
  45.1 0.1 collective-permute-start.17
  45.3 0.1 collective-permute-start.10
  45.3 4.0 %collective-permute-done.17.refs_1_ = bf16[32,2048]{1,0:T(8,128)(2,1)S(1)} collective-permute-done((bf16[32,2048]{1,0:T(8,128)(2,1)S(1)}, bf16[32,2048]{1,0:T(8,128)(2,1)S(1)}, u32[]{:S(2)}, u32[]{:S(2)}) %collective-permute-start.17) | collective-permute-done | bytes 131104 | tf_op jit(solution)/shard_map/ppermute | solution.py:35
  49.3 0.1 collective-permute-start.18
  49.4 3.3 %collective-permute-done.10.refs_1_ = bf16[32,2048]{1,0:T(8,128)(2,1)S(1)} collective-permute-done((bf16[32,2048]{1,0:T(8,128)(2,1)S(1)}, bf16[32,2048]{1,0:T(8,128)(2,1)S(1)}, u32[]{:S(2)}, u32[]{:S(2)}) %collective-permute-start.10) | collective-permute-done | bytes 131104 | tf_op jit(solution)/shard_map/ppermute | solution.py:35
  52.7 1.8 %collective-permute-start.11 = (bf16[32,2048]{1,0:T(8,128)(2,1)S(1)}, bf16[32,2048]{1,0:T(8,128)(2,1)S(1)}, u32[]{:S(2)}, u32[]{:S(2)}) collective-permute-start(bf16[32,2048]{1,0:T(8,128)(2,1)S(1)} %shard_map.72.refs_0_), channel_id=1, source_target_pairs={{0,4},{1,3},{2,6},{3,1},{4,0},{5,7},{6,2},{7,5},{8,12},{9,11},{10,... | collective-permute-start | bytes 393224 | tf_op jit(solution)/shard_map/ppermute | solution.py:35
  54.5 3.3 %collective-permute-done.11.refs_1_ = bf16[32,2048]{1,0:T(8,128)(2,1)S(1)} collective-permute-done((bf16[32,2048]{1,0:T(8,128)(2,1)S(1)}, bf16[32,2048]{1,0:T(8,128)(2,1)S(1)}, u32[]{:S(2)}, u32[]{:S(2)}) %collective-permute-start.11) | collective-permute-done | bytes 131104 | tf_op jit(solution)/shard_map/ppermute | solution.py:35
  57.8 0.1 collective-permute-start.12
  57.9 2.7 %collective-permute-start.19 = (bf16[128,2048]{1,0:T(8,128)(2,1)S(1)}, bf16[128,2048]{1,0:T(8,128)(2,1)S(1)}, u32[]{:S(2)}, u32[]{:S(2)}) collective-permute-start(bf16[128,2048]{1,0:T(8,128)(2,1)S(1)} %shard_map.79.own_ref), channel_id=1, source_target_pairs={{0,1},{1,0},{2,3},{3,2},{4,5},{5,4},{6,7},{7,6},{8,9},{9,8},{10,11... | collective-permute-start | bytes 1572872 | tf_op jit(solution)/shard_map/ppermute | solution.py:35
  60.6 2.8 %collective-permute-done.12.refs_1_ = bf16[64,2048]{1,0:T(8,128)(2,1)S(1)} collective-permute-done((bf16[64,2048]{1,0:T(8,128)(2,1)S(1)}, bf16[64,2048]{1,0:T(8,128)(2,1)S(1)}, u32[]{:S(2)}, u32[]{:S(2)}) %collective-permute-start.12) | collective-permute-done | bytes 262176 | tf_op jit(solution)/shard_map/ppermute | solution.py:35
  63.4 2.5 %collective-permute-start.13 = (bf16[128,2048]{1,0:T(8,128)(2,1)S(1)}, bf16[128,2048]{1,0:T(8,128)(2,1)S(1)}, u32[]{:S(2)}, u32[]{:S(2)}) collective-permute-start(bf16[128,2048]{1,0:T(8,128)(2,1)S(1)} %shard_map.74.own_ref), channel_id=1, source_target_pairs={{0,1},{1,0},{2,3},{3,2},{4,5},{5,4},{6,7},{7,6},{8,9},{9,8},{10,11... | collective-permute-start | bytes 1572872 | tf_op jit(solution)/shard_map/ppermute | solution.py:35
  65.9 3.8 %shard_map.80.refs_0_ = bf16[2048,4096]{1,0:T(8,128)(2,1)} custom-call(bf16[2048,256]{1,0:T(8,128)(2,1)S(1)} %bitcast.17, bf16[128,2048]{1,0:T(8,128)(2,1)S(1)} %shard_map.79.own_ref, bf16[128,2048]{1,0:T(8,128)(2,1)S(1)} %collective-permute-done.19.other_ref), custom_call_target="tpu_custom_call" | custom-call | flops 2147483648 | bytes 8388608 | tf_op jit(solution)/shard_map/pallas_call | solution.py:131
  69.7 3.8 %shard_map.81 = bf16[2048,4096]{1,0:T(8,128)(2,1)} custom-call(bf16[2048,256]{1,0:T(8,128)(2,1)S(1)} %bitcast.18, bf16[128,2048]{1,0:T(8,128)(2,1)S(1)} %shard_map.74.own_ref, bf16[128,2048]{1,0:T(8,128)(2,1)S(1)} %collective-permute-done.13.other_ref, bf16[2048,4096]{1,0:T(8,128)(2,1)} %shard_map.80.refs_0_), custom_call_target="tpu_custom_call", output_to_operand_aliasing={{}: (3, {})} | custom-call | flops 2147483648 | bytes 8388608 | tf_op jit(solution)/shard_map/pallas_call | solution.py:131
  (28 shorter events, 0.4 us)
Async XLA Ops:
  0.8 5.2 %collective-permute-start.2 = (s32[3,16]{1,0:T(4,128)S(1)}, s32[3,16]{1,0:T(4,128)S(1)}, u32[]{:S(2)}, u32[]{:S(2)}) collective-permute-start(s32[3,16]{1,0:T(4,128)S(1)} %add_add_fusion), channel_id=1, source_target_pairs={{12,0},{11,1},{14,2},{9,3},{8,4},{15,5},{10,6},{13,7},{4,8},{3,9},... | collective-permute-start | bytes 584 | tf_op jit(solution)/shard_map/ppermute | solution.py:165
  4.9 2.4 %collective-permute-start.1 = (s32[3,16]{1,0:T(4,128)S(1)}, s32[3,16]{1,0:T(4,128)S(1)}, u32[]{:S(2)}, u32[]{:S(2)}) collective-permute-start(s32[3,16]{1,0:T(4,128)S(1)} %add_add_fusion), channel_id=1, source_target_pairs={{4,0},{3,1},{6,2},{1,3},{0,4},{7,5},{2,6},{5,7},{12,8},{11,9},{14,... | collective-permute-start | bytes 584 | tf_op jit(solution)/shard_map/ppermute | solution.py:165
  5.2 3.3 %collective-permute-start = (s32[3,16]{1,0:T(4,128)S(1)}, s32[3,16]{1,0:T(4,128)S(1)}, u32[]{:S(2)}, u32[]{:S(2)}) collective-permute-start(s32[3,16]{1,0:T(4,128)S(1)} %add_add_fusion), channel_id=1, source_target_pairs={{8,0},{9,1},{10,2},{11,3},{12,4},{13,5},{14,6},{15,7},{0,8},{1,9},... | collective-permute-start | bytes 584 | tf_op jit(solution)/shard_map/ppermute | solution.py:165
  8.6 8.2 %collective-permute-start.5 = (s32[3,64]{1,0:T(4,128)S(1)}, s32[3,64]{1,0:T(4,128)S(1)}, u32[]{:S(2)}, u32[]{:S(2)}) collective-permute-start(s32[3,64]{1,0:T(4,128)S(1)} %pad_add_fusion), channel_id=1, source_target_pairs={{5,0},{2,1},{7,2},{0,3},{1,4},{6,5},{3,6},{4,7},{13,8},{10,9},{15,... | collective-permute-start | bytes 2312 | tf_op jit(solution)/shard_map/ppermute | solution.py:165
  12.1 4.6 %collective-permute-start.4 = (s32[3,64]{1,0:T(4,128)S(1)}, s32[3,64]{1,0:T(4,128)S(1)}, u32[]{:S(2)}, u32[]{:S(2)}) collective-permute-start(s32[3,64]{1,0:T(4,128)S(1)} %pad_add_fusion), channel_id=1, source_target_pairs={{1,0},{0,1},{3,2},{2,3},{5,4},{4,5},{7,6},{6,7},{9,8},{8,9},{11,10... | collective-permute-start | bytes 2312 | tf_op jit(solution)/shard_map/ppermute | solution.py:165
  12.1 4.6 %collective-permute-start.3 = (s32[3,64]{1,0:T(4,128)S(1)}, s32[3,64]{1,0:T(4,128)S(1)}, u32[]{:S(2)}, u32[]{:S(2)}) collective-permute-start(s32[3,64]{1,0:T(4,128)S(1)} %pad_add_fusion), channel_id=1, source_target_pairs={{2,0},{5,1},{0,2},{7,3},{6,4},{1,5},{4,6},{3,7},{10,8},{13,9},{8,1... | collective-permute-start | bytes 2312 | tf_op jit(solution)/shard_map/ppermute | solution.py:165
  16.7 6.0 %copy-start.1 = (s32[8]{0:T(128)S(1)}, s32[8]{0:T(128)}, u32[]{:S(2)}) copy-start(s32[8]{0:T(128)} %param.11) | copy-start | bytes 100
  17.4 10.4 %copy-start = (bf16[2,8,4096]{2,1,0:T(8,128)(2,1)S(1)}, bf16[2,8,4096]{2,1,0:T(8,128)(2,1)}, u32[]{:S(2)}) copy-start(bf16[2,8,4096]{2,1,0:T(8,128)(2,1)} %param.10) | copy-start | bytes 393220
  20.9 3.5 %collective-permute-start.6 = (bf16[128,2048]{1,0:T(8,128)(2,1)S(1)}, bf16[128,2048]{1,0:T(8,128)(2,1)S(1)}, u32[]{:S(2)}, u32[]{:S(2)}) collective-permute-start(bf16[128,2048]{1,0:T(8,128)(2,1)S(1)} %get-tuple-element.26), channel_id=1, source_target_pairs={{0,1},{1,0},{2,3},{3,2},{4,5},{5,4},{6,7},{7,6},{8,9},{9,8},{10,11... | collective-permute-start | bytes 1572872 | tf_op jit(solution)/shard_map/ppermute | solution.py:35
  24.4 6.0 %collective-permute-start.14 = (bf16[64,2048]{1,0:T(8,128)(2,1)S(1)}, bf16[64,2048]{1,0:T(8,128)(2,1)S(1)}, u32[]{:S(2)}, u32[]{:S(2)}) collective-permute-start(bf16[64,2048]{1,0:T(8,128)(2,1)S(1)} %get-tuple-element.27.refs_1_.refs_2_), channel_id=1, source_target_pairs={{0,2},{1,5},{2,0},{3,7},{4,6},{5,1},{6,4},{7,3},{8,10},{9,13},{10,... | collective-permute-start | bytes 786440 | tf_op jit(solution)/shard_map/ppermute | solution.py:35
  26.8 2.5 %collective-permute-start.7 = (bf16[128,2048]{1,0:T(8,128)(2,1)S(1)}, bf16[128,2048]{1,0:T(8,128)(2,1)S(1)}, u32[]{:S(2)}, u32[]{:S(2)}) collective-permute-start(bf16[128,2048]{1,0:T(8,128)(2,1)S(1)} %get-tuple-element.29), channel_id=1, source_target_pairs={{0,1},{1,0},{2,3},{3,2},{4,5},{5,4},{6,7},{7,6},{8,9},{9,8},{10,11... | collective-permute-start | bytes 1572872 | tf_op jit(solution)/shard_map/ppermute | solution.py:35
  29.4 6.8 %collective-permute-start.8 = (bf16[64,2048]{1,0:T(8,128)(2,1)S(1)}, bf16[64,2048]{1,0:T(8,128)(2,1)S(1)}, u32[]{:S(2)}, u32[]{:S(2)}) collective-permute-start(bf16[64,2048]{1,0:T(8,128)(2,1)S(1)} %get-tuple-element.31.refs_2_), channel_id=1, source_target_pairs={{0,2},{1,5},{2,0},{3,7},{4,6},{5,1},{6,4},{7,3},{8,10},{9,13},{10,... | collective-permute-start | bytes 786440 | tf_op jit(solution)/shard_map/ppermute | solution.py:35
  30.5 5.6 %collective-permute-start.15 = (bf16[32,2048]{1,0:T(8,128)(2,1)S(1)}, bf16[32,2048]{1,0:T(8,128)(2,1)S(1)}, u32[]{:S(2)}, u32[]{:S(2)}) collective-permute-start(bf16[32,2048]{1,0:T(8,128)(2,1)S(1)} %get-tuple-element.39), channel_id=1, source_target_pairs={{0,4},{1,3},{2,6},{3,1},{4,0},{5,7},{6,2},{7,5},{8,12},{9,11},{10,... | collective-permute-start | bytes 393224 | tf_op jit(solution)/shard_map/ppermute | solution.py:35
  36.1 9.0 %collective-permute-start.16 = (bf16[32,2048]{1,0:T(8,128)(2,1)S(1)}, bf16[32,2048]{1,0:T(8,128)(2,1)S(1)}, u32[]{:S(2)}, u32[]{:S(2)}) collective-permute-start(bf16[32,2048]{1,0:T(8,128)(2,1)S(1)} %get-tuple-element.42), channel_id=1, source_target_pairs={{0,8},{1,9},{2,10},{3,11},{4,12},{5,13},{6,14},{7,15},{8,0},{9,1},... | collective-permute-start | bytes 393224 | tf_op jit(solution)/shard_map/ppermute | solution.py:35
  36.3 8.9 %collective-permute-start.9 = (bf16[32,2048]{1,0:T(8,128)(2,1)S(1)}, bf16[32,2048]{1,0:T(8,128)(2,1)S(1)}, u32[]{:S(2)}, u32[]{:S(2)}) collective-permute-start(bf16[32,2048]{1,0:T(8,128)(2,1)S(1)} %get-tuple-element.33), channel_id=1, source_target_pairs={{0,4},{1,3},{2,6},{3,1},{4,0},{5,7},{6,2},{7,5},{8,12},{9,11},{10,... | collective-permute-start | bytes 393224 | tf_op jit(solution)/shard_map/ppermute | solution.py:35
  45.1 4.2 %collective-permute-start.17 = (bf16[32,2048]{1,0:T(8,128)(2,1)S(1)}, bf16[32,2048]{1,0:T(8,128)(2,1)S(1)}, u32[]{:S(2)}, u32[]{:S(2)}) collective-permute-start(bf16[32,2048]{1,0:T(8,128)(2,1)S(1)} %shard_map.77.refs_0_), channel_id=1, source_target_pairs={{0,4},{1,3},{2,6},{3,1},{4,0},{5,7},{6,2},{7,5},{8,12},{9,11},{10,... | collective-permute-start | bytes 393224 | tf_op jit(solution)/shard_map/ppermute | solution.py:35
  45.3 7.4 %collective-permute-start.10 = (bf16[32,2048]{1,0:T(8,128)(2,1)S(1)}, bf16[32,2048]{1,0:T(8,128)(2,1)S(1)}, u32[]{:S(2)}, u32[]{:S(2)}) collective-permute-start(bf16[32,2048]{1,0:T(8,128)(2,1)S(1)} %get-tuple-element.36), channel_id=1, source_target_pairs={{0,8},{1,9},{2,10},{3,11},{4,12},{5,13},{6,14},{7,15},{8,0},{9,1},... | collective-permute-start | bytes 393224 | tf_op jit(solution)/shard_map/ppermute | solution.py:35
  49.3 8.6 %collective-permute-start.18 = (bf16[64,2048]{1,0:T(8,128)(2,1)S(1)}, bf16[64,2048]{1,0:T(8,128)(2,1)S(1)}, u32[]{:S(2)}, u32[]{:S(2)}) collective-permute-start(bf16[64,2048]{1,0:T(8,128)(2,1)S(1)} %shard_map.78.refs_0_), channel_id=1, source_target_pairs={{0,2},{1,5},{2,0},{3,7},{4,6},{5,1},{6,4},{7,3},{8,10},{9,13},{10,... | collective-permute-start | bytes 786440 | tf_op jit(solution)/shard_map/ppermute | solution.py:35
  52.7 5.1 %collective-permute-start.11 = (bf16[32,2048]{1,0:T(8,128)(2,1)S(1)}, bf16[32,2048]{1,0:T(8,128)(2,1)S(1)}, u32[]{:S(2)}, u32[]{:S(2)}) collective-permute-start(bf16[32,2048]{1,0:T(8,128)(2,1)S(1)} %shard_map.72.refs_0_), channel_id=1, source_target_pairs={{0,4},{1,3},{2,6},{3,1},{4,0},{5,7},{6,2},{7,5},{8,12},{9,11},{10,... | collective-permute-start | bytes 393224 | tf_op jit(solution)/shard_map/ppermute | solution.py:35
  57.8 5.6 %collective-permute-start.12 = (bf16[64,2048]{1,0:T(8,128)(2,1)S(1)}, bf16[64,2048]{1,0:T(8,128)(2,1)S(1)}, u32[]{:S(2)}, u32[]{:S(2)}) collective-permute-start(bf16[64,2048]{1,0:T(8,128)(2,1)S(1)} %shard_map.73.refs_0_), channel_id=1, source_target_pairs={{0,2},{1,5},{2,0},{3,7},{4,6},{5,1},{6,4},{7,3},{8,10},{9,13},{10,... | collective-permute-start | bytes 786440 | tf_op jit(solution)/shard_map/ppermute | solution.py:35
  57.9 8.0 %collective-permute-start.19 = (bf16[128,2048]{1,0:T(8,128)(2,1)S(1)}, bf16[128,2048]{1,0:T(8,128)(2,1)S(1)}, u32[]{:S(2)}, u32[]{:S(2)}) collective-permute-start(bf16[128,2048]{1,0:T(8,128)(2,1)S(1)} %shard_map.79.own_ref), channel_id=1, source_target_pairs={{0,1},{1,0},{2,3},{3,2},{4,5},{5,4},{6,7},{7,6},{8,9},{9,8},{10,11... | collective-permute-start | bytes 1572872 | tf_op jit(solution)/shard_map/ppermute | solution.py:35
  63.4 6.3 %collective-permute-start.13 = (bf16[128,2048]{1,0:T(8,128)(2,1)S(1)}, bf16[128,2048]{1,0:T(8,128)(2,1)S(1)}, u32[]{:S(2)}, u32[]{:S(2)}) collective-permute-start(bf16[128,2048]{1,0:T(8,128)(2,1)S(1)} %shard_map.74.own_ref), channel_id=1, source_target_pairs={{0,1},{1,0},{2,3},{3,2},{4,5},{5,4},{6,7},{7,6},{8,9},{9,8},{10,11... | collective-permute-start | bytes 1572872 | tf_op jit(solution)/shard_map/ppermute | solution.py:35

commit v3 on v2

--- a/solution.py
+++ b/solution.py
@@ -139,9 +139,7 @@
         ],
         input_output_aliases={3: 0} if extra else {},
         compiler_params=pltpu.CompilerParams(vmem_limit_bytes=30 << 20),
-        cost_estimate=pl.CostEstimate(
-            flops=2 * rows * depth * width, bytes_accessed=2 * depth * width, transcendentals=0
-        ),
+        cost_estimate=pl.CostEstimate(flops=0, bytes_accessed=0, transcendentals=0),
     )(at, own, other, *extra)
 
 
@@ -155,7 +153,7 @@
     return total
 
 
-def gathered(x, count):
+def gathered(x, count, after):
     by_core = orders(count)
 
     def spread(core, block):
@@ -165,7 +163,8 @@
         return lax.ppermute(x, "beam", [(source_of(i), i) for i in range(count)])
 
     inner = count // 4
-    x = joined([x] + [fetch(x, lambda i, k=k: i ^ spread(i % 2, k)) for k in range(1, inner)])
+    parts = [x] + [fetch(x, lambda i, k=k: i ^ spread(i % 2, k)) for k in range(1, inner)]
+    x = beside(parts, after)
     return joined(
         [
             x,
@@ -190,6 +189,19 @@
         compiler_params=pltpu.CompilerParams(vmem_limit_bytes=4 << 20),
         cost_estimate=pl.CostEstimate(flops=0, bytes_accessed=0, transcendentals=0),
     )(*inputs, *after)
+
+
+def beside_kernel(*refs):
+    done = 0
+    for part_ref in refs[:-1]:
+        width = part_ref.shape[1]
+        refs[-1][:, done : done + width] = part_ref[...]
+        done += width
+
+
+def beside(parts, after):
+    shape = (parts[0].shape[0], sum(part.shape[1] for part in parts))
+    return step(beside_kernel, parts, [(shape, parts[0].dtype)], after)[0]
 
 
 def halve_kernel(keep_ref, came_ref, near_ref, send_ref):
@@ -272,19 +284,19 @@
     block = 2 * own_probes
     params = jnp.concatenate([probe_shift.T, probe_cutoff[None]], axis=0)
     params = jnp.concatenate([params, params], axis=1)
-    params = gathered(params, count)
+    s_flat = s_matrix.reshape(2 * local * tile_count, pixels)
+    depth = s_flat.shape[0] // PIECES
+    width = pixels // CHUNKS
+    pieces = [staged(s_flat, piece * depth, depth, width) for piece in range(PIECES)]
+    params = gathered(params, count, pieces[:1])
     rows = params.shape[1]
     imaginary = (jnp.arange(rows, dtype=jnp.int32) // own_probes % 2 == 1)[None, :]
     at = expanded(
         lax.axis_index("beam") * local, beam_weight, params[0], params[1], params[2], imaginary, tile_count
     )
-    s_flat = s_matrix.reshape(2 * local * tile_count, pixels)
     scale = jnp.exp2(target_exp.astype(jnp.float32))[None, :, None]
     scaled = (target.astype(jnp.float32) * scale).astype(jnp.bfloat16).reshape(block, pixels)
-    width = pixels // CHUNKS
     scaled = lax.optimization_barrier([scaled[:, c * width : (c + 1) * width] for c in range(CHUNKS)])
-    depth = s_flat.shape[0] // PIECES
-    pieces = [staged(s_flat, piece * depth, depth, width) for piece in range(PIECES)]
     states, after = [], []
     for chunk in range(CHUNKS):
         next_column = (chunk + 1) * width if chunk < CHUNKS - 1 else None

time: 73.8 us -> 71.1 us (0.963)
  waiting for transfers between devices: 31.3 us -> 25.9 us
  starting transfers between devices: 21.2 us -> 23.9 us
    ppermute x14, waiting for transfers between devices: 28.9 us -> 25.6 us  [swap(): return lax.ppermute(x, 'beam', pairs)]
    ppermute x14, starting transfers between devices: 13 us -> 15.8 us  [swap(): return lax.ppermute(x, 'beam', pairs)]
    ppermute x6, waiting for transfers between devices: 2.41 us -> 0.27 us  [fetch(): return lax.ppermute(x, 'beam', [(source_of(i), i) for i in range(count)])]
  transfers between devices with their start and end apart: 20 -> 20, of which waited for: 10 -> 13; matrix products, arithmetic and copies ran while one was open for 1% -> 1% of each run, Pallas kernels for 15% -> 12%
where the time goes in v3:
time: 71.1 us; the launch traced here: 70.8 us
  waiting for transfers between devices  25.9 us (36%)
  starting transfers between devices  23.9 us (34%)
  Pallas kernels  18.4 us (26%)
  other arithmetic  1.54 us (2%)
  local copies, waits for them, and re-layouts  0.78 us (1%)
    ppermute x14, waiting for transfers between devices, swap(): return lax.ppermute(x, 'beam', pairs)  25.6 us
    ppermute x14, starting transfers between devices, swap(): return lax.ppermute(x, 'beam', pairs)  15.8 us
    ppermute x6, starting transfers between devices, fetch(): return lax.ppermute(x, 'beam', [(source_of(i), i) for i in range(count)])  8.15 us
    pallas_call x2, Pallas kernels, backward(): pl.pallas_call(functools.partial(backward_kernel, chunk * width), in_spec...  7.62 us
    pallas_call x2, Pallas kernels, forward(): pl.pallas_call(functools.partial(forward_kernel, len(pieces), next_column...  5.81 us
    pallas_call x2, Pallas kernels, staged(): pl.pallas_call(functools.partial(stage_kernel, first_row), in_specs=[pl.B...  4.39 us
  transfers between devices with their start and end apart: 20, of which 13 were waited for; matrix products, arithmetic and copies ran while one was open for 1% of the time, Pallas kernels for 12%

profile of v3, /device:TPU:1, one launch (start us, length us, event | category | flops | bytes accessed | tf_op | source)
XLA Modules:
  0.0 70.8 jit_solution(5693379987664357745)
XLA Ops:
  0.0 0.8 %add_add_fusion.refs_0_ = s32[3,16]{1,0:T(4,128)S(1)} fusion(s32[1,8]{1,0:T(1,128)} %bitcast.27, s32[2,8]{1,0:T(2,128)} %bitcast.26), kind=kLoop, calls=%fused_computation.24 | loop fusion | flops 144 | bytes 288 | tf_op jit(solution)/shard_map/concatenate | solution.py:286
  0.8 4.1 %collective-permute-start.2 = (s32[3,16]{1,0:T(4,128)S(1)}, s32[3,16]{1,0:T(4,128)S(1)}, u32[]{:S(2)}, u32[]{:S(2)}) collective-permute-start(s32[3,16]{1,0:T(4,128)S(1)} %add_add_fusion.refs_0_), channel_id=1, source_target_pairs={{12,0},{11,1},{14,2},{9,3},{8,4},{15,5},{10,6},{13,7},{4,8},{3,9},... | collective-permute-start | bytes 584 | tf_op jit(solution)/shard_map/ppermute | solution.py:163
  4.9 0.2 collective-permute-start.1
  5.2 0.1 collective-permute-start
  5.3 0.8 %slice_bitcast_fusion = (f32[64]{0:T(128)S(1)}, f32[64]{0:T(128)S(1)}) fusion(f32[2,64]{1,0:T(2,128)} %param.7), kind=kLoop, calls=%fused_computation.45 | loop fusion | bytes 1024 | tf_op jit(solution)/shard_map/slice | solution.py:266
  6.1 2.2 %shard_map.64.refs_4_.refs_0_ = bf16[1024,2048]{1,0:T(8,128)(2,1)S(1)} custom-call(bf16[2048,4096]{1,0:T(8,128)(2,1)} %bitcast.19), custom_call_target="tpu_custom_call" | custom-call | bytes 4194304 | tf_op jit(solution)/shard_map/pallas_call | solution.py:46
  8.3 0.2 collective-permute-done.refs_1_
  8.5 0.1 shard_map.65
  8.6 3.6 %collective-permute-start.5 = (s32[3,64]{1,0:T(4,128)S(1)}, s32[3,64]{1,0:T(4,128)S(1)}, u32[]{:S(2)}, u32[]{:S(2)}) collective-permute-start(s32[3,64]{1,0:T(4,128)S(1)} %shard_map.65), channel_id=1, source_target_pairs={{5,0},{2,1},{7,2},{0,3},{1,4},{6,5},{3,6},{4,7},{13,8},{10,9},{15,... | collective-permute-start | bytes 2312 | tf_op jit(solution)/shard_map/ppermute | solution.py:163
  12.1 0.1 collective-permute-start.3
  12.3 2.2 %shard_map.66.refs_1_ = bf16[1024,2048]{1,0:T(8,128)(2,1)S(1)} custom-call(bf16[2048,4096]{1,0:T(8,128)(2,1)} %bitcast.20), custom_call_target="tpu_custom_call" | custom-call | bytes 4194304 | tf_op jit(solution)/shard_map/pallas_call | solution.py:46
  14.5 0.1 collective-permute-done.3
  14.6 0.1 fusion.12
  14.7 0.4 broadcast_select_fusion.1
  15.1 0.1 broadcast_select_fusion
  15.2 0.0 copy-start.1
  15.2 3.5 %shard_map.67 = (f32[128,2048]{1,0:T(8,128)S(1)}, bf16[128,2048]{1,0:T(8,128)(2,1)S(1)}, bf16[2048,2048]{1,0:T(8,128)(2,1)S(1)}) custom-call(bf16[2048,256]{1,0:T(8,128)(2,1)S(1)} %bitcast.15, bf16[1024,2048]{1,0:T(8,128)(2,1)S(1)} %shard_map.64.refs_4_.refs_0_, bf16[1024,2048]{1,0:T(8,128)(2,1)S(1)} %shard_map.66.refs_1_, bf16[2048,4096]{1,0:T(8,128)(2,1)} %bitcast.21), custom_call_target="tpu_custom_call" | custom-call | flops 2147483648 | bytes 8388608 | tf_op jit(solution)/shard_map/pallas_call | solution.py:89
  18.7 1.9 %collective-permute-start.6 = (bf16[128,2048]{1,0:T(8,128)(2,1)S(1)}, bf16[128,2048]{1,0:T(8,128)(2,1)S(1)}, u32[]{:S(2)}, u32[]{:S(2)}) collective-permute-start(bf16[128,2048]{1,0:T(8,128)(2,1)S(1)} %get-tuple-element.26), channel_id=1, source_target_pairs={{0,1},{1,0},{2,3},{3,2},{4,5},{5,4},{6,7},{7,6},{8,9},{9,8},{10,11... | collective-permute-start | bytes 1572872 | tf_op jit(solution)/shard_map/ppermute | solution.py:35
  20.6 1.5 %collective-permute-done.6.refs_1_ = bf16[128,2048]{1,0:T(8,128)(2,1)S(1)} collective-permute-done((bf16[128,2048]{1,0:T(8,128)(2,1)S(1)}, bf16[128,2048]{1,0:T(8,128)(2,1)S(1)}, u32[]{:S(2)}, u32[]{:S(2)}) %collective-permute-start.6) | collective-permute-done | bytes 524320 | tf_op jit(solution)/shard_map/ppermute | solution.py:35
  22.1 0.1 shard_map.68
  22.2 2.4 %shard_map.69 = (f32[128,2048]{1,0:T(8,128)S(1)}, bf16[128,2048]{1,0:T(8,128)(2,1)S(1)}) custom-call(bf16[2048,256]{1,0:T(8,128)(2,1)S(1)} %bitcast.16, bf16[2048,2048]{1,0:T(8,128)(2,1)S(1)} %get-tuple-element.24.refs_0_, bf16[64,2048]{1,0:T(8,128)(2,1)S(1)} %get-tuple-element.27.refs_1_.refs_2_), custom_call_target="tpu_custom_call" | custom-call | flops 2147483648 | bytes 8388608 | tf_op jit(solution)/shard_map/pallas_call | solution.py:89
  24.6 0.4 collective-permute-start.7
  25.0 1.5 %collective-permute-done.7.refs_1_ = bf16[128,2048]{1,0:T(8,128)(2,1)S(1)} collective-permute-done((bf16[128,2048]{1,0:T(8,128)(2,1)S(1)}, bf16[128,2048]{1,0:T(8,128)(2,1)S(1)}, u32[]{:S(2)}, u32[]{:S(2)}) %collective-permute-start.7) | collective-permute-done | bytes 524320 | tf_op jit(solution)/shard_map/ppermute | solution.py:35
  26.5 0.1 shard_map.70
  26.7 0.1 collective-permute-start.8
  26.7 0.1 fusion
  26.8 3.7 %collective-permute-done.14.refs_1_ = bf16[64,2048]{1,0:T(8,128)(2,1)S(1)} collective-permute-done((bf16[64,2048]{1,0:T(8,128)(2,1)S(1)}, bf16[64,2048]{1,0:T(8,128)(2,1)S(1)}, u32[]{:S(2)}, u32[]{:S(2)}) %collective-permute-start.14) | collective-permute-done | bytes 262176 | tf_op jit(solution)/shard_map/ppermute | solution.py:35
  30.5 0.1 shard_map.76
  30.6 1.1 %collective-permute-start.15 = (bf16[32,2048]{1,0:T(8,128)(2,1)S(1)}, bf16[32,2048]{1,0:T(8,128)(2,1)S(1)}, u32[]{:S(2)}, u32[]{:S(2)}) collective-permute-start(bf16[32,2048]{1,0:T(8,128)(2,1)S(1)} %get-tuple-element.39), channel_id=1, source_target_pairs={{0,4},{1,3},{2,6},{3,1},{4,0},{5,7},{6,2},{7,5},{8,12},{9,11},{10,... | collective-permute-start | bytes 393224 | tf_op jit(solution)/shard_map/ppermute | solution.py:35
  31.7 1.6 %collective-permute-done.8.refs_1_ = bf16[64,2048]{1,0:T(8,128)(2,1)S(1)} collective-permute-done((bf16[64,2048]{1,0:T(8,128)(2,1)S(1)}, bf16[64,2048]{1,0:T(8,128)(2,1)S(1)}, u32[]{:S(2)}, u32[]{:S(2)}) %collective-permute-start.8) | collective-permute-done | bytes 262176 | tf_op jit(solution)/shard_map/ppermute | solution.py:35
  33.4 1.1 %collective-permute-start.9 = (bf16[32,2048]{1,0:T(8,128)(2,1)S(1)}, bf16[32,2048]{1,0:T(8,128)(2,1)S(1)}, u32[]{:S(2)}, u32[]{:S(2)}) collective-permute-start(bf16[32,2048]{1,0:T(8,128)(2,1)S(1)} %get-tuple-element.33), channel_id=1, source_target_pairs={{0,4},{1,3},{2,6},{3,1},{4,0},{5,7},{6,2},{7,5},{8,12},{9,11},{10,... | collective-permute-start | bytes 393224 | tf_op jit(solution)/shard_map/ppermute | solution.py:35
  34.5 0.8 %collective-permute-done.15.refs_1_ = bf16[32,2048]{1,0:T(8,128)(2,1)S(1)} collective-permute-done((bf16[32,2048]{1,0:T(8,128)(2,1)S(1)}, bf16[32,2048]{1,0:T(8,128)(2,1)S(1)}, u32[]{:S(2)}, u32[]{:S(2)}) %collective-permute-start.15) | collective-permute-done | bytes 131104 | tf_op jit(solution)/shard_map/ppermute | solution.py:35
  35.4 1.3 %collective-permute-start.16 = (bf16[32,2048]{1,0:T(8,128)(2,1)S(1)}, bf16[32,2048]{1,0:T(8,128)(2,1)S(1)}, u32[]{:S(2)}, u32[]{:S(2)}) collective-permute-start(bf16[32,2048]{1,0:T(8,128)(2,1)S(1)} %get-tuple-element.42), channel_id=1, source_target_pairs={{0,8},{1,9},{2,10},{3,11},{4,12},{5,13},{6,14},{7,15},{8,0},{9,1},... | collective-permute-start | bytes 393224 | tf_op jit(solution)/shard_map/ppermute | solution.py:35
  36.7 0.6 collective-permute-done.9.refs_1_
  37.3 1.3 %collective-permute-start.10 = (bf16[32,2048]{1,0:T(8,128)(2,1)S(1)}, bf16[32,2048]{1,0:T(8,128)(2,1)S(1)}, u32[]{:S(2)}, u32[]{:S(2)}) collective-permute-start(bf16[32,2048]{1,0:T(8,128)(2,1)S(1)} %get-tuple-element.36), channel_id=1, source_target_pairs={{0,8},{1,9},{2,10},{3,11},{4,12},{5,13},{6,14},{7,15},{8,0},{9,1},... | collective-permute-start | bytes 393224 | tf_op jit(solution)/shard_map/ppermute | solution.py:35
  38.6 7.5 %collective-permute-done.16.refs_1_ = bf16[32,2048]{1,0:T(8,128)(2,1)S(1)} collective-permute-done((bf16[32,2048]{1,0:T(8,128)(2,1)S(1)}, bf16[32,2048]{1,0:T(8,128)(2,1)S(1)}, u32[]{:S(2)}, u32[]{:S(2)}) %collective-permute-start.16) | collective-permute-done | bytes 131104 | tf_op jit(solution)/shard_map/ppermute | solution.py:35
  46.1 1.3 %collective-permute-start.17 = (bf16[32,2048]{1,0:T(8,128)(2,1)S(1)}, bf16[32,2048]{1,0:T(8,128)(2,1)S(1)}, u32[]{:S(2)}, u32[]{:S(2)}) collective-permute-start(bf16[32,2048]{1,0:T(8,128)(2,1)S(1)} %shard_map.78.refs_0_), channel_id=1, source_target_pairs={{0,4},{1,3},{2,6},{3,1},{4,0},{5,7},{6,2},{7,5},{8,12},{9,11},{10,... | collective-permute-start | bytes 393224 | tf_op jit(solution)/shard_map/ppermute | solution.py:35
  47.4 1.4 %collective-permute-done.10.refs_1_ = bf16[32,2048]{1,0:T(8,128)(2,1)S(1)} collective-permute-done((bf16[32,2048]{1,0:T(8,128)(2,1)S(1)}, bf16[32,2048]{1,0:T(8,128)(2,1)S(1)}, u32[]{:S(2)}, u32[]{:S(2)}) %collective-permute-start.10) | collective-permute-done | bytes 131104 | tf_op jit(solution)/shard_map/ppermute | solution.py:35
  48.9 1.3 %collective-permute-start.11 = (bf16[32,2048]{1,0:T(8,128)(2,1)S(1)}, bf16[32,2048]{1,0:T(8,128)(2,1)S(1)}, u32[]{:S(2)}, u32[]{:S(2)}) collective-permute-start(bf16[32,2048]{1,0:T(8,128)(2,1)S(1)} %shard_map.73.refs_0_), channel_id=1, source_target_pairs={{0,4},{1,3},{2,6},{3,1},{4,0},{5,7},{6,2},{7,5},{8,12},{9,11},{10,... | collective-permute-start | bytes 393224 | tf_op jit(solution)/shard_map/ppermute | solution.py:35
  50.3 0.1 collective-permute-start.18
  50.3 2.7 %collective-permute-done.11.refs_1_ = bf16[32,2048]{1,0:T(8,128)(2,1)S(1)} collective-permute-done((bf16[32,2048]{1,0:T(8,128)(2,1)S(1)}, bf16[32,2048]{1,0:T(8,128)(2,1)S(1)}, u32[]{:S(2)}, u32[]{:S(2)}) %collective-permute-start.11) | collective-permute-done | bytes 131104 | tf_op jit(solution)/shard_map/ppermute | solution.py:35
  53.1 0.1 collective-permute-start.12
  53.1 4.1 %collective-permute-done.18.refs_1_ = bf16[64,2048]{1,0:T(8,128)(2,1)S(1)} collective-permute-done((bf16[64,2048]{1,0:T(8,128)(2,1)S(1)}, bf16[64,2048]{1,0:T(8,128)(2,1)S(1)}, u32[]{:S(2)}, u32[]{:S(2)}) %collective-permute-start.18) | collective-permute-done | bytes 262176 | tf_op jit(solution)/shard_map/ppermute | solution.py:35
  57.3 2.7 %collective-permute-start.19 = (bf16[128,2048]{1,0:T(8,128)(2,1)S(1)}, bf16[128,2048]{1,0:T(8,128)(2,1)S(1)}, u32[]{:S(2)}, u32[]{:S(2)}) collective-permute-start(bf16[128,2048]{1,0:T(8,128)(2,1)S(1)} %shard_map.80.own_ref), channel_id=1, source_target_pairs={{0,1},{1,0},{2,3},{3,2},{4,5},{5,4},{6,7},{7,6},{8,9},{9,8},{10,11... | collective-permute-start | bytes 1572872 | tf_op jit(solution)/shard_map/ppermute | solution.py:35
  60.0 0.1 collective-permute-done.12.refs_1_
  60.1 3.1 %collective-permute-start.13 = (bf16[128,2048]{1,0:T(8,128)(2,1)S(1)}, bf16[128,2048]{1,0:T(8,128)(2,1)S(1)}, u32[]{:S(2)}, u32[]{:S(2)}) collective-permute-start(bf16[128,2048]{1,0:T(8,128)(2,1)S(1)} %shard_map.75.own_ref), channel_id=1, source_target_pairs={{0,1},{1,0},{2,3},{3,2},{4,5},{5,4},{6,7},{7,6},{8,9},{9,8},{10,11... | collective-permute-start | bytes 1572872 | tf_op jit(solution)/shard_map/ppermute | solution.py:35
  63.2 3.8 %shard_map.81.refs_0_ = bf16[2048,4096]{1,0:T(8,128)(2,1)} custom-call(bf16[2048,256]{1,0:T(8,128)(2,1)S(1)} %bitcast.17, bf16[128,2048]{1,0:T(8,128)(2,1)S(1)} %shard_map.80.own_ref, bf16[128,2048]{1,0:T(8,128)(2,1)S(1)} %collective-permute-done.19.other_ref), custom_call_target="tpu_custom_call" | custom-call | tf_op jit(solution)/shard_map/pallas_call | solution.py:131
  67.0 3.8 %shard_map.82 = bf16[2048,4096]{1,0:T(8,128)(2,1)} custom-call(bf16[2048,256]{1,0:T(8,128)(2,1)S(1)} %bitcast.18, bf16[128,2048]{1,0:T(8,128)(2,1)S(1)} %shard_map.75.own_ref, bf16[128,2048]{1,0:T(8,128)(2,1)S(1)} %collective-permute-done.13.other_ref, bf16[2048,4096]{1,0:T(8,128)(2,1)} %shard_map.81.refs_0_), custom_call_target="tpu_custom_call", output_to_operand_aliasing={{}: (3, {})} | custom-call | tf_op jit(solution)/shard_map/pallas_call | solution.py:131
  (28 shorter events, 0.4 us)
Async XLA Ops:
  0.8 7.5 %collective-permute-start.2 = (s32[3,16]{1,0:T(4,128)S(1)}, s32[3,16]{1,0:T(4,128)S(1)}, u32[]{:S(2)}, u32[]{:S(2)}) collective-permute-start(s32[3,16]{1,0:T(4,128)S(1)} %add_add_fusion.refs_0_), channel_id=1, source_target_pairs={{12,0},{11,1},{14,2},{9,3},{8,4},{15,5},{10,6},{13,7},{4,8},{3,9},... | collective-permute-start | bytes 584 | tf_op jit(solution)/shard_map/ppermute | solution.py:163
  4.9 3.4 %collective-permute-start.1 = (s32[3,16]{1,0:T(4,128)S(1)}, s32[3,16]{1,0:T(4,128)S(1)}, u32[]{:S(2)}, u32[]{:S(2)}) collective-permute-start(s32[3,16]{1,0:T(4,128)S(1)} %add_add_fusion.refs_0_), channel_id=1, source_target_pairs={{4,0},{3,1},{6,2},{1,3},{0,4},{7,5},{2,6},{5,7},{12,8},{11,9},{14,... | collective-permute-start | bytes 584 | tf_op jit(solution)/shard_map/ppermute | solution.py:163
  5.2 3.3 %collective-permute-start = (s32[3,16]{1,0:T(4,128)S(1)}, s32[3,16]{1,0:T(4,128)S(1)}, u32[]{:S(2)}, u32[]{:S(2)}) collective-permute-start(s32[3,16]{1,0:T(4,128)S(1)} %add_add_fusion.refs_0_), channel_id=1, source_target_pairs={{8,0},{9,1},{10,2},{11,3},{12,4},{13,5},{14,6},{15,7},{0,8},{1,9},... | collective-permute-start | bytes 584 | tf_op jit(solution)/shard_map/ppermute | solution.py:163
  8.6 5.9 %collective-permute-start.5 = (s32[3,64]{1,0:T(4,128)S(1)}, s32[3,64]{1,0:T(4,128)S(1)}, u32[]{:S(2)}, u32[]{:S(2)}) collective-permute-start(s32[3,64]{1,0:T(4,128)S(1)} %shard_map.65), channel_id=1, source_target_pairs={{5,0},{2,1},{7,2},{0,3},{1,4},{6,5},{3,6},{4,7},{13,8},{10,9},{15,... | collective-permute-start | bytes 2312 | tf_op jit(solution)/shard_map/ppermute | solution.py:163
  12.1 2.3 %collective-permute-start.4 = (s32[3,64]{1,0:T(4,128)S(1)}, s32[3,64]{1,0:T(4,128)S(1)}, u32[]{:S(2)}, u32[]{:S(2)}) collective-permute-start(s32[3,64]{1,0:T(4,128)S(1)} %shard_map.65), channel_id=1, source_target_pairs={{1,0},{0,1},{3,2},{2,3},{5,4},{4,5},{7,6},{6,7},{9,8},{8,9},{11,10... | collective-permute-start | bytes 2312 | tf_op jit(solution)/shard_map/ppermute | solution.py:163
  12.1 2.4 %collective-permute-start.3 = (s32[3,64]{1,0:T(4,128)S(1)}, s32[3,64]{1,0:T(4,128)S(1)}, u32[]{:S(2)}, u32[]{:S(2)}) collective-permute-start(s32[3,64]{1,0:T(4,128)S(1)} %shard_map.65), channel_id=1, source_target_pairs={{2,0},{5,1},{0,2},{7,3},{6,4},{1,5},{4,6},{3,7},{10,8},{13,9},{8,1... | collective-permute-start | bytes 2312 | tf_op jit(solution)/shard_map/ppermute | solution.py:163
  15.2 9.8 %copy-start.1 = (s32[8]{0:T(128)S(1)}, s32[8]{0:T(128)}, u32[]{:S(2)}) copy-start(s32[8]{0:T(128)} %param.11) | copy-start | bytes 100
  15.2 11.5 %copy-start = (bf16[2,8,4096]{2,1,0:T(8,128)(2,1)S(1)}, bf16[2,8,4096]{2,1,0:T(8,128)(2,1)}, u32[]{:S(2)}) copy-start(bf16[2,8,4096]{2,1,0:T(8,128)(2,1)} %param.10) | copy-start | bytes 393220
  18.7 3.4 %collective-permute-start.6 = (bf16[128,2048]{1,0:T(8,128)(2,1)S(1)}, bf16[128,2048]{1,0:T(8,128)(2,1)S(1)}, u32[]{:S(2)}, u32[]{:S(2)}) collective-permute-start(bf16[128,2048]{1,0:T(8,128)(2,1)S(1)} %get-tuple-element.26), channel_id=1, source_target_pairs={{0,1},{1,0},{2,3},{3,2},{4,5},{5,4},{6,7},{7,6},{8,9},{9,8},{10,11... | collective-permute-start | bytes 1572872 | tf_op jit(solution)/shard_map/ppermute | solution.py:35
  24.6 2.0 %collective-permute-start.7 = (bf16[128,2048]{1,0:T(8,128)(2,1)S(1)}, bf16[128,2048]{1,0:T(8,128)(2,1)S(1)}, u32[]{:S(2)}, u32[]{:S(2)}) collective-permute-start(bf16[128,2048]{1,0:T(8,128)(2,1)S(1)} %get-tuple-element.29), channel_id=1, source_target_pairs={{0,1},{1,0},{2,3},{3,2},{4,5},{5,4},{6,7},{7,6},{8,9},{9,8},{10,11... | collective-permute-start | bytes 1572872 | tf_op jit(solution)/shard_map/ppermute | solution.py:35
  25.0 5.5 %collective-permute-start.14 = (bf16[64,2048]{1,0:T(8,128)(2,1)S(1)}, bf16[64,2048]{1,0:T(8,128)(2,1)S(1)}, u32[]{:S(2)}, u32[]{:S(2)}) collective-permute-start(bf16[64,2048]{1,0:T(8,128)(2,1)S(1)} %get-tuple-element.27.refs_1_.refs_2_), channel_id=1, source_target_pairs={{0,2},{1,5},{2,0},{3,7},{4,6},{5,1},{6,4},{7,3},{8,10},{9,13},{10,... | collective-permute-start | bytes 786440 | tf_op jit(solution)/shard_map/ppermute | solution.py:35
  26.7 6.7 %collective-permute-start.8 = (bf16[64,2048]{1,0:T(8,128)(2,1)S(1)}, bf16[64,2048]{1,0:T(8,128)(2,1)S(1)}, u32[]{:S(2)}, u32[]{:S(2)}) collective-permute-start(bf16[64,2048]{1,0:T(8,128)(2,1)S(1)} %get-tuple-element.31.refs_2_), channel_id=1, source_target_pairs={{0,2},{1,5},{2,0},{3,7},{4,6},{5,1},{6,4},{7,3},{8,10},{9,13},{10,... | collective-permute-start | bytes 786440 | tf_op jit(solution)/shard_map/ppermute | solution.py:35
  30.6 4.8 %collective-permute-start.15 = (bf16[32,2048]{1,0:T(8,128)(2,1)S(1)}, bf16[32,2048]{1,0:T(8,128)(2,1)S(1)}, u32[]{:S(2)}, u32[]{:S(2)}) collective-permute-start(bf16[32,2048]{1,0:T(8,128)(2,1)S(1)} %get-tuple-element.39), channel_id=1, source_target_pairs={{0,4},{1,3},{2,6},{3,1},{4,0},{5,7},{6,2},{7,5},{8,12},{9,11},{10,... | collective-permute-start | bytes 393224 | tf_op jit(solution)/shard_map/ppermute | solution.py:35
  33.4 3.9 %collective-permute-start.9 = (bf16[32,2048]{1,0:T(8,128)(2,1)S(1)}, bf16[32,2048]{1,0:T(8,128)(2,1)S(1)}, u32[]{:S(2)}, u32[]{:S(2)}) collective-permute-start(bf16[32,2048]{1,0:T(8,128)(2,1)S(1)} %get-tuple-element.33), channel_id=1, source_target_pairs={{0,4},{1,3},{2,6},{3,1},{4,0},{5,7},{6,2},{7,5},{8,12},{9,11},{10,... | collective-permute-start | bytes 393224 | tf_op jit(solution)/shard_map/ppermute | solution.py:35
  35.4 10.6 %collective-permute-start.16 = (bf16[32,2048]{1,0:T(8,128)(2,1)S(1)}, bf16[32,2048]{1,0:T(8,128)(2,1)S(1)}, u32[]{:S(2)}, u32[]{:S(2)}) collective-permute-start(bf16[32,2048]{1,0:T(8,128)(2,1)S(1)} %get-tuple-element.42), channel_id=1, source_target_pairs={{0,8},{1,9},{2,10},{3,11},{4,12},{5,13},{6,14},{7,15},{8,0},{9,1},... | collective-permute-start | bytes 393224 | tf_op jit(solution)/shard_map/ppermute | solution.py:35
  37.3 11.5 %collective-permute-start.10 = (bf16[32,2048]{1,0:T(8,128)(2,1)S(1)}, bf16[32,2048]{1,0:T(8,128)(2,1)S(1)}, u32[]{:S(2)}, u32[]{:S(2)}) collective-permute-start(bf16[32,2048]{1,0:T(8,128)(2,1)S(1)} %get-tuple-element.36), channel_id=1, source_target_pairs={{0,8},{1,9},{2,10},{3,11},{4,12},{5,13},{6,14},{7,15},{8,0},{9,1},... | collective-permute-start | bytes 393224 | tf_op jit(solution)/shard_map/ppermute | solution.py:35
  46.1 4.2 %collective-permute-start.17 = (bf16[32,2048]{1,0:T(8,128)(2,1)S(1)}, bf16[32,2048]{1,0:T(8,128)(2,1)S(1)}, u32[]{:S(2)}, u32[]{:S(2)}) collective-permute-start(bf16[32,2048]{1,0:T(8,128)(2,1)S(1)} %shard_map.78.refs_0_), channel_id=1, source_target_pairs={{0,4},{1,3},{2,6},{3,1},{4,0},{5,7},{6,2},{7,5},{8,12},{9,11},{10,... | collective-permute-start | bytes 393224 | tf_op jit(solution)/shard_map/ppermute | solution.py:35
  48.9 4.2 %collective-permute-start.11 = (bf16[32,2048]{1,0:T(8,128)(2,1)S(1)}, bf16[32,2048]{1,0:T(8,128)(2,1)S(1)}, u32[]{:S(2)}, u32[]{:S(2)}) collective-permute-start(bf16[32,2048]{1,0:T(8,128)(2,1)S(1)} %shard_map.73.refs_0_), channel_id=1, source_target_pairs={{0,4},{1,3},{2,6},{3,1},{4,0},{5,7},{6,2},{7,5},{8,12},{9,11},{10,... | collective-permute-start | bytes 393224 | tf_op jit(solution)/shard_map/ppermute | solution.py:35
  50.3 7.0 %collective-permute-start.18 = (bf16[64,2048]{1,0:T(8,128)(2,1)S(1)}, bf16[64,2048]{1,0:T(8,128)(2,1)S(1)}, u32[]{:S(2)}, u32[]{:S(2)}) collective-permute-start(bf16[64,2048]{1,0:T(8,128)(2,1)S(1)} %shard_map.79.refs_0_), channel_id=1, source_target_pairs={{0,2},{1,5},{2,0},{3,7},{4,6},{5,1},{6,4},{7,3},{8,10},{9,13},{10,... | collective-permute-start | bytes 786440 | tf_op jit(solution)/shard_map/ppermute | solution.py:35
  53.1 7.0 %collective-permute-start.12 = (bf16[64,2048]{1,0:T(8,128)(2,1)S(1)}, bf16[64,2048]{1,0:T(8,128)(2,1)S(1)}, u32[]{:S(2)}, u32[]{:S(2)}) collective-permute-start(bf16[64,2048]{1,0:T(8,128)(2,1)S(1)} %shard_map.74.refs_0_), channel_id=1, source_target_pairs={{0,2},{1,5},{2,0},{3,7},{4,6},{5,1},{6,4},{7,3},{8,10},{9,13},{10,... | collective-permute-start | bytes 786440 | tf_op jit(solution)/shard_map/ppermute | solution.py:35
  57.3 5.9 %collective-permute-start.19 = (bf16[128,2048]{1,0:T(8,128)(2,1)S(1)}, bf16[128,2048]{1,0:T(8,128)(2,1)S(1)}, u32[]{:S(2)}, u32[]{:S(2)}) collective-permute-start(bf16[128,2048]{1,0:T(8,128)(2,1)S(1)} %shard_map.80.own_ref), channel_id=1, source_target_pairs={{0,1},{1,0},{2,3},{3,2},{4,5},{5,4},{6,7},{7,6},{8,9},{9,8},{10,11... | collective-permute-start | bytes 1572872 | tf_op jit(solution)/shard_map/ppermute | solution.py:35
  60.1 6.9 %collective-permute-start.13 = (bf16[128,2048]{1,0:T(8,128)(2,1)S(1)}, bf16[128,2048]{1,0:T(8,128)(2,1)S(1)}, u32[]{:S(2)}, u32[]{:S(2)}) collective-permute-start(bf16[128,2048]{1,0:T(8,128)(2,1)S(1)} %shard_map.75.own_ref), channel_id=1, source_target_pairs={{0,1},{1,0},{2,3},{3,2},{4,5},{5,4},{6,7},{7,6},{8,9},{9,8},{10,11... | collective-permute-start | bytes 1572872 | tf_op jit(solution)/shard_map/ppermute | solution.py:35

commit v4 on v3

--- a/solution.py
+++ b/solution.py
@@ -54,47 +54,42 @@
     )(pltpu.with_memory_space_constraint(s_flat, pltpu.HBM))
 
 
-def forward_kernel(count, next_column, waits, at_ref, *refs):
+def forward_kernel(count, waits, first, fetch, at_ref, *refs):
     pieces, refs = refs[:count], refs[count + waits :]
     copy = None
-    if next_column is None:
-        keep_ref, send_ref = refs
+    if fetch is None:
+        (out_ref,) = refs
     else:
-        s_ref, keep_ref, send_ref, next_ref, sem = refs
-        columns = next_ref.shape[1]
-        copy = pltpu.make_async_copy(s_ref.at[:, next_column : next_column + columns], next_ref, sem)
+        s_ref, out_ref, next_ref, sem = refs
+        copy = pltpu.make_async_copy(s_ref.at[fetch], next_ref, sem)
         copy.start()
-    a = at_ref[...].T
-    half, width = keep_ref.shape
+    rows, width = out_ref.shape
+    a = at_ref[:, first : first + rows].T
     for start in range(0, width, FWD_COLUMNS):
         stop = start + FWD_COLUMNS
         wave, done = 0.0, 0
         for piece in pieces:
-            rows = piece.shape[0]
+            depth = piece.shape[0]
             wave += jnp.dot(
-                a[:, done : done + rows], piece[:, start:stop], preferred_element_type=jnp.float32
+                a[:, done : done + depth], piece[:, start:stop], preferred_element_type=jnp.float32
             )
-            done += rows
-        keep_ref[:, start:stop] = wave[:half]
-        send_ref[:, start:stop] = wave[half:].astype(jnp.bfloat16)
+            done += depth
+        out_ref[:, start:stop] = wave.astype(out_ref.dtype)
     if copy is not None:
         copy.wait()
 
 
-def forward(at, pieces, s_flat, next_column, after):
-    depth, rows = at.shape
-    half, width = rows // 2, pieces[0].shape[1]
+def forward(at, pieces, first, dtype, s_flat, fetch, after):
+    depth, rows = at.shape[0], at.shape[1] // 2
+    width = pieces[0].shape[1]
     whole = pl.BlockSpec(memory_space=pltpu.VMEM)
-    more = next_column is not None
+    more = fetch is not None
+    block = [pltpu.VMEM(tuple(part.stop - part.start for part in fetch), s_flat.dtype)] if more else []
     return pl.pallas_call(
-        functools.partial(forward_kernel, len(pieces), next_column, len(after)),
+        functools.partial(forward_kernel, len(pieces), len(after), first, fetch),
         in_specs=[whole] * (1 + len(pieces)) + [pl.BlockSpec(memory_space=pl.ANY)] * (len(after) + more),
-        out_specs=[whole] * (2 + more),
-        out_shape=[
-            jax.ShapeDtypeStruct((half, width), jnp.float32),
-            jax.ShapeDtypeStruct((half, width), jnp.bfloat16),
-        ]
-        + [pltpu.VMEM((depth, width), s_flat.dtype)] * more,
+        out_specs=[whole] * (1 + more),
+        out_shape=[jax.ShapeDtypeStruct((rows, width), dtype)] + block,
         scratch_shapes=[pltpu.SemaphoreType.DMA] * more,
         compiler_params=pltpu.CompilerParams(vmem_limit_bytes=30 << 20),
         cost_estimate=pl.CostEstimate(
@@ -297,11 +292,15 @@
     scale = jnp.exp2(target_exp.astype(jnp.float32))[None, :, None]
     scaled = (target.astype(jnp.float32) * scale).astype(jnp.bfloat16).reshape(block, pixels)
     scaled = lax.optimization_barrier([scaled[:, c * width : (c + 1) * width] for c in range(CHUNKS)])
-    states, after = [], []
+    states, after, total = [], [], s_flat.shape[0]
     for chunk in range(CHUNKS):
-        next_column = (chunk + 1) * width if chunk < CHUNKS - 1 else None
-        keep, send, *pieces = forward(at, pieces, s_flat, next_column, after)
-        states.append(halved(keep, swap(send, count, -1), after))
+        columns = slice((chunk + 1) * width, (chunk + 2) * width)
+        fetch = [(slice(row, row + total // 2), columns) for row in (0, total // 2)]
+        fetch = fetch if chunk < CHUNKS - 1 else [None, None]
+        send, *one = forward(at, pieces, rows // 2, jnp.bfloat16, s_flat, fetch[0], after)
+        keep, *two = forward(at, pieces, 0, jnp.float32, s_flat, fetch[1], [send])
+        pieces = one + two
+        states.append(halved(keep, swap(send, count, -1), []))
         after = [states[-1][1]]
     for stage in range(stages - 1):
         for chunk in range(CHUNKS):

time: 71.1 us -> 69.5 us (0.977)
  waiting for transfers between devices: 25.9 us -> 22.9 us
  Pallas kernels: 18.4 us -> 19.6 us
    ppermute x14, waiting for transfers between devices: 25.6 us -> 22.6 us  [swap(): return lax.ppermute(x, 'beam', pairs)]
    pallas_call x2 -> x4, Pallas kernels: 5.81 us -> 7.04 us  [forward(): pl.pallas_call(functools.partial(forward_kernel, len(pieces), len(after),...]
  transfers between devices with their start and end apart: 20 -> 20, of which waited for: 13 -> 12; matrix products, arithmetic and copies ran while one was open for 1% -> 1% of each run, Pallas kernels for 12% -> 18%
where the time goes in v4:
time: 69.5 us; the launch traced here: 69.2 us
  starting transfers between devices  24.1 us (35%)
  waiting for transfers between devices  22.9 us (33%)
  Pallas kernels  19.6 us (28%)
  other arithmetic  1.54 us (2%)
  local copies, waits for them, and re-layouts  0.78 us (1%)
    ppermute x14, waiting for transfers between devices, swap(): return lax.ppermute(x, 'beam', pairs)  22.6 us
    ppermute x14, starting transfers between devices, swap(): return lax.ppermute(x, 'beam', pairs)  16 us
    ppermute x6, starting transfers between devices, fetch(): return lax.ppermute(x, 'beam', [(source_of(i), i) for i in range(count)])  8.15 us
    pallas_call x2, Pallas kernels, backward(): pl.pallas_call(functools.partial(backward_kernel, chunk * width), in_spec...  7.62 us
    pallas_call x4, Pallas kernels, forward(): pl.pallas_call(functools.partial(forward_kernel, len(pieces), len(after),...  7.04 us
    pallas_call x2, Pallas kernels, staged(): pl.pallas_call(functools.partial(stage_kernel, first_row), in_specs=[pl.B...  4.39 us
  transfers between devices with their start and end apart: 20, of which 12 were waited for; matrix products, arithmetic and copies ran while one was open for 1% of the time, Pallas kernels for 18%

profile of v4, /device:TPU:1, one launch (start us, length us, event | category | flops | bytes accessed | tf_op | source)
XLA Modules:
  0.0 69.2 jit_solution(4986052502479724384)
XLA Ops:
  0.0 0.8 %add_add_fusion.refs_0_ = s32[3,16]{1,0:T(4,128)S(1)} fusion(s32[1,8]{1,0:T(1,128)} %bitcast.30, s32[2,8]{1,0:T(2,128)} %bitcast.29), kind=kLoop, calls=%fused_computation.24 | loop fusion | flops 144 | bytes 288 | tf_op jit(solution)/shard_map/concatenate | solution.py:281
  0.8 4.1 %collective-permute-start.2 = (s32[3,16]{1,0:T(4,128)S(1)}, s32[3,16]{1,0:T(4,128)S(1)}, u32[]{:S(2)}, u32[]{:S(2)}) collective-permute-start(s32[3,16]{1,0:T(4,128)S(1)} %add_add_fusion.refs_0_), channel_id=1, source_target_pairs={{12,0},{11,1},{14,2},{9,3},{8,4},{15,5},{10,6},{13,7},{4,8},{3,9},... | collective-permute-start | bytes 584 | tf_op jit(solution)/shard_map/ppermute | solution.py:158
  4.9 0.2 collective-permute-start.1
  5.2 0.1 collective-permute-start
  5.3 0.8 %slice_bitcast_fusion = (f32[64]{0:T(128)S(1)}, f32[64]{0:T(128)S(1)}) fusion(f32[2,64]{1,0:T(2,128)} %param.7), kind=kLoop, calls=%fused_computation.45 | loop fusion | bytes 1024 | tf_op jit(solution)/shard_map/slice | solution.py:261
  6.1 2.2 %shard_map.64.refs_4_.refs_0_ = bf16[1024,2048]{1,0:T(8,128)(2,1)S(1)} custom-call(bf16[2048,4096]{1,0:T(8,128)(2,1)} %bitcast.21), custom_call_target="tpu_custom_call" | custom-call | bytes 4194304 | tf_op jit(solution)/shard_map/pallas_call | solution.py:46
  8.3 0.2 collective-permute-done.refs_1_
  8.5 0.1 shard_map.65
  8.6 3.6 %collective-permute-start.5 = (s32[3,64]{1,0:T(4,128)S(1)}, s32[3,64]{1,0:T(4,128)S(1)}, u32[]{:S(2)}, u32[]{:S(2)}) collective-permute-start(s32[3,64]{1,0:T(4,128)S(1)} %shard_map.65), channel_id=1, source_target_pairs={{5,0},{2,1},{7,2},{0,3},{1,4},{6,5},{3,6},{4,7},{13,8},{10,9},{15,... | collective-permute-start | bytes 2312 | tf_op jit(solution)/shard_map/ppermute | solution.py:158
  12.1 0.1 collective-permute-start.3
  12.3 2.2 %shard_map.66.refs_1_ = bf16[1024,2048]{1,0:T(8,128)(2,1)S(1)} custom-call(bf16[2048,4096]{1,0:T(8,128)(2,1)} %bitcast.22), custom_call_target="tpu_custom_call" | custom-call | bytes 4194304 | tf_op jit(solution)/shard_map/pallas_call | solution.py:46
  14.5 0.1 collective-permute-done.3
  14.6 0.1 fusion.12
  14.7 0.4 broadcast_select_fusion.1
  15.1 0.1 broadcast_select_fusion
  15.2 2.2 %shard_map.67 = (bf16[128,2048]{1,0:T(8,128)(2,1)S(1)}, bf16[1024,2048]{1,0:T(8,128)(2,1)S(1)}) custom-call(bf16[2048,256]{1,0:T(8,128)(2,1)S(1)} %bitcast.15, bf16[1024,2048]{1,0:T(8,128)(2,1)S(1)} %shard_map.64.refs_4_.refs_0_, bf16[1024,2048]{1,0:T(8,128)(2,1)S(1)} %shard_map.66.refs_1_, bf16[2048,4096]{1,0:T(8,128)(2,1)} %bitcast.23), custom_call_target="tpu_custom_call" | custom-call | flops 1073741824 | bytes 8388608 | tf_op jit(solution)/shard_map/pallas_call | solution.py:88
  17.4 1.9 %collective-permute-start.6 = (bf16[128,2048]{1,0:T(8,128)(2,1)S(1)}, bf16[128,2048]{1,0:T(8,128)(2,1)S(1)}, u32[]{:S(2)}, u32[]{:S(2)}) collective-permute-start(bf16[128,2048]{1,0:T(8,128)(2,1)S(1)} %get-tuple-element.24.refs_2_), channel_id=1, source_target_pairs={{0,1},{1,0},{2,3},{3,2},{4,5},{5,4},{6,7},{7,6},{8,9},{9,8},{10,11... | collective-permute-start | bytes 1572872 | tf_op jit(solution)/shard_map/ppermute | solution.py:35
  19.3 2.2 %shard_map.68 = (f32[128,2048]{1,0:T(8,128)S(1)}, bf16[1024,2048]{1,0:T(8,128)(2,1)S(1)}) custom-call(bf16[2048,256]{1,0:T(8,128)(2,1)S(1)} %bitcast.16, bf16[1024,2048]{1,0:T(8,128)(2,1)S(1)} %shard_map.64.refs_4_.refs_0_, bf16[1024,2048]{1,0:T(8,128)(2,1)S(1)} %shard_map.66.refs_1_, bf16[128,2048]{1,0:T(8,128)(2,1)S(1)} %get-tuple-element.24.refs_2_, ...), custom_call_target="tpu_custom_call" | custom-call | flops 1073741824 | bytes 8388608 | tf_op jit(solution)/shard_map/pallas_call | solution.py:88
  21.6 0.1 shard_map.69
  21.7 1.3 %shard_map.70.refs_2_ = bf16[128,2048]{1,0:T(8,128)(2,1)S(1)} custom-call(bf16[2048,256]{1,0:T(8,128)(2,1)S(1)} %bitcast.17, bf16[1024,2048]{1,0:T(8,128)(2,1)S(1)} %get-tuple-element.23.refs_0_, bf16[1024,2048]{1,0:T(8,128)(2,1)S(1)} %get-tuple-element.25.refs_1_, bf16[64,2048]{1,0:T(8,128)(2,1)S(1)} %get-tuple-element.27.refs_2_), custom_call_target="tpu_custom_call" | custom-call | flops 1073741824 | bytes 8388608 | tf_op jit(solution)/shard_map/pallas_call | solution.py:88
  23.0 0.1 collective-permute-start.7
  23.1 0.1 collective-permute-start.14
  23.2 1.3 %shard_map.71.refs_0_ = f32[128,2048]{1,0:T(8,128)S(1)} custom-call(bf16[2048,256]{1,0:T(8,128)(2,1)S(1)} %bitcast.18, bf16[1024,2048]{1,0:T(8,128)(2,1)S(1)} %get-tuple-element.23.refs_0_, bf16[1024,2048]{1,0:T(8,128)(2,1)S(1)} %get-tuple-element.25.refs_1_, bf16[128,2048]{1,0:T(8,128)(2,1)S(1)} %shard_map.70.refs_2_), custom_call_target="tpu_custom_call" | custom-call | flops 1073741824 | bytes 8388608 | tf_op jit(solution)/shard_map/pallas_call | solution.py:88
  24.5 0.5 collective-permute-done.7.refs_1_
  25.0 0.1 shard_map.72
  25.1 1.0 %collective-permute-start.8 = (bf16[64,2048]{1,0:T(8,128)(2,1)S(1)}, bf16[64,2048]{1,0:T(8,128)(2,1)S(1)}, u32[]{:S(2)}, u32[]{:S(2)}) collective-permute-start(bf16[64,2048]{1,0:T(8,128)(2,1)S(1)} %get-tuple-element.29.refs_2_), channel_id=1, source_target_pairs={{0,2},{1,5},{2,0},{3,7},{4,6},{5,1},{6,4},{7,3},{8,10},{9,13},{10,... | collective-permute-start | bytes 786440 | tf_op jit(solution)/shard_map/ppermute | solution.py:35
  26.1 0.1 fusion
  26.2 2.5 %collective-permute-done.14.refs_1_ = bf16[64,2048]{1,0:T(8,128)(2,1)S(1)} collective-permute-done((bf16[64,2048]{1,0:T(8,128)(2,1)S(1)}, bf16[64,2048]{1,0:T(8,128)(2,1)S(1)}, u32[]{:S(2)}, u32[]{:S(2)}) %collective-permute-start.14) | collective-permute-done | bytes 262176 | tf_op jit(solution)/shard_map/ppermute | solution.py:35
  28.7 1.1 %collective-permute-start.15 = (bf16[32,2048]{1,0:T(8,128)(2,1)S(1)}, bf16[32,2048]{1,0:T(8,128)(2,1)S(1)}, u32[]{:S(2)}, u32[]{:S(2)}) collective-permute-start(bf16[32,2048]{1,0:T(8,128)(2,1)S(1)} %get-tuple-element.37), channel_id=1, source_target_pairs={{0,4},{1,3},{2,6},{3,1},{4,0},{5,7},{6,2},{7,5},{8,12},{9,11},{10,... | collective-permute-start | bytes 393224 | tf_op jit(solution)/shard_map/ppermute | solution.py:35
  29.9 1.6 %collective-permute-done.8.refs_1_ = bf16[64,2048]{1,0:T(8,128)(2,1)S(1)} collective-permute-done((bf16[64,2048]{1,0:T(8,128)(2,1)S(1)}, bf16[64,2048]{1,0:T(8,128)(2,1)S(1)}, u32[]{:S(2)}, u32[]{:S(2)}) %collective-permute-start.8) | collective-permute-done | bytes 262176 | tf_op jit(solution)/shard_map/ppermute | solution.py:35
  31.5 1.1 %collective-permute-start.9 = (bf16[32,2048]{1,0:T(8,128)(2,1)S(1)}, bf16[32,2048]{1,0:T(8,128)(2,1)S(1)}, u32[]{:S(2)}, u32[]{:S(2)}) collective-permute-start(bf16[32,2048]{1,0:T(8,128)(2,1)S(1)} %get-tuple-element.31), channel_id=1, source_target_pairs={{0,4},{1,3},{2,6},{3,1},{4,0},{5,7},{6,2},{7,5},{8,12},{9,11},{10,... | collective-permute-start | bytes 393224 | tf_op jit(solution)/shard_map/ppermute | solution.py:35
  32.7 1.2 %collective-permute-done.15.refs_1_ = bf16[32,2048]{1,0:T(8,128)(2,1)S(1)} collective-permute-done((bf16[32,2048]{1,0:T(8,128)(2,1)S(1)}, bf16[32,2048]{1,0:T(8,128)(2,1)S(1)}, u32[]{:S(2)}, u32[]{:S(2)}) %collective-permute-start.15) | collective-permute-done | bytes 131104 | tf_op jit(solution)/shard_map/ppermute | solution.py:35
  33.9 1.3 %collective-permute-start.16 = (bf16[32,2048]{1,0:T(8,128)(2,1)S(1)}, bf16[32,2048]{1,0:T(8,128)(2,1)S(1)}, u32[]{:S(2)}, u32[]{:S(2)}) collective-permute-start(bf16[32,2048]{1,0:T(8,128)(2,1)S(1)} %get-tuple-element.40), channel_id=1, source_target_pairs={{0,8},{1,9},{2,10},{3,11},{4,12},{5,13},{6,14},{7,15},{8,0},{9,1},... | collective-permute-start | bytes 393224 | tf_op jit(solution)/shard_map/ppermute | solution.py:35
  35.1 0.3 collective-permute-done.9.refs_1_
  35.5 1.3 %collective-permute-start.10 = (bf16[32,2048]{1,0:T(8,128)(2,1)S(1)}, bf16[32,2048]{1,0:T(8,128)(2,1)S(1)}, u32[]{:S(2)}, u32[]{:S(2)}) collective-permute-start(bf16[32,2048]{1,0:T(8,128)(2,1)S(1)} %get-tuple-element.34), channel_id=1, source_target_pairs={{0,8},{1,9},{2,10},{3,11},{4,12},{5,13},{6,14},{7,15},{8,0},{9,1},... | collective-permute-start | bytes 393224 | tf_op jit(solution)/shard_map/ppermute | solution.py:35
  36.7 7.9 %collective-permute-done.16.refs_1_ = bf16[32,2048]{1,0:T(8,128)(2,1)S(1)} collective-permute-done((bf16[32,2048]{1,0:T(8,128)(2,1)S(1)}, bf16[32,2048]{1,0:T(8,128)(2,1)S(1)}, u32[]{:S(2)}, u32[]{:S(2)}) %collective-permute-start.16) | collective-permute-done | bytes 131104 | tf_op jit(solution)/shard_map/ppermute | solution.py:35
  44.6 1.1 %collective-permute-start.17 = (bf16[32,2048]{1,0:T(8,128)(2,1)S(1)}, bf16[32,2048]{1,0:T(8,128)(2,1)S(1)}, u32[]{:S(2)}, u32[]{:S(2)}) collective-permute-start(bf16[32,2048]{1,0:T(8,128)(2,1)S(1)} %shard_map.80.refs_0_), channel_id=1, source_target_pairs={{0,4},{1,3},{2,6},{3,1},{4,0},{5,7},{6,2},{7,5},{8,12},{9,11},{10,... | collective-permute-start | bytes 393224 | tf_op jit(solution)/shard_map/ppermute | solution.py:35
  45.8 1.7 %collective-permute-done.10.refs_1_ = bf16[32,2048]{1,0:T(8,128)(2,1)S(1)} collective-permute-done((bf16[32,2048]{1,0:T(8,128)(2,1)S(1)}, bf16[32,2048]{1,0:T(8,128)(2,1)S(1)}, u32[]{:S(2)}, u32[]{:S(2)}) %collective-permute-start.10) | collective-permute-done | bytes 131104 | tf_op jit(solution)/shard_map/ppermute | solution.py:35
  47.5 1.1 %collective-permute-start.11 = (bf16[32,2048]{1,0:T(8,128)(2,1)S(1)}, bf16[32,2048]{1,0:T(8,128)(2,1)S(1)}, u32[]{:S(2)}, u32[]{:S(2)}) collective-permute-start(bf16[32,2048]{1,0:T(8,128)(2,1)S(1)} %shard_map.75.refs_0_), channel_id=1, source_target_pairs={{0,4},{1,3},{2,6},{3,1},{4,0},{5,7},{6,2},{7,5},{8,12},{9,11},{10,... | collective-permute-start | bytes 393224 | tf_op jit(solution)/shard_map/ppermute | solution.py:35
  48.6 0.1 collective-permute-start.18
  48.7 2.7 %collective-permute-done.11.refs_1_ = bf16[32,2048]{1,0:T(8,128)(2,1)S(1)} collective-permute-done((bf16[32,2048]{1,0:T(8,128)(2,1)S(1)}, bf16[32,2048]{1,0:T(8,128)(2,1)S(1)}, u32[]{:S(2)}, u32[]{:S(2)}) %collective-permute-start.11) | collective-permute-done | bytes 131104 | tf_op jit(solution)/shard_map/ppermute | solution.py:35
  51.4 0.1 collective-permute-start.12
  51.4 4.2 %collective-permute-done.18.refs_1_ = bf16[64,2048]{1,0:T(8,128)(2,1)S(1)} collective-permute-done((bf16[64,2048]{1,0:T(8,128)(2,1)S(1)}, bf16[64,2048]{1,0:T(8,128)(2,1)S(1)}, u32[]{:S(2)}, u32[]{:S(2)}) %collective-permute-start.18) | collective-permute-done | bytes 262176 | tf_op jit(solution)/shard_map/ppermute | solution.py:35
  55.6 2.6 %collective-permute-start.19 = (bf16[128,2048]{1,0:T(8,128)(2,1)S(1)}, bf16[128,2048]{1,0:T(8,128)(2,1)S(1)}, u32[]{:S(2)}, u32[]{:S(2)}) collective-permute-start(bf16[128,2048]{1,0:T(8,128)(2,1)S(1)} %shard_map.82.own_ref), channel_id=1, source_target_pairs={{0,1},{1,0},{2,3},{3,2},{4,5},{5,4},{6,7},{7,6},{8,9},{9,8},{10,11... | collective-permute-start | bytes 1572872 | tf_op jit(solution)/shard_map/ppermute | solution.py:35
  58.2 0.2 collective-permute-done.12.refs_1_
  58.4 3.1 %collective-permute-start.13 = (bf16[128,2048]{1,0:T(8,128)(2,1)S(1)}, bf16[128,2048]{1,0:T(8,128)(2,1)S(1)}, u32[]{:S(2)}, u32[]{:S(2)}) collective-permute-start(bf16[128,2048]{1,0:T(8,128)(2,1)S(1)} %shard_map.77.own_ref), channel_id=1, source_target_pairs={{0,1},{1,0},{2,3},{3,2},{4,5},{5,4},{6,7},{7,6},{8,9},{9,8},{10,11... | collective-permute-start | bytes 1572872 | tf_op jit(solution)/shard_map/ppermute | solution.py:35
  61.6 3.8 %shard_map.83.refs_0_ = bf16[2048,4096]{1,0:T(8,128)(2,1)} custom-call(bf16[2048,256]{1,0:T(8,128)(2,1)S(1)} %bitcast.19, bf16[128,2048]{1,0:T(8,128)(2,1)S(1)} %shard_map.82.own_ref, bf16[128,2048]{1,0:T(8,128)(2,1)S(1)} %collective-permute-done.19.other_ref), custom_call_target="tpu_custom_call" | custom-call | tf_op jit(solution)/shard_map/pallas_call | solution.py:126
  65.4 3.8 %shard_map.84 = bf16[2048,4096]{1,0:T(8,128)(2,1)} custom-call(bf16[2048,256]{1,0:T(8,128)(2,1)S(1)} %bitcast.20, bf16[128,2048]{1,0:T(8,128)(2,1)S(1)} %shard_map.77.own_ref, bf16[128,2048]{1,0:T(8,128)(2,1)S(1)} %collective-permute-done.13.other_ref, bf16[2048,4096]{1,0:T(8,128)(2,1)} %shard_map.83.refs_0_), custom_call_target="tpu_custom_call", output_to_operand_aliasing={{}: (3, {})} | custom-call | tf_op jit(solution)/shard_map/pallas_call | solution.py:126
  (30 shorter events, 0.4 us)
Async XLA Ops:
  0.8 7.5 %collective-permute-start.2 = (s32[3,16]{1,0:T(4,128)S(1)}, s32[3,16]{1,0:T(4,128)S(1)}, u32[]{:S(2)}, u32[]{:S(2)}) collective-permute-start(s32[3,16]{1,0:T(4,128)S(1)} %add_add_fusion.refs_0_), channel_id=1, source_target_pairs={{12,0},{11,1},{14,2},{9,3},{8,4},{15,5},{10,6},{13,7},{4,8},{3,9},... | collective-permute-start | bytes 584 | tf_op jit(solution)/shard_map/ppermute | solution.py:158
  4.9 3.4 %collective-permute-start.1 = (s32[3,16]{1,0:T(4,128)S(1)}, s32[3,16]{1,0:T(4,128)S(1)}, u32[]{:S(2)}, u32[]{:S(2)}) collective-permute-start(s32[3,16]{1,0:T(4,128)S(1)} %add_add_fusion.refs_0_), channel_id=1, source_target_pairs={{4,0},{3,1},{6,2},{1,3},{0,4},{7,5},{2,6},{5,7},{12,8},{11,9},{14,... | collective-permute-start | bytes 584 | tf_op jit(solution)/shard_map/ppermute | solution.py:158
  5.2 3.3 %collective-permute-start = (s32[3,16]{1,0:T(4,128)S(1)}, s32[3,16]{1,0:T(4,128)S(1)}, u32[]{:S(2)}, u32[]{:S(2)}) collective-permute-start(s32[3,16]{1,0:T(4,128)S(1)} %add_add_fusion.refs_0_), channel_id=1, source_target_pairs={{8,0},{9,1},{10,2},{11,3},{12,4},{13,5},{14,6},{15,7},{0,8},{1,9},... | collective-permute-start | bytes 584 | tf_op jit(solution)/shard_map/ppermute | solution.py:158
  8.6 5.9 %collective-permute-start.5 = (s32[3,64]{1,0:T(4,128)S(1)}, s32[3,64]{1,0:T(4,128)S(1)}, u32[]{:S(2)}, u32[]{:S(2)}) collective-permute-start(s32[3,64]{1,0:T(4,128)S(1)} %shard_map.65), channel_id=1, source_target_pairs={{5,0},{2,1},{7,2},{0,3},{1,4},{6,5},{3,6},{4,7},{13,8},{10,9},{15,... | collective-permute-start | bytes 2312 | tf_op jit(solution)/shard_map/ppermute | solution.py:158
  12.1 2.3 %collective-permute-start.4 = (s32[3,64]{1,0:T(4,128)S(1)}, s32[3,64]{1,0:T(4,128)S(1)}, u32[]{:S(2)}, u32[]{:S(2)}) collective-permute-start(s32[3,64]{1,0:T(4,128)S(1)} %shard_map.65), channel_id=1, source_target_pairs={{1,0},{0,1},{3,2},{2,3},{5,4},{4,5},{7,6},{6,7},{9,8},{8,9},{11,10... | collective-permute-start | bytes 2312 | tf_op jit(solution)/shard_map/ppermute | solution.py:158
  12.1 2.4 %collective-permute-start.3 = (s32[3,64]{1,0:T(4,128)S(1)}, s32[3,64]{1,0:T(4,128)S(1)}, u32[]{:S(2)}, u32[]{:S(2)}) collective-permute-start(s32[3,64]{1,0:T(4,128)S(1)} %shard_map.65), channel_id=1, source_target_pairs={{2,0},{5,1},{0,2},{7,3},{6,4},{1,5},{4,6},{3,7},{10,8},{13,9},{8,1... | collective-permute-start | bytes 2312 | tf_op jit(solution)/shard_map/ppermute | solution.py:158
  17.4 4.2 %collective-permute-start.6 = (bf16[128,2048]{1,0:T(8,128)(2,1)S(1)}, bf16[128,2048]{1,0:T(8,128)(2,1)S(1)}, u32[]{:S(2)}, u32[]{:S(2)}) collective-permute-start(bf16[128,2048]{1,0:T(8,128)(2,1)S(1)} %get-tuple-element.24.refs_2_), channel_id=1, source_target_pairs={{0,1},{1,0},{2,3},{3,2},{4,5},{5,4},{6,7},{7,6},{8,9},{9,8},{10,11... | collective-permute-start | bytes 1572872 | tf_op jit(solution)/shard_map/ppermute | solution.py:35
  21.7 1.4 %copy-start.1 = (s32[8]{0:T(128)S(1)}, s32[8]{0:T(128)}, u32[]{:S(2)}) copy-start(s32[8]{0:T(128)} %param.11) | copy-start | bytes 100
  23.0 2.0 %collective-permute-start.7 = (bf16[128,2048]{1,0:T(8,128)(2,1)S(1)}, bf16[128,2048]{1,0:T(8,128)(2,1)S(1)}, u32[]{:S(2)}, u32[]{:S(2)}) collective-permute-start(bf16[128,2048]{1,0:T(8,128)(2,1)S(1)} %shard_map.70.refs_2_), channel_id=1, source_target_pairs={{0,1},{1,0},{2,3},{3,2},{4,5},{5,4},{6,7},{7,6},{8,9},{9,8},{10,11... | collective-permute-start | bytes 1572872 | tf_op jit(solution)/shard_map/ppermute | solution.py:35
  23.1 3.0 %copy-start = (bf16[2,8,4096]{2,1,0:T(8,128)(2,1)S(1)}, bf16[2,8,4096]{2,1,0:T(8,128)(2,1)}, u32[]{:S(2)}) copy-start(bf16[2,8,4096]{2,1,0:T(8,128)(2,1)} %param.10) | copy-start | bytes 393220
  23.1 5.6 %collective-permute-start.14 = (bf16[64,2048]{1,0:T(8,128)(2,1)S(1)}, bf16[64,2048]{1,0:T(8,128)(2,1)S(1)}, u32[]{:S(2)}, u32[]{:S(2)}) collective-permute-start(bf16[64,2048]{1,0:T(8,128)(2,1)S(1)} %get-tuple-element.27.refs_2_), channel_id=1, source_target_pairs={{0,2},{1,5},{2,0},{3,7},{4,6},{5,1},{6,4},{7,3},{8,10},{9,13},{10,... | collective-permute-start | bytes 786440 | tf_op jit(solution)/shard_map/ppermute | solution.py:35
  25.1 6.4 %collective-permute-start.8 = (bf16[64,2048]{1,0:T(8,128)(2,1)S(1)}, bf16[64,2048]{1,0:T(8,128)(2,1)S(1)}, u32[]{:S(2)}, u32[]{:S(2)}) collective-permute-start(bf16[64,2048]{1,0:T(8,128)(2,1)S(1)} %get-tuple-element.29.refs_2_), channel_id=1, source_target_pairs={{0,2},{1,5},{2,0},{3,7},{4,6},{5,1},{6,4},{7,3},{8,10},{9,13},{10,... | collective-permute-start | bytes 786440 | tf_op jit(solution)/shard_map/ppermute | solution.py:35
  28.7 5.1 %collective-permute-start.15 = (bf16[32,2048]{1,0:T(8,128)(2,1)S(1)}, bf16[32,2048]{1,0:T(8,128)(2,1)S(1)}, u32[]{:S(2)}, u32[]{:S(2)}) collective-permute-start(bf16[32,2048]{1,0:T(8,128)(2,1)S(1)} %get-tuple-element.37), channel_id=1, source_target_pairs={{0,4},{1,3},{2,6},{3,1},{4,0},{5,7},{6,2},{7,5},{8,12},{9,11},{10,... | collective-permute-start | bytes 393224 | tf_op jit(solution)/shard_map/ppermute | solution.py:35
  31.5 3.9 %collective-permute-start.9 = (bf16[32,2048]{1,0:T(8,128)(2,1)S(1)}, bf16[32,2048]{1,0:T(8,128)(2,1)S(1)}, u32[]{:S(2)}, u32[]{:S(2)}) collective-permute-start(bf16[32,2048]{1,0:T(8,128)(2,1)S(1)} %get-tuple-element.31), channel_id=1, source_target_pairs={{0,4},{1,3},{2,6},{3,1},{4,0},{5,7},{6,2},{7,5},{8,12},{9,11},{10,... | collective-permute-start | bytes 393224 | tf_op jit(solution)/shard_map/ppermute | solution.py:35
  33.9 10.7 %collective-permute-start.16 = (bf16[32,2048]{1,0:T(8,128)(2,1)S(1)}, bf16[32,2048]{1,0:T(8,128)(2,1)S(1)}, u32[]{:S(2)}, u32[]{:S(2)}) collective-permute-start(bf16[32,2048]{1,0:T(8,128)(2,1)S(1)} %get-tuple-element.40), channel_id=1, source_target_pairs={{0,8},{1,9},{2,10},{3,11},{4,12},{5,13},{6,14},{7,15},{8,0},{9,1},... | collective-permute-start | bytes 393224 | tf_op jit(solution)/shard_map/ppermute | solution.py:35
  35.5 12.0 %collective-permute-start.10 = (bf16[32,2048]{1,0:T(8,128)(2,1)S(1)}, bf16[32,2048]{1,0:T(8,128)(2,1)S(1)}, u32[]{:S(2)}, u32[]{:S(2)}) collective-permute-start(bf16[32,2048]{1,0:T(8,128)(2,1)S(1)} %get-tuple-element.34), channel_id=1, source_target_pairs={{0,8},{1,9},{2,10},{3,11},{4,12},{5,13},{6,14},{7,15},{8,0},{9,1},... | collective-permute-start | bytes 393224 | tf_op jit(solution)/shard_map/ppermute | solution.py:35
  44.6 3.9 %collective-permute-start.17 = (bf16[32,2048]{1,0:T(8,128)(2,1)S(1)}, bf16[32,2048]{1,0:T(8,128)(2,1)S(1)}, u32[]{:S(2)}, u32[]{:S(2)}) collective-permute-start(bf16[32,2048]{1,0:T(8,128)(2,1)S(1)} %shard_map.80.refs_0_), channel_id=1, source_target_pairs={{0,4},{1,3},{2,6},{3,1},{4,0},{5,7},{6,2},{7,5},{8,12},{9,11},{10,... | collective-permute-start | bytes 393224 | tf_op jit(solution)/shard_map/ppermute | solution.py:35
  47.5 3.9 %collective-permute-start.11 = (bf16[32,2048]{1,0:T(8,128)(2,1)S(1)}, bf16[32,2048]{1,0:T(8,128)(2,1)S(1)}, u32[]{:S(2)}, u32[]{:S(2)}) collective-permute-start(bf16[32,2048]{1,0:T(8,128)(2,1)S(1)} %shard_map.75.refs_0_), channel_id=1, source_target_pairs={{0,4},{1,3},{2,6},{3,1},{4,0},{5,7},{6,2},{7,5},{8,12},{9,11},{10,... | collective-permute-start | bytes 393224 | tf_op jit(solution)/shard_map/ppermute | solution.py:35
  48.6 7.0 %collective-permute-start.18 = (bf16[64,2048]{1,0:T(8,128)(2,1)S(1)}, bf16[64,2048]{1,0:T(8,128)(2,1)S(1)}, u32[]{:S(2)}, u32[]{:S(2)}) collective-permute-start(bf16[64,2048]{1,0:T(8,128)(2,1)S(1)} %shard_map.81.refs_0_), channel_id=1, source_target_pairs={{0,2},{1,5},{2,0},{3,7},{4,6},{5,1},{6,4},{7,3},{8,10},{9,13},{10,... | collective-permute-start | bytes 786440 | tf_op jit(solution)/shard_map/ppermute | solution.py:35
  51.4 7.0 %collective-permute-start.12 = (bf16[64,2048]{1,0:T(8,128)(2,1)S(1)}, bf16[64,2048]{1,0:T(8,128)(2,1)S(1)}, u32[]{:S(2)}, u32[]{:S(2)}) collective-permute-start(bf16[64,2048]{1,0:T(8,128)(2,1)S(1)} %shard_map.76.refs_0_), channel_id=1, source_target_pairs={{0,2},{1,5},{2,0},{3,7},{4,6},{5,1},{6,4},{7,3},{8,10},{9,13},{10,... | collective-permute-start | bytes 786440 | tf_op jit(solution)/shard_map/ppermute | solution.py:35
  55.6 5.9 %collective-permute-start.19 = (bf16[128,2048]{1,0:T(8,128)(2,1)S(1)}, bf16[128,2048]{1,0:T(8,128)(2,1)S(1)}, u32[]{:S(2)}, u32[]{:S(2)}) collective-permute-start(bf16[128,2048]{1,0:T(8,128)(2,1)S(1)} %shard_map.82.own_ref), channel_id=1, source_target_pairs={{0,1},{1,0},{2,3},{3,2},{4,5},{5,4},{6,7},{7,6},{8,9},{9,8},{10,11... | collective-permute-start | bytes 1572872 | tf_op jit(solution)/shard_map/ppermute | solution.py:35
  58.4 7.0 %collective-permute-start.13 = (bf16[128,2048]{1,0:T(8,128)(2,1)S(1)}, bf16[128,2048]{1,0:T(8,128)(2,1)S(1)}, u32[]{:S(2)}, u32[]{:S(2)}) collective-permute-start(bf16[128,2048]{1,0:T(8,128)(2,1)S(1)} %shard_map.77.own_ref), channel_id=1, source_target_pairs={{0,1},{1,0},{2,3},{3,2},{4,5},{5,4},{6,7},{7,6},{8,9},{9,8},{10,11... | collective-permute-start | bytes 1572872 | tf_op jit(solution)/shard_map/ppermute | solution.py:35

commit v5 on v4

--- a/solution.py
+++ b/solution.py
@@ -15,7 +15,7 @@
 CHUNKS = 2
 PIECES = 2
 FWD_COLUMNS = 512
-BWD_ROWS = 256
+BWD_ROWS = 128
 
 
 def orders(count):

time: 69.5 us -> 69.4 us (level)
  transfers between devices with their start and end apart: 20 -> 20, of which waited for: 12 -> 12; matrix products, arithmetic and copies ran while one was open for 1% -> 1% of each run, Pallas kernels for 18% -> 17%
where the time goes in v5:
time: 69.4 us; the launch traced here: 69.1 us
  starting transfers between devices  24.1 us (35%)
  waiting for transfers between devices  22.9 us (33%)
  Pallas kernels  19.5 us (28%)
  other arithmetic  1.54 us (2%)
  local copies, waits for them, and re-layouts  0.78 us (1%)
    ppermute x14, waiting for transfers between devices, swap(): return lax.ppermute(x, 'beam', pairs)  22.6 us
    ppermute x14, starting transfers between devices, swap(): return lax.ppermute(x, 'beam', pairs)  16 us
    ppermute x6, starting transfers between devices, fetch(): return lax.ppermute(x, 'beam', [(source_of(i), i) for i in range(count)])  8.15 us
    pallas_call x2, Pallas kernels, backward(): pl.pallas_call(functools.partial(backward_kernel, chunk * width), in_spec...  7.47 us
    pallas_call x4, Pallas kernels, forward(): pl.pallas_call(functools.partial(forward_kernel, len(pieces), len(after),...  7.04 us
    pallas_call x2, Pallas kernels, staged(): pl.pallas_call(functools.partial(stage_kernel, first_row), in_specs=[pl.B...  4.39 us
  transfers between devices with their start and end apart: 20, of which 12 were waited for; matrix products, arithmetic and copies ran while one was open for 1% of the time, Pallas kernels for 17%

profile of v5, /device:TPU:1, one launch (start us, length us, event | category | flops | bytes accessed | tf_op | source)
XLA Modules:
  0.0 69.1 jit_solution(6722991084551412190)
XLA Ops:
  0.0 0.8 %add_add_fusion.refs_0_ = s32[3,16]{1,0:T(4,128)S(1)} fusion(s32[1,8]{1,0:T(1,128)} %bitcast.30, s32[2,8]{1,0:T(2,128)} %bitcast.29), kind=kLoop, calls=%fused_computation.24 | loop fusion | flops 144 | bytes 288 | tf_op jit(solution)/shard_map/concatenate | solution.py:281
  0.8 4.1 %collective-permute-start.2 = (s32[3,16]{1,0:T(4,128)S(1)}, s32[3,16]{1,0:T(4,128)S(1)}, u32[]{:S(2)}, u32[]{:S(2)}) collective-permute-start(s32[3,16]{1,0:T(4,128)S(1)} %add_add_fusion.refs_0_), channel_id=1, source_target_pairs={{12,0},{11,1},{14,2},{9,3},{8,4},{15,5},{10,6},{13,7},{4,8},{3,9},... | collective-permute-start | bytes 584 | tf_op jit(solution)/shard_map/ppermute | solution.py:158
  4.9 0.2 collective-permute-start.1
  5.2 0.1 collective-permute-start
  5.3 0.8 %slice_bitcast_fusion = (f32[64]{0:T(128)S(1)}, f32[64]{0:T(128)S(1)}) fusion(f32[2,64]{1,0:T(2,128)} %param.7), kind=kLoop, calls=%fused_computation.45 | loop fusion | bytes 1024 | tf_op jit(solution)/shard_map/slice | solution.py:261
  6.1 2.2 %shard_map.64.refs_4_.refs_0_ = bf16[1024,2048]{1,0:T(8,128)(2,1)S(1)} custom-call(bf16[2048,4096]{1,0:T(8,128)(2,1)} %bitcast.21), custom_call_target="tpu_custom_call" | custom-call | bytes 4194304 | tf_op jit(solution)/shard_map/pallas_call | solution.py:46
  8.3 0.2 collective-permute-done.refs_1_
  8.5 0.1 shard_map.65
  8.6 3.6 %collective-permute-start.5 = (s32[3,64]{1,0:T(4,128)S(1)}, s32[3,64]{1,0:T(4,128)S(1)}, u32[]{:S(2)}, u32[]{:S(2)}) collective-permute-start(s32[3,64]{1,0:T(4,128)S(1)} %shard_map.65), channel_id=1, source_target_pairs={{5,0},{2,1},{7,2},{0,3},{1,4},{6,5},{3,6},{4,7},{13,8},{10,9},{15,... | collective-permute-start | bytes 2312 | tf_op jit(solution)/shard_map/ppermute | solution.py:158
  12.1 0.1 collective-permute-start.3
  12.3 2.2 %shard_map.66.refs_1_ = bf16[1024,2048]{1,0:T(8,128)(2,1)S(1)} custom-call(bf16[2048,4096]{1,0:T(8,128)(2,1)} %bitcast.22), custom_call_target="tpu_custom_call" | custom-call | bytes 4194304 | tf_op jit(solution)/shard_map/pallas_call | solution.py:46
  14.5 0.1 collective-permute-done.3
  14.6 0.1 fusion.12
  14.7 0.4 broadcast_select_fusion.1
  15.1 0.1 broadcast_select_fusion
  15.2 2.2 %shard_map.67 = (bf16[128,2048]{1,0:T(8,128)(2,1)S(1)}, bf16[1024,2048]{1,0:T(8,128)(2,1)S(1)}) custom-call(bf16[2048,256]{1,0:T(8,128)(2,1)S(1)} %bitcast.15, bf16[1024,2048]{1,0:T(8,128)(2,1)S(1)} %shard_map.64.refs_4_.refs_0_, bf16[1024,2048]{1,0:T(8,128)(2,1)S(1)} %shard_map.66.refs_1_, bf16[2048,4096]{1,0:T(8,128)(2,1)} %bitcast.23), custom_call_target="tpu_custom_call" | custom-call | flops 1073741824 | bytes 8388608 | tf_op jit(solution)/shard_map/pallas_call | solution.py:88
  17.4 1.9 %collective-permute-start.6 = (bf16[128,2048]{1,0:T(8,128)(2,1)S(1)}, bf16[128,2048]{1,0:T(8,128)(2,1)S(1)}, u32[]{:S(2)}, u32[]{:S(2)}) collective-permute-start(bf16[128,2048]{1,0:T(8,128)(2,1)S(1)} %get-tuple-element.24.refs_2_), channel_id=1, source_target_pairs={{0,1},{1,0},{2,3},{3,2},{4,5},{5,4},{6,7},{7,6},{8,9},{9,8},{10,11... | collective-permute-start | bytes 1572872 | tf_op jit(solution)/shard_map/ppermute | solution.py:35
  19.3 2.2 %shard_map.68 = (f32[128,2048]{1,0:T(8,128)S(1)}, bf16[1024,2048]{1,0:T(8,128)(2,1)S(1)}) custom-call(bf16[2048,256]{1,0:T(8,128)(2,1)S(1)} %bitcast.16, bf16[1024,2048]{1,0:T(8,128)(2,1)S(1)} %shard_map.64.refs_4_.refs_0_, bf16[1024,2048]{1,0:T(8,128)(2,1)S(1)} %shard_map.66.refs_1_, bf16[128,2048]{1,0:T(8,128)(2,1)S(1)} %get-tuple-element.24.refs_2_, ...), custom_call_target="tpu_custom_call" | custom-call | flops 1073741824 | bytes 8388608 | tf_op jit(solution)/shard_map/pallas_call | solution.py:88
  21.6 0.1 shard_map.69
  21.7 1.3 %shard_map.70.refs_2_ = bf16[128,2048]{1,0:T(8,128)(2,1)S(1)} custom-call(bf16[2048,256]{1,0:T(8,128)(2,1)S(1)} %bitcast.17, bf16[1024,2048]{1,0:T(8,128)(2,1)S(1)} %get-tuple-element.23.refs_0_, bf16[1024,2048]{1,0:T(8,128)(2,1)S(1)} %get-tuple-element.25.refs_1_, bf16[64,2048]{1,0:T(8,128)(2,1)S(1)} %get-tuple-element.27.refs_2_), custom_call_target="tpu_custom_call" | custom-call | flops 1073741824 | bytes 8388608 | tf_op jit(solution)/shard_map/pallas_call | solution.py:88
  23.0 0.1 collective-permute-start.7
  23.1 0.1 collective-permute-start.14
  23.2 1.3 %shard_map.71.refs_0_ = f32[128,2048]{1,0:T(8,128)S(1)} custom-call(bf16[2048,256]{1,0:T(8,128)(2,1)S(1)} %bitcast.18, bf16[1024,2048]{1,0:T(8,128)(2,1)S(1)} %get-tuple-element.23.refs_0_, bf16[1024,2048]{1,0:T(8,128)(2,1)S(1)} %get-tuple-element.25.refs_1_, bf16[128,2048]{1,0:T(8,128)(2,1)S(1)} %shard_map.70.refs_2_), custom_call_target="tpu_custom_call" | custom-call | flops 1073741824 | bytes 8388608 | tf_op jit(solution)/shard_map/pallas_call | solution.py:88
  24.5 0.5 collective-permute-done.7.refs_1_
  25.0 0.1 shard_map.72
  25.1 1.0 %collective-permute-start.8 = (bf16[64,2048]{1,0:T(8,128)(2,1)S(1)}, bf16[64,2048]{1,0:T(8,128)(2,1)S(1)}, u32[]{:S(2)}, u32[]{:S(2)}) collective-permute-start(bf16[64,2048]{1,0:T(8,128)(2,1)S(1)} %get-tuple-element.29.refs_2_), channel_id=1, source_target_pairs={{0,2},{1,5},{2,0},{3,7},{4,6},{5,1},{6,4},{7,3},{8,10},{9,13},{10,... | collective-permute-start | bytes 786440 | tf_op jit(solution)/shard_map/ppermute | solution.py:35
  26.1 0.1 fusion
  26.2 2.5 %collective-permute-done.14.refs_1_ = bf16[64,2048]{1,0:T(8,128)(2,1)S(1)} collective-permute-done((bf16[64,2048]{1,0:T(8,128)(2,1)S(1)}, bf16[64,2048]{1,0:T(8,128)(2,1)S(1)}, u32[]{:S(2)}, u32[]{:S(2)}) %collective-permute-start.14) | collective-permute-done | bytes 262176 | tf_op jit(solution)/shard_map/ppermute | solution.py:35
  28.7 1.1 %collective-permute-start.15 = (bf16[32,2048]{1,0:T(8,128)(2,1)S(1)}, bf16[32,2048]{1,0:T(8,128)(2,1)S(1)}, u32[]{:S(2)}, u32[]{:S(2)}) collective-permute-start(bf16[32,2048]{1,0:T(8,128)(2,1)S(1)} %get-tuple-element.37), channel_id=1, source_target_pairs={{0,4},{1,3},{2,6},{3,1},{4,0},{5,7},{6,2},{7,5},{8,12},{9,11},{10,... | collective-permute-start | bytes 393224 | tf_op jit(solution)/shard_map/ppermute | solution.py:35
  29.9 1.6 %collective-permute-done.8.refs_1_ = bf16[64,2048]{1,0:T(8,128)(2,1)S(1)} collective-permute-done((bf16[64,2048]{1,0:T(8,128)(2,1)S(1)}, bf16[64,2048]{1,0:T(8,128)(2,1)S(1)}, u32[]{:S(2)}, u32[]{:S(2)}) %collective-permute-start.8) | collective-permute-done | bytes 262176 | tf_op jit(solution)/shard_map/ppermute | solution.py:35
  31.5 1.1 %collective-permute-start.9 = (bf16[32,2048]{1,0:T(8,128)(2,1)S(1)}, bf16[32,2048]{1,0:T(8,128)(2,1)S(1)}, u32[]{:S(2)}, u32[]{:S(2)}) collective-permute-start(bf16[32,2048]{1,0:T(8,128)(2,1)S(1)} %get-tuple-element.31), channel_id=1, source_target_pairs={{0,4},{1,3},{2,6},{3,1},{4,0},{5,7},{6,2},{7,5},{8,12},{9,11},{10,... | collective-permute-start | bytes 393224 | tf_op jit(solution)/shard_map/ppermute | solution.py:35
  32.7 1.2 %collective-permute-done.15.refs_1_ = bf16[32,2048]{1,0:T(8,128)(2,1)S(1)} collective-permute-done((bf16[32,2048]{1,0:T(8,128)(2,1)S(1)}, bf16[32,2048]{1,0:T(8,128)(2,1)S(1)}, u32[]{:S(2)}, u32[]{:S(2)}) %collective-permute-start.15) | collective-permute-done | bytes 131104 | tf_op jit(solution)/shard_map/ppermute | solution.py:35
  33.9 1.3 %collective-permute-start.16 = (bf16[32,2048]{1,0:T(8,128)(2,1)S(1)}, bf16[32,2048]{1,0:T(8,128)(2,1)S(1)}, u32[]{:S(2)}, u32[]{:S(2)}) collective-permute-start(bf16[32,2048]{1,0:T(8,128)(2,1)S(1)} %get-tuple-element.40), channel_id=1, source_target_pairs={{0,8},{1,9},{2,10},{3,11},{4,12},{5,13},{6,14},{7,15},{8,0},{9,1},... | collective-permute-start | bytes 393224 | tf_op jit(solution)/shard_map/ppermute | solution.py:35
  35.1 0.3 collective-permute-done.9.refs_1_
  35.5 1.3 %collective-permute-start.10 = (bf16[32,2048]{1,0:T(8,128)(2,1)S(1)}, bf16[32,2048]{1,0:T(8,128)(2,1)S(1)}, u32[]{:S(2)}, u32[]{:S(2)}) collective-permute-start(bf16[32,2048]{1,0:T(8,128)(2,1)S(1)} %get-tuple-element.34), channel_id=1, source_target_pairs={{0,8},{1,9},{2,10},{3,11},{4,12},{5,13},{6,14},{7,15},{8,0},{9,1},... | collective-permute-start | bytes 393224 | tf_op jit(solution)/shard_map/ppermute | solution.py:35
  36.7 7.9 %collective-permute-done.16.refs_1_ = bf16[32,2048]{1,0:T(8,128)(2,1)S(1)} collective-permute-done((bf16[32,2048]{1,0:T(8,128)(2,1)S(1)}, bf16[32,2048]{1,0:T(8,128)(2,1)S(1)}, u32[]{:S(2)}, u32[]{:S(2)}) %collective-permute-start.16) | collective-permute-done | bytes 131104 | tf_op jit(solution)/shard_map/ppermute | solution.py:35
  44.6 1.1 %collective-permute-start.17 = (bf16[32,2048]{1,0:T(8,128)(2,1)S(1)}, bf16[32,2048]{1,0:T(8,128)(2,1)S(1)}, u32[]{:S(2)}, u32[]{:S(2)}) collective-permute-start(bf16[32,2048]{1,0:T(8,128)(2,1)S(1)} %shard_map.80.refs_0_), channel_id=1, source_target_pairs={{0,4},{1,3},{2,6},{3,1},{4,0},{5,7},{6,2},{7,5},{8,12},{9,11},{10,... | collective-permute-start | bytes 393224 | tf_op jit(solution)/shard_map/ppermute | solution.py:35
  45.8 1.7 %collective-permute-done.10.refs_1_ = bf16[32,2048]{1,0:T(8,128)(2,1)S(1)} collective-permute-done((bf16[32,2048]{1,0:T(8,128)(2,1)S(1)}, bf16[32,2048]{1,0:T(8,128)(2,1)S(1)}, u32[]{:S(2)}, u32[]{:S(2)}) %collective-permute-start.10) | collective-permute-done | bytes 131104 | tf_op jit(solution)/shard_map/ppermute | solution.py:35
  47.5 1.1 %collective-permute-start.11 = (bf16[32,2048]{1,0:T(8,128)(2,1)S(1)}, bf16[32,2048]{1,0:T(8,128)(2,1)S(1)}, u32[]{:S(2)}, u32[]{:S(2)}) collective-permute-start(bf16[32,2048]{1,0:T(8,128)(2,1)S(1)} %shard_map.75.refs_0_), channel_id=1, source_target_pairs={{0,4},{1,3},{2,6},{3,1},{4,0},{5,7},{6,2},{7,5},{8,12},{9,11},{10,... | collective-permute-start | bytes 393224 | tf_op jit(solution)/shard_map/ppermute | solution.py:35
  48.6 0.1 collective-permute-start.18
  48.7 2.7 %collective-permute-done.11.refs_1_ = bf16[32,2048]{1,0:T(8,128)(2,1)S(1)} collective-permute-done((bf16[32,2048]{1,0:T(8,128)(2,1)S(1)}, bf16[32,2048]{1,0:T(8,128)(2,1)S(1)}, u32[]{:S(2)}, u32[]{:S(2)}) %collective-permute-start.11) | collective-permute-done | bytes 131104 | tf_op jit(solution)/shard_map/ppermute | solution.py:35
  51.4 0.1 collective-permute-start.12
  51.4 4.2 %collective-permute-done.18.refs_1_ = bf16[64,2048]{1,0:T(8,128)(2,1)S(1)} collective-permute-done((bf16[64,2048]{1,0:T(8,128)(2,1)S(1)}, bf16[64,2048]{1,0:T(8,128)(2,1)S(1)}, u32[]{:S(2)}, u32[]{:S(2)}) %collective-permute-start.18) | collective-permute-done | bytes 262176 | tf_op jit(solution)/shard_map/ppermute | solution.py:35
  55.6 2.6 %collective-permute-start.19 = (bf16[128,2048]{1,0:T(8,128)(2,1)S(1)}, bf16[128,2048]{1,0:T(8,128)(2,1)S(1)}, u32[]{:S(2)}, u32[]{:S(2)}) collective-permute-start(bf16[128,2048]{1,0:T(8,128)(2,1)S(1)} %shard_map.82.own_ref), channel_id=1, source_target_pairs={{0,1},{1,0},{2,3},{3,2},{4,5},{5,4},{6,7},{7,6},{8,9},{9,8},{10,11... | collective-permute-start | bytes 1572872 | tf_op jit(solution)/shard_map/ppermute | solution.py:35
  58.2 0.2 collective-permute-done.12.refs_1_
  58.4 3.1 %collective-permute-start.13 = (bf16[128,2048]{1,0:T(8,128)(2,1)S(1)}, bf16[128,2048]{1,0:T(8,128)(2,1)S(1)}, u32[]{:S(2)}, u32[]{:S(2)}) collective-permute-start(bf16[128,2048]{1,0:T(8,128)(2,1)S(1)} %shard_map.77.own_ref), channel_id=1, source_target_pairs={{0,1},{1,0},{2,3},{3,2},{4,5},{5,4},{6,7},{7,6},{8,9},{9,8},{10,11... | collective-permute-start | bytes 1572872 | tf_op jit(solution)/shard_map/ppermute | solution.py:35
  61.6 3.7 %shard_map.83.refs_0_ = bf16[2048,4096]{1,0:T(8,128)(2,1)} custom-call(bf16[2048,256]{1,0:T(8,128)(2,1)S(1)} %bitcast.19, bf16[128,2048]{1,0:T(8,128)(2,1)S(1)} %shard_map.82.own_ref, bf16[128,2048]{1,0:T(8,128)(2,1)S(1)} %collective-permute-done.19.other_ref), custom_call_target="tpu_custom_call" | custom-call | tf_op jit(solution)/shard_map/pallas_call | solution.py:126
  65.3 3.7 %shard_map.84 = bf16[2048,4096]{1,0:T(8,128)(2,1)} custom-call(bf16[2048,256]{1,0:T(8,128)(2,1)S(1)} %bitcast.20, bf16[128,2048]{1,0:T(8,128)(2,1)S(1)} %shard_map.77.own_ref, bf16[128,2048]{1,0:T(8,128)(2,1)S(1)} %collective-permute-done.13.other_ref, bf16[2048,4096]{1,0:T(8,128)(2,1)} %shard_map.83.refs_0_), custom_call_target="tpu_custom_call", output_to_operand_aliasing={{}: (3, {})} | custom-call | tf_op jit(solution)/shard_map/pallas_call | solution.py:126
  (30 shorter events, 0.4 us)
Async XLA Ops:
  0.8 7.5 %collective-permute-start.2 = (s32[3,16]{1,0:T(4,128)S(1)}, s32[3,16]{1,0:T(4,128)S(1)}, u32[]{:S(2)}, u32[]{:S(2)}) collective-permute-start(s32[3,16]{1,0:T(4,128)S(1)} %add_add_fusion.refs_0_), channel_id=1, source_target_pairs={{12,0},{11,1},{14,2},{9,3},{8,4},{15,5},{10,6},{13,7},{4,8},{3,9},... | collective-permute-start | bytes 584 | tf_op jit(solution)/shard_map/ppermute | solution.py:158
  4.9 3.4 %collective-permute-start.1 = (s32[3,16]{1,0:T(4,128)S(1)}, s32[3,16]{1,0:T(4,128)S(1)}, u32[]{:S(2)}, u32[]{:S(2)}) collective-permute-start(s32[3,16]{1,0:T(4,128)S(1)} %add_add_fusion.refs_0_), channel_id=1, source_target_pairs={{4,0},{3,1},{6,2},{1,3},{0,4},{7,5},{2,6},{5,7},{12,8},{11,9},{14,... | collective-permute-start | bytes 584 | tf_op jit(solution)/shard_map/ppermute | solution.py:158
  5.2 3.3 %collective-permute-start = (s32[3,16]{1,0:T(4,128)S(1)}, s32[3,16]{1,0:T(4,128)S(1)}, u32[]{:S(2)}, u32[]{:S(2)}) collective-permute-start(s32[3,16]{1,0:T(4,128)S(1)} %add_add_fusion.refs_0_), channel_id=1, source_target_pairs={{8,0},{9,1},{10,2},{11,3},{12,4},{13,5},{14,6},{15,7},{0,8},{1,9},... | collective-permute-start | bytes 584 | tf_op jit(solution)/shard_map/ppermute | solution.py:158
  8.6 5.9 %collective-permute-start.5 = (s32[3,64]{1,0:T(4,128)S(1)}, s32[3,64]{1,0:T(4,128)S(1)}, u32[]{:S(2)}, u32[]{:S(2)}) collective-permute-start(s32[3,64]{1,0:T(4,128)S(1)} %shard_map.65), channel_id=1, source_target_pairs={{5,0},{2,1},{7,2},{0,3},{1,4},{6,5},{3,6},{4,7},{13,8},{10,9},{15,... | collective-permute-start | bytes 2312 | tf_op jit(solution)/shard_map/ppermute | solution.py:158
  12.1 2.3 %collective-permute-start.4 = (s32[3,64]{1,0:T(4,128)S(1)}, s32[3,64]{1,0:T(4,128)S(1)}, u32[]{:S(2)}, u32[]{:S(2)}) collective-permute-start(s32[3,64]{1,0:T(4,128)S(1)} %shard_map.65), channel_id=1, source_target_pairs={{1,0},{0,1},{3,2},{2,3},{5,4},{4,5},{7,6},{6,7},{9,8},{8,9},{11,10... | collective-permute-start | bytes 2312 | tf_op jit(solution)/shard_map/ppermute | solution.py:158
  12.1 2.4 %collective-permute-start.3 = (s32[3,64]{1,0:T(4,128)S(1)}, s32[3,64]{1,0:T(4,128)S(1)}, u32[]{:S(2)}, u32[]{:S(2)}) collective-permute-start(s32[3,64]{1,0:T(4,128)S(1)} %shard_map.65), channel_id=1, source_target_pairs={{2,0},{5,1},{0,2},{7,3},{6,4},{1,5},{4,6},{3,7},{10,8},{13,9},{8,1... | collective-permute-start | bytes 2312 | tf_op jit(solution)/shard_map/ppermute | solution.py:158
  17.4 4.2 %collective-permute-start.6 = (bf16[128,2048]{1,0:T(8,128)(2,1)S(1)}, bf16[128,2048]{1,0:T(8,128)(2,1)S(1)}, u32[]{:S(2)}, u32[]{:S(2)}) collective-permute-start(bf16[128,2048]{1,0:T(8,128)(2,1)S(1)} %get-tuple-element.24.refs_2_), channel_id=1, source_target_pairs={{0,1},{1,0},{2,3},{3,2},{4,5},{5,4},{6,7},{7,6},{8,9},{9,8},{10,11... | collective-permute-start | bytes 1572872 | tf_op jit(solution)/shard_map/ppermute | solution.py:35
  21.7 1.4 %copy-start.1 = (s32[8]{0:T(128)S(1)}, s32[8]{0:T(128)}, u32[]{:S(2)}) copy-start(s32[8]{0:T(128)} %param.11) | copy-start | bytes 100
  23.0 2.0 %collective-permute-start.7 = (bf16[128,2048]{1,0:T(8,128)(2,1)S(1)}, bf16[128,2048]{1,0:T(8,128)(2,1)S(1)}, u32[]{:S(2)}, u32[]{:S(2)}) collective-permute-start(bf16[128,2048]{1,0:T(8,128)(2,1)S(1)} %shard_map.70.refs_2_), channel_id=1, source_target_pairs={{0,1},{1,0},{2,3},{3,2},{4,5},{5,4},{6,7},{7,6},{8,9},{9,8},{10,11... | collective-permute-start | bytes 1572872 | tf_op jit(solution)/shard_map/ppermute | solution.py:35
  23.1 3.0 %copy-start = (bf16[2,8,4096]{2,1,0:T(8,128)(2,1)S(1)}, bf16[2,8,4096]{2,1,0:T(8,128)(2,1)}, u32[]{:S(2)}) copy-start(bf16[2,8,4096]{2,1,0:T(8,128)(2,1)} %param.10) | copy-start | bytes 393220
  23.1 5.6 %collective-permute-start.14 = (bf16[64,2048]{1,0:T(8,128)(2,1)S(1)}, bf16[64,2048]{1,0:T(8,128)(2,1)S(1)}, u32[]{:S(2)}, u32[]{:S(2)}) collective-permute-start(bf16[64,2048]{1,0:T(8,128)(2,1)S(1)} %get-tuple-element.27.refs_2_), channel_id=1, source_target_pairs={{0,2},{1,5},{2,0},{3,7},{4,6},{5,1},{6,4},{7,3},{8,10},{9,13},{10,... | collective-permute-start | bytes 786440 | tf_op jit(solution)/shard_map/ppermute | solution.py:35
  25.1 6.4 %collective-permute-start.8 = (bf16[64,2048]{1,0:T(8,128)(2,1)S(1)}, bf16[64,2048]{1,0:T(8,128)(2,1)S(1)}, u32[]{:S(2)}, u32[]{:S(2)}) collective-permute-start(bf16[64,2048]{1,0:T(8,128)(2,1)S(1)} %get-tuple-element.29.refs_2_), channel_id=1, source_target_pairs={{0,2},{1,5},{2,0},{3,7},{4,6},{5,1},{6,4},{7,3},{8,10},{9,13},{10,... | collective-permute-start | bytes 786440 | tf_op jit(solution)/shard_map/ppermute | solution.py:35
  28.7 5.1 %collective-permute-start.15 = (bf16[32,2048]{1,0:T(8,128)(2,1)S(1)}, bf16[32,2048]{1,0:T(8,128)(2,1)S(1)}, u32[]{:S(2)}, u32[]{:S(2)}) collective-permute-start(bf16[32,2048]{1,0:T(8,128)(2,1)S(1)} %get-tuple-element.37), channel_id=1, source_target_pairs={{0,4},{1,3},{2,6},{3,1},{4,0},{5,7},{6,2},{7,5},{8,12},{9,11},{10,... | collective-permute-start | bytes 393224 | tf_op jit(solution)/shard_map/ppermute | solution.py:35
  31.5 3.9 %collective-permute-start.9 = (bf16[32,2048]{1,0:T(8,128)(2,1)S(1)}, bf16[32,2048]{1,0:T(8,128)(2,1)S(1)}, u32[]{:S(2)}, u32[]{:S(2)}) collective-permute-start(bf16[32,2048]{1,0:T(8,128)(2,1)S(1)} %get-tuple-element.31), channel_id=1, source_target_pairs={{0,4},{1,3},{2,6},{3,1},{4,0},{5,7},{6,2},{7,5},{8,12},{9,11},{10,... | collective-permute-start | bytes 393224 | tf_op jit(solution)/shard_map/ppermute | solution.py:35
  33.9 10.7 %collective-permute-start.16 = (bf16[32,2048]{1,0:T(8,128)(2,1)S(1)}, bf16[32,2048]{1,0:T(8,128)(2,1)S(1)}, u32[]{:S(2)}, u32[]{:S(2)}) collective-permute-start(bf16[32,2048]{1,0:T(8,128)(2,1)S(1)} %get-tuple-element.40), channel_id=1, source_target_pairs={{0,8},{1,9},{2,10},{3,11},{4,12},{5,13},{6,14},{7,15},{8,0},{9,1},... | collective-permute-start | bytes 393224 | tf_op jit(solution)/shard_map/ppermute | solution.py:35
  35.5 12.0 %collective-permute-start.10 = (bf16[32,2048]{1,0:T(8,128)(2,1)S(1)}, bf16[32,2048]{1,0:T(8,128)(2,1)S(1)}, u32[]{:S(2)}, u32[]{:S(2)}) collective-permute-start(bf16[32,2048]{1,0:T(8,128)(2,1)S(1)} %get-tuple-element.34), channel_id=1, source_target_pairs={{0,8},{1,9},{2,10},{3,11},{4,12},{5,13},{6,14},{7,15},{8,0},{9,1},... | collective-permute-start | bytes 393224 | tf_op jit(solution)/shard_map/ppermute | solution.py:35
  44.6 3.9 %collective-permute-start.17 = (bf16[32,2048]{1,0:T(8,128)(2,1)S(1)}, bf16[32,2048]{1,0:T(8,128)(2,1)S(1)}, u32[]{:S(2)}, u32[]{:S(2)}) collective-permute-start(bf16[32,2048]{1,0:T(8,128)(2,1)S(1)} %shard_map.80.refs_0_), channel_id=1, source_target_pairs={{0,4},{1,3},{2,6},{3,1},{4,0},{5,7},{6,2},{7,5},{8,12},{9,11},{10,... | collective-permute-start | bytes 393224 | tf_op jit(solution)/shard_map/ppermute | solution.py:35
  47.5 3.9 %collective-permute-start.11 = (bf16[32,2048]{1,0:T(8,128)(2,1)S(1)}, bf16[32,2048]{1,0:T(8,128)(2,1)S(1)}, u32[]{:S(2)}, u32[]{:S(2)}) collective-permute-start(bf16[32,2048]{1,0:T(8,128)(2,1)S(1)} %shard_map.75.refs_0_), channel_id=1, source_target_pairs={{0,4},{1,3},{2,6},{3,1},{4,0},{5,7},{6,2},{7,5},{8,12},{9,11},{10,... | collective-permute-start | bytes 393224 | tf_op jit(solution)/shard_map/ppermute | solution.py:35
  48.6 7.0 %collective-permute-start.18 = (bf16[64,2048]{1,0:T(8,128)(2,1)S(1)}, bf16[64,2048]{1,0:T(8,128)(2,1)S(1)}, u32[]{:S(2)}, u32[]{:S(2)}) collective-permute-start(bf16[64,2048]{1,0:T(8,128)(2,1)S(1)} %shard_map.81.refs_0_), channel_id=1, source_target_pairs={{0,2},{1,5},{2,0},{3,7},{4,6},{5,1},{6,4},{7,3},{8,10},{9,13},{10,... | collective-permute-start | bytes 786440 | tf_op jit(solution)/shard_map/ppermute | solution.py:35
  51.4 7.0 %collective-permute-start.12 = (bf16[64,2048]{1,0:T(8,128)(2,1)S(1)}, bf16[64,2048]{1,0:T(8,128)(2,1)S(1)}, u32[]{:S(2)}, u32[]{:S(2)}) collective-permute-start(bf16[64,2048]{1,0:T(8,128)(2,1)S(1)} %shard_map.76.refs_0_), channel_id=1, source_target_pairs={{0,2},{1,5},{2,0},{3,7},{4,6},{5,1},{6,4},{7,3},{8,10},{9,13},{10,... | collective-permute-start | bytes 786440 | tf_op jit(solution)/shard_map/ppermute | solution.py:35
  55.6 5.9 %collective-permute-start.19 = (bf16[128,2048]{1,0:T(8,128)(2,1)S(1)}, bf16[128,2048]{1,0:T(8,128)(2,1)S(1)}, u32[]{:S(2)}, u32[]{:S(2)}) collective-permute-start(bf16[128,2048]{1,0:T(8,128)(2,1)S(1)} %shard_map.82.own_ref), channel_id=1, source_target_pairs={{0,1},{1,0},{2,3},{3,2},{4,5},{5,4},{6,7},{7,6},{8,9},{9,8},{10,11... | collective-permute-start | bytes 1572872 | tf_op jit(solution)/shard_map/ppermute | solution.py:35
  58.4 6.9 %collective-permute-start.13 = (bf16[128,2048]{1,0:T(8,128)(2,1)S(1)}, bf16[128,2048]{1,0:T(8,128)(2,1)S(1)}, u32[]{:S(2)}, u32[]{:S(2)}) collective-permute-start(bf16[128,2048]{1,0:T(8,128)(2,1)S(1)} %shard_map.77.own_ref), channel_id=1, source_target_pairs={{0,1},{1,0},{2,3},{3,2},{4,5},{5,4},{6,7},{7,6},{8,9},{9,8},{10,11... | collective-permute-start | bytes 1572872 | tf_op jit(solution)/shard_map/ppermute | solution.py:35
